TPU v7x, 32 devices: a whole 2x2x4 slice. The times are simulated.
32 devices in a mesh: clip: 4 (over z), cam: 2 (over y), slab: 4 (over x, core).
Axes of the slice: x: 2, y: 2, z: 4, core: 2. Of those that a mesh axis runs over, the one named last changes fastest.
Arguments:
- t_query: bfloat16 [8, 512, 1408], P(('clip', 'cam'), 'slab'), parts along dimension 0, may hold values from -8 to 8
- t_key: bfloat16 [8, 512, 1408], P(('clip', 'cam'), 'slab'), parts along dimension 0, may hold values from -6 to 6
- t_value: bfloat16 [8, 512, 1408], P(('clip', 'cam'), 'slab'), parts along dimension 0, may hold values from -6 to 6
- t_resid: bfloat16 [8, 512, 1408], P(('clip', 'cam'), 'slab'), parts along dimension 0, may hold values from -8 to 8
- w_out_teacher: bfloat16 [1408, 1408], P(('cam', 'slab')), may hold values from -0.15625 to 0.15625
- pred_query: bfloat16 [8, 384, 384], P(('clip', 'cam'), 'slab'), parts along dimension 0, may hold values from -6 to 6
- pred_context: bfloat16 [8, 128, 384], P(('clip', 'cam'), 'slab'), parts along dimension 0, may hold values from -6 to 6
- w_query: bfloat16 [384, 384], P(('cam', 'slab')), may hold values from -1 to 1
- w_key: bfloat16 [384, 384], P(('cam', 'slab')), may hold values from -1 to 1
- w_value: bfloat16 [384, 384], P(('cam', 'slab')), may hold values from -0.3125 to 0.3125
- w_out: bfloat16 [384, 384], P(('cam', 'slab')), may hold values from -0.3125 to 0.3125
- w_proj: bfloat16 [384, 1408], P(('cam', 'slab')), may hold values from -0.3125 to 0.3125
- mask_list: int32 [8, 384], P(('clip', 'cam'), 'slab'), parts along dimension 0, may hold values from 0 to 127, as said below
- owners: int32 [8, 384], P('clip'), parts along dimension 0, may hold values from 0 to 7, as said below
Outputs:
- errors: bfloat16 [8, 4, 192, 1408], P(('clip', 'cam'), 'slab'), parts along dimension 0
There are 4 independent parts, one for each index of `clip`. A program takes and returns all parts, laid end to end along the dimension named above; an argument that names none is the same for every part. Nothing has to cross between parts.
Inputs may be any that keep to these rules, and one draw needn't show every extreme that they name: `mask_list`: each camera slab lists 96 distinct local token indices in increasing order. `owners`: an owner is the device cam * 4 + slab of the same clip. Each camera slab names each owner at most 24 times, and in every draw one owner is named exactly 24 times by every camera slab.
All inputs are finite; a program needn't handle non-finite values.
Results may differ from a plain program's by a relative error of at most 0.0076.
Values may be sent and summed in bfloat16 or wider, within the bound.
No kernel may reach another device: no remote copies, remote signals or barrier semaphores. Data moves between devices by JAX's collectives and lax.ppermute only.
A program may use at most 64 MiB of HBM per device.

v0:
```python
import math

import jax
import jax.numpy as jnp
from jax import lax
from jax.sharding import PartitionSpec as P

HEADS = 16
P_HEADS = 12


def norm_rows(values_in):
    average = jnp.mean(values_in, axis=-1, keepdims=True)
    centered = values_in - average
    variance = jnp.mean(centered * centered, axis=-1, keepdims=True)
    return centered * lax.rsqrt(variance + 1e-06)


def empty_state(row_count, head_count, head_size):
    return (
        jnp.full((row_count, head_count), -1e30, jnp.float32),
        jnp.zeros((row_count, head_count), jnp.float32),
        jnp.zeros((row_count, head_count, head_size), jnp.float32),
    )


def attend_block(state_now, query_heads, key_rows, value_rows):
    head_count = query_heads.shape[1]
    head_size = query_heads.shape[2]
    running_max, weight_sum, accumulated = state_now
    for offset in range(0, key_rows.shape[0], 512):
        key_block = key_rows[offset : offset + 512].reshape(-1, head_count, head_size)
        value_block = value_rows[offset : offset + 512].reshape(-1, head_count, head_size)
        scores = jnp.einsum(
            "rhd,khd->rhk", query_heads, key_block, preferred_element_type=jnp.float32
        ) / math.sqrt(head_size)
        new_max = jnp.maximum(running_max, jnp.max(scores, axis=2))
        rescale = jnp.exp(running_max - new_max)
        exponent = jnp.exp(scores - new_max[:, :, None])
        weight_sum = weight_sum * rescale + jnp.sum(exponent, axis=2)
        accumulated = accumulated * rescale[:, :, None] + jnp.einsum(
            "rhk,khd->rhd",
            exponent.astype(jnp.bfloat16),
            value_block,
            preferred_element_type=jnp.float32,
        )
        running_max = new_max
    return (running_max, weight_sum, accumulated)


def finish_heads(weight_sum, accumulated):
    mixed = accumulated / weight_sum[:, :, None]
    return mixed.reshape(mixed.shape[0], -1).astype(jnp.bfloat16)


def shards(
    t_query,
    t_key,
    t_value,
    t_resid,
    w_out_teacher,
    pred_query,
    pred_context,
    w_query,
    w_key,
    w_value,
    w_out,
    w_proj,
    mask_list,
    owners,
):
    model_width = t_query.shape[2]
    head_size = model_width // HEADS
    local_rows = mask_list[0]
    masked_count = local_rows.shape[0]
    masked_query = jnp.take(t_query[0], local_rows, axis=0)
    masked_resid = jnp.take(t_resid[0], local_rows, axis=0)
    query_heads = masked_query.reshape(masked_count, HEADS, head_size)
    pieces = (
        lax.all_gather(t_key[0], "slab", axis=0, tiled=True),
        lax.all_gather(t_value[0], "slab", axis=0, tiled=True),
    )
    running_max, weight_sum, accumulated = attend_block(
        empty_state(masked_count, HEADS, head_size), query_heads, pieces[0], pieces[1]
    )
    teacher_attended = finish_heads(weight_sum, accumulated)
    projected = jnp.dot(
        teacher_attended,
        lax.all_gather(w_out_teacher, ("cam", "slab"), axis=0, tiled=True),
        preferred_element_type=jnp.float32,
    )
    targets = norm_rows(masked_resid.astype(jnp.float32) + projected).astype(jnp.bfloat16)
    devices = lax.axis_size(("cam", "slab"))
    capacity = 2 * masked_count // devices
    myself = lax.axis_index(("cam", "slab"))
    owner_table = owners.reshape(devices, masked_count)
    own_dest = lax.dynamic_index_in_dim(owner_table, myself, 0, keepdims=False)
    onehot = (own_dest[:, None] == jnp.arange(devices, dtype=jnp.int32)[None, :]).astype(jnp.int32)
    order_rank = jnp.sum(onehot * (jnp.cumsum(onehot, axis=0) - onehot), axis=1)
    slot_index = own_dest * capacity + order_rank
    pred_width = pred_query.shape[2]
    slot_total = devices * capacity
    send_targets = (
        jnp.zeros((slot_total, model_width), jnp.bfloat16)
        .at[slot_index]
        .set(targets)
        .reshape(devices, capacity, model_width)
    )
    send_queries = (
        jnp.zeros((slot_total, pred_width), jnp.bfloat16)
        .at[slot_index]
        .set(pred_query[0])
        .reshape(devices, capacity, pred_width)
    )
    recv_targets, recv_queries = (
        lax.all_to_all(send_targets, ("cam", "slab"), split_axis=0, concat_axis=0, tiled=True),
        lax.all_to_all(send_queries, ("cam", "slab"), split_axis=0, concat_axis=0, tiled=True),
    )
    counts = jnp.sum((owner_table == myself).astype(jnp.int32), axis=1)
    filled = (jnp.arange(capacity, dtype=jnp.int32)[None, :] < counts[:, None]).reshape(-1)
    query_rows = recv_queries.reshape(slot_total, pred_width)
    goal_rows = recv_targets.reshape(slot_total, model_width)
    row_total = query_rows.shape[0]
    full_query, full_key, full_value, full_out, full_proj = (
        lax.all_gather(w_query, ("cam", "slab"), axis=0, tiled=True),
        lax.all_gather(w_key, ("cam", "slab"), axis=0, tiled=True),
        lax.all_gather(w_value, ("cam", "slab"), axis=0, tiled=True),
        lax.all_gather(w_out, ("cam", "slab"), axis=0, tiled=True),
        lax.all_gather(w_proj, ("cam", "slab"), axis=0, tiled=True),
    )
    pred_head = pred_width // P_HEADS
    pred_heads = (
        jnp.dot(query_rows, full_query, preferred_element_type=jnp.float32)
        .astype(jnp.bfloat16)
        .reshape(row_total, P_HEADS, pred_head)
    )
    start_state = empty_state(row_total, P_HEADS, pred_head)
    context_keys = jnp.dot(pred_context[0], full_key, preferred_element_type=jnp.float32).astype(
        jnp.bfloat16
    )
    context_values = jnp.dot(
        pred_context[0], full_value, preferred_element_type=jnp.float32
    ).astype(jnp.bfloat16)
    pieces = (
        lax.all_gather(context_keys, ("cam", "slab"), axis=0, tiled=True),
        lax.all_gather(context_values, ("cam", "slab"), axis=0, tiled=True),
    )
    running_max, weight_sum, accumulated = attend_block(
        start_state, pred_heads, pieces[0], pieces[1]
    )
    pred_attended = finish_heads(weight_sum, accumulated)
    pred_hidden = query_rows.astype(jnp.float32) + jnp.dot(
        pred_attended, full_out, preferred_element_type=jnp.float32
    )
    predicted = norm_rows(pred_hidden).astype(jnp.bfloat16)
    difference = jnp.dot(
        predicted, full_proj, preferred_element_type=jnp.float32
    ) - goal_rows.astype(jnp.float32)
    error_rows = jnp.where(filled[:, None], difference, 0.0).astype(jnp.bfloat16)
    return error_rows.reshape(1, 1, slot_total, model_width)


def solution(mesh):
    placed = (
        P(("clip", "cam"), "slab", None),
        P(("clip", "cam"), "slab", None),
        P(("clip", "cam"), "slab", None),
        P(("clip", "cam"), "slab", None),
        P(("cam", "slab"), None),
        P(("clip", "cam"), "slab", None),
        P(("clip", "cam"), "slab", None),
        P(("cam", "slab"), None),
        P(("cam", "slab"), None),
        P(("cam", "slab"), None),
        P(("cam", "slab"), None),
        P(("cam", "slab"), None),
        P(("clip", "cam"), "slab"),
        P("clip", None),
    )
    return jax.shard_map(
        shards,
        mesh=mesh,
        in_specs=placed,
        out_specs=P(("clip", "cam"), "slab", None, None),
        check_vma=False,
    )
```

profile of v0, /device:TPU:0, one launch (start us, length us, event | category | flops | bytes accessed | tf_op | source)
XLA Modules:
  0.0 128.6 jit_solution(16104770518346735013)
XLA Ops:
  6.5 0.7 all-gather.11.cloned.1.call-update
  7.3 0.7 all-gather.13.cloned.1.call-update
  8.1 0.7 all-gather.9.cloned.1.call-update
  8.8 0.8 reshape.140
  9.9 1.9 %scatter_custom_fusion = bf16[192,384]{1,0:T(8,128)(2,1)} fusion(s32[96]{0:T(128)S(1)} %fusion.45, bf16[1,96,384]{2,1,0:T(8,128)(2,1)} %param.21, bf16[]{:T(256)} %constant.14.clone.1), kind=kCustom, calls=%fused_computation.47 | custom fusion | bytes 221186 | tf_op jit(solution)/shard_map/scatter | solution.py:112
  11.8 5.2 %all-to-all-start = ((bf16[8,24,384]{2,1,0:T(8,128)(2,1)}), bf16[8,24,384]{2,1,0:T(8,128)(2,1)S(1)}, u32[]{:S(2)}, u32[]{:S(2)}) async-start(bf16[8,24,384]{2,1,0:T(8,128)(2,1)} %bitcast.5), calls=%async_computation | async-start | bytes 294912 | tf_op jit(solution)/shard_map/all_to_all | solution.py:117
  17.1 0.5 all-gather.7.cloned.1.call-update
  17.6 0.7 compare_select_fusion
  18.3 0.7 compare_and_fusion
  19.0 11.1 %all_gather.30 = bf16[384,384]{1,0:T(8,128)(2,1)S(1)} all-gather(bf16[48,384]{1,0:T(8,128)(2,1)} %param.24), channel_id=1, replica_groups=mesh['clip'=4,'cam'=2,'slab'=4] {'cam','slab'}, dimensions={0}, use_global_device_ids=true | all-gather | bytes 331776 | tf_op jit(solution)/shard_map/all_gather | solution.py:126
  30.3 9.2 %all_gather.31 = bf16[256,384]{1,0:T(8,128)(2,1)S(1)} all-gather(bf16[32,384]{1,0:T(8,128)(2,1)S(1)} %convolution_convert_fusion.2), channel_id=1, replica_groups=mesh['clip'=4,'cam'=2,'slab'=4] {'cam','slab'}, dimensions={0}, use_global_device_ids=true | all-gather | bytes 221184 | tf_op jit(solution)/shard_map/all_gather | solution.py:145
  39.6 9.8 %all_gather.33 = bf16[384,384]{1,0:T(8,128)(2,1)S(1)} all-gather(bf16[48,384]{1,0:T(8,128)(2,1)S(1)} %copy-done.4), channel_id=1, replica_groups=mesh['clip'=4,'cam'=2,'slab'=4] {'cam','slab'}, dimensions={0}, use_global_device_ids=true | all-gather | bytes 331776 | tf_op jit(solution)/shard_map/all_gather | solution.py:127
  49.6 8.8 %all_gather.34 = bf16[256,384]{1,0:T(8,128)(2,1)S(1)} all-gather(bf16[32,384]{1,0:T(8,128)(2,1)S(1)} %convolution_convert_fusion.1), channel_id=1, replica_groups=mesh['clip'=4,'cam'=2,'slab'=4] {'cam','slab'}, dimensions={0}, use_global_device_ids=true | all-gather | bytes 221184 | tf_op jit(solution)/shard_map/all_gather | solution.py:146
  58.5 0.8 gather_fusion.1
  59.5 0.9 copy.27
  60.4 1.5 %gather_fusion = bf16[96,1408]{1,0:T(8,128)(2,1)} fusion(bf16[128,1408]{1,0:T(8,128)(2,1)S(1)} %bitcast.101, s32[1024]{0:T(1024)S(1)} %pad_clamp_fusion), kind=kCustom, calls=%fused_computation.clone | custom fusion | bytes 541056 | tf_op jit(solution)/shard_map/jit(_take)/gather | solution.py:77
  62.1 9.9 %all_gather.32 = bf16[384,384]{1,0:T(8,128)(2,1)S(1)} all-gather(bf16[48,384]{1,0:T(8,128)(2,1)S(1)} %copy-done.5), channel_id=1, replica_groups=mesh['clip'=4,'cam'=2,'slab'=4] {'cam','slab'}, dimensions={0}, use_global_device_ids=true | all-gather | bytes 331776 | tf_op jit(solution)/shard_map/all_gather | solution.py:125
  72.0 9.2 %all_gather.35 = bf16[384,384]{1,0:T(8,128)(2,1)S(1)} all-gather(bf16[48,384]{1,0:T(8,128)(2,1)S(1)} %copy-done.6), channel_id=1, replica_groups=mesh['clip'=4,'cam'=2,'slab'=4] {'cam','slab'}, dimensions={0}, use_global_device_ids=true | all-gather | bytes 331776 | tf_op jit(solution)/shard_map/all_gather | solution.py:128
  81.6 0.7 bitcast_reduce_fusion.1
  82.4 0.9 fusion.7
  83.3 0.6 fusion.24
  84.0 1.0 fusion.52
  85.0 2.6 %copy.24 = bf16[1,512,1408]{1,2,0:T(8,128)(2,1)} copy(bf16[1,512,1408]{2,1,0:T(8,128)(2,1)} %all-gather.11.cloned.1.call-done) | data formatting | bytes 2883584 | tf_op jit(solution)/shard_map/all_gather | solution.py:80
  87.6 2.2 %bitcast_reduce_fusion = (f32[96,16]{0,1:T(8,128)S(1)}, f32[16,96,512]{2,1,0:T(8,128)S(1)}) fusion(bf16[96,16,88]{0,2,1:T(8,128)(2,1)} %bitcast.105, bf16[512,16,88]{0,2,1:T(8,128)(2,1)} %bitcast.102), kind=kOutput, calls=%fused_computation.5 | convolution fusion | flops 139983360 | bytes 4864000 | tf_op jit(solution)/shard_map/rhd,khd->rhk/dot_general | solution.py:34
  89.8 1.0 fusion.2
  90.8 2.6 %copy.26 = bf16[1,512,1408]{1,2,0:T(8,128)(2,1)} copy(bf16[1,512,1408]{2,1,0:T(8,128)(2,1)} %all-gather.13.cloned.1.call-done) | data formatting | bytes 2883584 | tf_op jit(solution)/shard_map/all_gather | solution.py:81
  93.4 3.0 %fusion.30 = bf16[96,16,88]{0,2,1:T(8,128)(2,1)} fusion(bf16[512,16,88]{0,2,1:T(8,128)(2,1)} %bitcast.104, f32[16,96,512]{2,1,0:T(8,128)S(1)} %get-tuple-element.11, f32[96,16]{0,1:T(8,128)S(1)} %broadcast_maximum_fusion.1, f32[96,16]{0,1:T(8,128)S(1)} %get-tuple-element.9, f32[96,16]{0,1:T(8,128)S(1)} %get-tuple-element.8), kind=kOutput, calls=%fused_computation.32 | convolution fusion | flops 141176832 | bytes 4876288 | tf_op jit(solution)/shard_map/rhk,khd->rhd/dot_general | solution.py:41
  96.4 3.1 %fusion.51 = (f32[96]{0:T(128)S(1)}, f32[96,1408]{1,0:T(8,128)S(1)}) fusion(bf16[96,1408]{0,1:T(8,128)(2,1)} %bitcast.110, bf16[1408,1408]{1,0:T(8,128)(2,1)} %all-gather.9.cloned.1.call-done, bf16[96,1408]{1,0:T(8,128)(2,1)} %gather_fusion, pred[96]{0:T(512)(128)(4,1)S(1)} %compare_and_fusion), kind=kOutput, calls=%fused_computation.77 | convolution fusion | flops 381173664 | bytes 5046752 | tf_op jit(solution)/shard_map/dot_general | solution.py:87
  99.8 1.9 %scatter_custom_fusion.1 = bf16[192,1408]{1,0:T(8,128)(2,1)} fusion(s32[96]{0:T(128)S(1)} %fusion.45, f32[96,1408]{1,0:T(8,128)S(1)} %get-tuple-element.13, f32[96]{0:T(128)S(1)} %add_rsqrt_fusion.1, f32[96]{0:T(128)S(1)} %broadcast_multiply_fusion.1, bf16[]{:T(256)} %constant.14.clone.1), kind=kCustom, calls=%fused_computation.40 | custom fusion | flops 405504 | bytes 1082370 | tf_op jit(solution)/shard_map/scatter | solution.py:106
  101.7 3.5 %all-to-all-start.1 = ((bf16[8,24,1408]{2,1,0:T(8,128)(2,1)}), bf16[8,24,1408]{2,1,0:T(8,128)(2,1)S(1)}, u32[]{:S(2)}, u32[]{:S(2)}) async-start(bf16[8,24,1408]{2,1,0:T(8,128)(2,1)} %bitcast.23), calls=%async_computation.1 | async-start | bytes 1081344 | tf_op jit(solution)/shard_map/all_to_all | solution.py:116
  105.5 14.0 %all-gather.7.cloned.1.call-done = bf16[384,1408]{1,0:T(8,128)(2,1)} async-done(((bf16[48,1408]{1,0:T(8,128)(2,1)}), bf16[384,1408]{1,0:T(8,128)(2,1)}) %all-gather.7.cloned.1.call-update) | async-done | bytes 1081360 | tf_op jit(solution)/shard_map/all_gather | solution.py:129
  119.6 2.6 %fusion.5 = bf16[1,1,192,1408]{3,2,1,0:T(8,128)(2,1)} fusion(bf16[384,1408]{1,0:T(8,128)(2,1)} %all-gather.7.cloned.1.call-done, bf16[192,1408]{1,0:T(8,128)(2,1)S(1)} %bitcast.103, pred[192]{0:T(512)(128)(4,1)S(1)} %lt.44, f32[192,384]{1,0:T(8,128)S(1)} %copy-done.2, f32[192]{0:T(256)S(1)} %add_rsqrt_fusion, f32[192]{0:T(256)S(1)} %broadcast_multiply_fusion), kind=kOutput, calls=%fused_computation.13 | convolution fusion | flops 208920576 | bytes 2459328 | tf_op jit(solution)/shard_map/dot_general | solution.py:156
  (49 shorter events, 2.4 us)
Async XLA Ops:
  6.5 52.0 %copy-start = (bf16[1,128,1408]{2,1,0:T(8,128)(2,1)S(1)}, bf16[1,128,1408]{2,1,0:T(8,128)(2,1)}, u32[]{:S(2)}) copy-start(bf16[1,128,1408]{2,1,0:T(8,128)(2,1)} %param.16) | copy-start | bytes 1081348
  6.5 23.6 %copy-start.3 = (bf16[1,32,384]{2,1,0:T(8,128)(2,1)S(1)}, bf16[1,32,384]{2,1,0:T(8,128)(2,1)}, u32[]{:S(2)}) copy-start(bf16[1,32,384]{2,1,0:T(8,128)(2,1)} %param.22) | copy-start | bytes 73732
  6.5 33.1 %copy-start.4 = (bf16[48,384]{1,0:T(8,128)(2,1)S(1)}, bf16[48,384]{1,0:T(8,128)(2,1)}, u32[]{:S(2)}) copy-start(bf16[48,384]{1,0:T(8,128)(2,1)} %param.25) | copy-start | bytes 110596
  6.5 78.4 %all-gather.11.cloned.1.call-start = ((), (), s32[]{:S(2)}) async-start(), calls=%async_computation.4 | async-start | bytes 1802240 | tf_op jit(solution)/shard_map/all_gather | solution.py:80
  7.3 83.6 %all-gather.13.cloned.1.call-start = ((), (), s32[]{:S(2)}) async-start(), calls=%async_computation.5 | async-start | bytes 1802240 | tf_op jit(solution)/shard_map/all_gather | solution.py:81
  8.0 88.4 %all-gather.9.cloned.1.call-start = ((), (), s32[]{:S(2)}) async-start(), calls=%async_computation.3 | async-start | bytes 4460544 | tf_op jit(solution)/shard_map/all_gather | solution.py:89
  11.8 69.4 %all-to-all-start = ((bf16[8,24,384]{2,1,0:T(8,128)(2,1)}), bf16[8,24,384]{2,1,0:T(8,128)(2,1)S(1)}, u32[]{:S(2)}, u32[]{:S(2)}) async-start(bf16[8,24,384]{2,1,0:T(8,128)(2,1)} %bitcast.5), calls=%async_computation | async-start | bytes 294912 | tf_op jit(solution)/shard_map/all_to_all | solution.py:117
  17.0 102.5 %all-gather.7.cloned.1.call-start = ((), (), s32[]{:S(2)}) async-start(), calls=%async_computation.2 | async-start | bytes 1216512 | tf_op jit(solution)/shard_map/all_gather | solution.py:129
  49.4 11.0 %copy-start.1 = (bf16[1,128,1408]{2,1,0:T(8,128)(2,1)S(1)}, bf16[1,128,1408]{2,1,0:T(8,128)(2,1)}, u32[]{:S(2)}) copy-start(bf16[1,128,1408]{2,1,0:T(8,128)(2,1)} %param.19) | copy-start | bytes 1081348
  59.4 2.7 %copy-start.5 = (bf16[48,384]{1,0:T(8,128)(2,1)S(1)}, bf16[48,384]{1,0:T(8,128)(2,1)}, u32[]{:S(2)}) copy-start(bf16[48,384]{1,0:T(8,128)(2,1)} %param.23) | copy-start | bytes 110596
  59.4 12.6 %copy-start.6 = (bf16[48,384]{1,0:T(8,128)(2,1)S(1)}, bf16[48,384]{1,0:T(8,128)(2,1)}, u32[]{:S(2)}) copy-start(bf16[48,384]{1,0:T(8,128)(2,1)} %param.26) | copy-start | bytes 110596
  99.6 5.7 %copy-start.2 = (f32[192,384]{1,0:T(8,128)S(1)}, f32[192,384]{1,0:T(8,128)}, u32[]{:S(2)}) copy-start(f32[192,384]{1,0:T(8,128)} %get-tuple-element.17) | copy-start | bytes 884740
  101.7 17.8 %all-to-all-start.1 = ((bf16[8,24,1408]{2,1,0:T(8,128)(2,1)}), bf16[8,24,1408]{2,1,0:T(8,128)(2,1)S(1)}, u32[]{:S(2)}, u32[]{:S(2)}) async-start(bf16[8,24,1408]{2,1,0:T(8,128)(2,1)} %bitcast.23), calls=%async_computation.1 | async-start | bytes 1081344 | tf_op jit(solution)/shard_map/all_to_all | solution.py:116
Sparse Core Ops, SparseCore 0:
  8.9 23.3 all-gather.10
  33.8 20.4 all-gather.12
  56.2 36.8 all-gather.8
  94.8 24.6 all-gather.6
where the time goes:
time: 129 us
  blocking collectives  58 us (45%)
  waiting for transfers between devices  16.7 us (13%)
  matrix products  13.8 us (11%)
  between operations  13.3 us (10%)
  local copies, waits for them, and re-layouts  11.7 us (9%)
  starting transfers between devices  8.82 us (7%)
  other arithmetic  6.36 us (5%)
    all_gather x1, waiting for transfers between devices, shards(): lax.all_gather(w_proj, ('cam', 'slab'), axis=0, tiled=True)  14 us
    all_gather x1, blocking collectives, shards(): lax.all_gather(w_key, ('cam', 'slab'), axis=0, tiled=True)  11.1 us
    all_gather x1, blocking collectives, shards(): lax.all_gather(w_query, ('cam', 'slab'), axis=0, tiled=True)  9.88 us
    all_gather x1, blocking collectives, shards(): lax.all_gather(w_value, ('cam', 'slab'), axis=0, tiled=True)  9.76 us
    all_gather x1, blocking collectives, shards(): lax.all_gather(w_out, ('cam', 'slab'), axis=0, tiled=True)  9.24 us
    all_gather x1, blocking collectives, shards(): lax.all_gather(context_keys, ('cam', 'slab'), axis=0, tiled=True)  9.15 us
    all_gather x1, blocking collectives, shards(): lax.all_gather(context_values, ('cam', 'slab'), axis=0, tiled=True)  8.8 us
    all_to_all x1, starting transfers between devices, shards(): lax.all_to_all(send_queries, ('cam', 'slab'), split_axis=0, concat_axis=0...  5.17 us
  transfers between devices with their start and end apart: 6, of which 1 were waited for; matrix products, arithmetic and copies ran while one was open for 23% of the time, Pallas kernels for 0%

commit v1 on v0

--- a/solution.py
+++ b/solution.py
@@ -93,34 +93,16 @@
     devices = lax.axis_size(("cam", "slab"))
     capacity = 2 * masked_count // devices
     myself = lax.axis_index(("cam", "slab"))
-    owner_table = owners.reshape(devices, masked_count)
-    own_dest = lax.dynamic_index_in_dim(owner_table, myself, 0, keepdims=False)
-    onehot = (own_dest[:, None] == jnp.arange(devices, dtype=jnp.int32)[None, :]).astype(jnp.int32)
-    order_rank = jnp.sum(onehot * (jnp.cumsum(onehot, axis=0) - onehot), axis=1)
+    own_dest = lax.dynamic_index_in_dim(
+        owners.reshape(devices, masked_count), myself, 0, keepdims=False
+    )
+    earlier = jnp.tril(jnp.ones((masked_count, masked_count), jnp.bool_), -1)
+    same_owner = own_dest[:, None] == own_dest[None, :]
+    order_rank = jnp.sum((same_owner & earlier).astype(jnp.int32), axis=1)
     slot_index = own_dest * capacity + order_rank
-    pred_width = pred_query.shape[2]
     slot_total = devices * capacity
-    send_targets = (
-        jnp.zeros((slot_total, model_width), jnp.bfloat16)
-        .at[slot_index]
-        .set(targets)
-        .reshape(devices, capacity, model_width)
-    )
-    send_queries = (
-        jnp.zeros((slot_total, pred_width), jnp.bfloat16)
-        .at[slot_index]
-        .set(pred_query[0])
-        .reshape(devices, capacity, pred_width)
-    )
-    recv_targets, recv_queries = (
-        lax.all_to_all(send_targets, ("cam", "slab"), split_axis=0, concat_axis=0, tiled=True),
-        lax.all_to_all(send_queries, ("cam", "slab"), split_axis=0, concat_axis=0, tiled=True),
-    )
-    counts = jnp.sum((owner_table == myself).astype(jnp.int32), axis=1)
-    filled = (jnp.arange(capacity, dtype=jnp.int32)[None, :] < counts[:, None]).reshape(-1)
-    query_rows = recv_queries.reshape(slot_total, pred_width)
-    goal_rows = recv_targets.reshape(slot_total, model_width)
-    row_total = query_rows.shape[0]
+    query_rows = pred_query[0]
+    pred_width = query_rows.shape[1]
     full_query, full_key, full_value, full_out, full_proj = (
         lax.all_gather(w_query, ("cam", "slab"), axis=0, tiled=True),
         lax.all_gather(w_key, ("cam", "slab"), axis=0, tiled=True),
@@ -132,21 +114,17 @@
     pred_heads = (
         jnp.dot(query_rows, full_query, preferred_element_type=jnp.float32)
         .astype(jnp.bfloat16)
-        .reshape(row_total, P_HEADS, pred_head)
+        .reshape(masked_count, P_HEADS, pred_head)
     )
-    start_state = empty_state(row_total, P_HEADS, pred_head)
-    context_keys = jnp.dot(pred_context[0], full_key, preferred_element_type=jnp.float32).astype(
-        jnp.bfloat16
-    )
-    context_values = jnp.dot(
-        pred_context[0], full_value, preferred_element_type=jnp.float32
-    ).astype(jnp.bfloat16)
-    pieces = (
-        lax.all_gather(context_keys, ("cam", "slab"), axis=0, tiled=True),
-        lax.all_gather(context_values, ("cam", "slab"), axis=0, tiled=True),
-    )
+    start_state = empty_state(masked_count, P_HEADS, pred_head)
+    context = lax.all_gather(pred_context[0], ("cam", "slab"), axis=0, tiled=True)
+    context_keys = jnp.dot(context, full_key, preferred_element_type=jnp.float32)
+    context_values = jnp.dot(context, full_value, preferred_element_type=jnp.float32)
     running_max, weight_sum, accumulated = attend_block(
-        start_state, pred_heads, pieces[0], pieces[1]
+        start_state,
+        pred_heads,
+        context_keys.astype(jnp.bfloat16),
+        context_values.astype(jnp.bfloat16),
     )
     pred_attended = finish_heads(weight_sum, accumulated)
     pred_hidden = query_rows.astype(jnp.float32) + jnp.dot(
@@ -155,9 +133,15 @@
     predicted = norm_rows(pred_hidden).astype(jnp.bfloat16)
     difference = jnp.dot(
         predicted, full_proj, preferred_element_type=jnp.float32
-    ) - goal_rows.astype(jnp.float32)
-    error_rows = jnp.where(filled[:, None], difference, 0.0).astype(jnp.bfloat16)
-    return error_rows.reshape(1, 1, slot_total, model_width)
+    ) - targets.astype(jnp.float32)
+    sent = (
+        jnp.zeros((slot_total, model_width), jnp.bfloat16)
+        .at[slot_index]
+        .set(difference.astype(jnp.bfloat16))
+        .reshape(devices, capacity, model_width)
+    )
+    errors = lax.all_to_all(sent, ("cam", "slab"), split_axis=0, concat_axis=0, tiled=True)
+    return errors.reshape(1, 1, slot_total, model_width)
 
 
 def solution(mesh):

time: 129 us -> 139 us (1.078)
  waiting for transfers between devices: 16.7 us -> 38.2 us
  starting transfers between devices: 8.82 us -> 0.12 us
  matrix products: 13.8 us -> 10.6 us
  other arithmetic: 6.36 us -> 3.53 us
  blocking collectives: 58 us -> 60.3 us
    all_gather x1, waiting for transfers between devices: 0.01 us -> 13.5 us  [shards(): lax.all_gather(w_out_teacher, ('cam', 'slab'), axis=0, tiled=True)]
    all_to_all x0 -> x1, blocking collectives: none -> 12.5 us  [shards(): lax.all_to_all(sent, ('cam', 'slab'), split_axis=0, concat_axis=0, tiled=...]
    all_to_all x2 -> x0, starting transfers between devices: 8.71 us -> none  [the longest x1 5.17 us: shards(): lax.all_to_all(send_queries, ('cam', 'slab'), split_axis=0, concat_axis=0...]
    all_gather x1, waiting for transfers between devices: 14 us -> 22 us  [shards(): lax.all_gather(w_proj, ('cam', 'slab'), axis=0, tiled=True)]
    all_gather x2 -> x1, blocking collectives: 18 us -> 11.3 us  [shards(): lax.all_gather(pred_context[0], ('cam', 'slab'), axis=0, tiled=True)]
    scatter x1 -> x0, other arithmetic: 1.94 us -> none  [shards(): send_targets = jnp.zeros((slot_total, model_width), jnp.bfloat16).at[slot...]
    unnamed x14 -> x25, local copies, waits for them, and re-layouts: 0.03 us -> 1.84 us
    all_gather x1, blocking collectives: 11.1 us -> 9.39 us  [shards(): lax.all_gather(w_key, ('cam', 'slab'), axis=0, tiled=True)]
  transfers between devices with their start and end apart: 6 -> 4, of which waited for: 1 -> 2; matrix products, arithmetic and copies ran while one was open for 23% -> 16% of each run, Pallas kernels for 0% -> 0%
where the time goes in v1:
time: 139 us; the launch traced here: 138 us
  blocking collectives  60.3 us (43%)
  waiting for transfers between devices  38.2 us (27%)
  between operations  13.4 us (10%)
  local copies, waits for them, and re-layouts  12 us (9%)
  matrix products  10.6 us (8%)
  other arithmetic  3.53 us (3%)
    all_gather x1, waiting for transfers between devices, shards(): lax.all_gather(w_proj, ('cam', 'slab'), axis=0, tiled=True)  22 us
    all_gather x1, waiting for transfers between devices, shards(): lax.all_gather(w_out_teacher, ('cam', 'slab'), axis=0, tiled=True)  13.5 us
    all_to_all x1, blocking collectives, shards(): lax.all_to_all(sent, ('cam', 'slab'), split_axis=0, concat_axis=0, tiled=...  12.5 us
    all_gather x1, blocking collectives, shards(): lax.all_gather(pred_context[0], ('cam', 'slab'), axis=0, tiled=True)  11.3 us
    all_gather x1, blocking collectives, shards(): lax.all_gather(w_value, ('cam', 'slab'), axis=0, tiled=True)  9.47 us
    all_gather x1, blocking collectives, shards(): lax.all_gather(w_key, ('cam', 'slab'), axis=0, tiled=True)  9.39 us
    all_gather x1, blocking collectives, shards(): lax.all_gather(w_query, ('cam', 'slab'), axis=0, tiled=True)  9.09 us
    all_gather x1, blocking collectives, shards(): lax.all_gather(w_out, ('cam', 'slab'), axis=0, tiled=True)  8.57 us
  transfers between devices with their start and end apart: 4, of which 2 were waited for; matrix products, arithmetic and copies ran while one was open for 16% of the time, Pallas kernels for 0%

profile of v1, /device:TPU:0, one launch (start us, length us, event | category | flops | bytes accessed | tf_op | source)
XLA Modules:
  0.0 138.1 jit_solution(5042486007964011495)
XLA Ops:
  6.5 0.7 all-gather.12.cloned.1.call-update
  7.3 0.7 all-gather.14.cloned.1.call-update
  8.1 0.7 all-gather.10.cloned.1.call-update
  8.8 0.5 all-gather.8.cloned.1.call-update
  9.3 0.7 compare_select_fusion
  10.0 0.7 compare_and_fusion
  10.7 0.8 gather_fusion.1
  11.6 0.9 copy.33
  12.5 1.5 %gather_fusion = bf16[96,1408]{1,0:T(8,128)(2,1)} fusion(bf16[128,1408]{1,0:T(8,128)(2,1)S(1)} %bitcast.86, s32[1024]{0:T(1024)S(1)} %pad_clamp_fusion), kind=kCustom, calls=%fused_computation.clone | custom fusion | bytes 541056 | tf_op jit(solution)/shard_map/jit(_take)/gather | solution.py:77
  14.1 11.3 %all-gather = bf16[1,256,384]{2,1,0:T(8,128)(2,1)S(1)} all-gather(bf16[1,32,384]{2,1,0:T(8,128)(2,1)S(1)} %copy-done.10), channel_id=2, replica_groups=mesh['clip'=4,'cam'=2,'slab'=4] {'cam','slab'}, dimensions={1}, use_global_device_ids=true | all-gather | bytes 221184 | tf_op jit(solution)/shard_map/all_gather | solution.py:120
  25.4 9.4 %all_gather.28 = bf16[384,384]{1,0:T(8,128)(2,1)S(1)} all-gather(bf16[48,384]{1,0:T(8,128)(2,1)S(1)} %copy-done.6), channel_id=1, replica_groups=mesh['clip'=4,'cam'=2,'slab'=4] {'cam','slab'}, dimensions={0}, use_global_device_ids=true | all-gather | bytes 331776 | tf_op jit(solution)/shard_map/all_gather | solution.py:108
  35.2 9.1 %all_gather.29 = bf16[384,384]{1,0:T(8,128)(2,1)S(1)} all-gather(bf16[48,384]{1,0:T(8,128)(2,1)S(1)} %copy-done.7), channel_id=1, replica_groups=mesh['clip'=4,'cam'=2,'slab'=4] {'cam','slab'}, dimensions={0}, use_global_device_ids=true | all-gather | bytes 331776 | tf_op jit(solution)/shard_map/all_gather | solution.py:107
  44.6 0.5 fusion.42
  45.1 0.5 fusion.24
  45.6 9.5 %all_gather.30 = bf16[384,384]{1,0:T(8,128)(2,1)S(1)} all-gather(bf16[48,384]{1,0:T(8,128)(2,1)S(1)} %copy-done.8), channel_id=1, replica_groups=mesh['clip'=4,'cam'=2,'slab'=4] {'cam','slab'}, dimensions={0}, use_global_device_ids=true | all-gather | bytes 331776 | tf_op jit(solution)/shard_map/all_gather | solution.py:109
  55.6 8.6 %all_gather.31 = bf16[384,384]{1,0:T(8,128)(2,1)S(1)} all-gather(bf16[48,384]{1,0:T(8,128)(2,1)S(1)} %copy-done.9), channel_id=1, replica_groups=mesh['clip'=4,'cam'=2,'slab'=4] {'cam','slab'}, dimensions={0}, use_global_device_ids=true | all-gather | bytes 331776 | tf_op jit(solution)/shard_map/all_gather | solution.py:110
  64.1 0.4 fusion.23
  64.5 0.3 fusion.43
  64.9 0.6 copy-done.3
  66.1 2.6 %copy.30 = bf16[1,512,1408]{1,2,0:T(8,128)(2,1)} copy(bf16[1,512,1408]{2,1,0:T(8,128)(2,1)} %all-gather.12.cloned.1.call-done) | data formatting | bytes 2883584 | tf_op jit(solution)/shard_map/all_gather | solution.py:80
  68.7 2.2 %bitcast_reduce_fusion = (f32[96,16]{0,1:T(8,128)S(1)}, f32[16,96,512]{2,1,0:T(8,128)S(1)}) fusion(bf16[96,16,88]{0,2,1:T(8,128)(2,1)} %bitcast.91, bf16[512,16,88]{0,2,1:T(8,128)(2,1)} %bitcast.87), kind=kOutput, calls=%fused_computation.4 | convolution fusion | flops 139983360 | bytes 4864000 | tf_op jit(solution)/shard_map/rhd,khd->rhk/dot_general | solution.py:34
  70.9 2.6 %copy.32 = bf16[1,512,1408]{1,2,0:T(8,128)(2,1)} copy(bf16[1,512,1408]{2,1,0:T(8,128)(2,1)} %all-gather.14.cloned.1.call-done) | data formatting | bytes 2883584 | tf_op jit(solution)/shard_map/all_gather | solution.py:81
  73.5 1.0 fusion.1
  74.5 0.4 copy-done.2
  74.9 1.6 %fusion.18 = bf16[96,16,88]{0,2,1:T(8,128)(2,1)} fusion(bf16[512,16,88]{0,2,1:T(8,128)(2,1)S(1)} %bitcast.90, f32[16,96,512]{2,1,0:T(8,128)S(1)} %get-tuple-element.11, f32[96,16]{0,1:T(8,128)S(1)} %broadcast_maximum_fusion, f32[96,16]{0,1:T(8,128)S(1)} %get-tuple-element.9, f32[96,16]{0,1:T(8,128)S(1)} %get-tuple-element.8), kind=kOutput, calls=%fused_computation.22 | convolution fusion | flops 141176832 | bytes 4876288 | tf_op jit(solution)/shard_map/rhk,khd->rhd/dot_general | solution.py:41
  76.5 13.5 %all-gather.10.cloned.1.call-done = bf16[1408,1408]{1,0:T(8,128)(2,1)} async-done(((bf16[176,1408]{1,0:T(8,128)(2,1)}), bf16[1408,1408]{1,0:T(8,128)(2,1)}) %all-gather.10.cloned.1.call-update) | async-done | bytes 3964944 | tf_op jit(solution)/shard_map/all_gather | solution.py:89
  90.1 3.2 %fusion.41 = (f32[96]{0:T(128)S(1)}, f32[96,1408]{1,0:T(8,128)S(1)}) fusion(bf16[96,1408]{0,1:T(8,128)(2,1)} %bitcast.94, bf16[1408,1408]{1,0:T(8,128)(2,1)} %all-gather.10.cloned.1.call-done, bf16[96,1408]{1,0:T(8,128)(2,1)} %gather_fusion, pred[96]{0:T(512)(128)(4,1)S(1)} %compare_and_fusion), kind=kOutput, calls=%fused_computation.67 | convolution fusion | flops 381173664 | bytes 5046752 | tf_op jit(solution)/shard_map/dot_general | solution.py:87
  93.5 22.0 %all-gather.8.cloned.1.call-done = bf16[384,1408]{1,0:T(8,128)(2,1)} async-done(((bf16[48,1408]{1,0:T(8,128)(2,1)}), bf16[384,1408]{1,0:T(8,128)(2,1)}) %all-gather.8.cloned.1.call-update) | async-done | bytes 1081360 | tf_op jit(solution)/shard_map/all_gather | solution.py:111
  115.5 1.6 %fusion.3 = bf16[96,1408]{1,0:T(8,128)(2,1)S(1)} fusion(bf16[384,1408]{1,0:T(8,128)(2,1)} %all-gather.8.cloned.1.call-done, f32[96,1408]{1,0:T(8,128)S(1)} %get-tuple-element.13, f32[96]{0:T(128)S(1)} %add_rsqrt_fusion, f32[96]{0:T(128)S(1)} %broadcast_multiply_fusion, f32[96,384]{1,0:T(8,128)S(1)} %copy-done.4, f32[96]{0:T(128)S(1)} %add_rsqrt_fusion.1, ...), kind=kOutput, calls=%fused_computation.10 | convolution fusion | flops 104730624 | bytes 2041344 | tf_op jit(solution)/shard_map/dot_general | solution.py:134
  117.1 1.2 scatter_custom_fusion
  118.3 12.5 %all_to_all.5 = bf16[8,24,1408]{2,1,0:T(8,128)(2,1)S(1)} all-to-all(bf16[8,24,1408]{2,1,0:T(8,128)(2,1)S(1)} %bitcast.88), channel_id=1, replica_groups=mesh['clip'=4,'cam'=2,'slab'=4] {'cam','slab'}, dimensions={0} | all-to-all | bytes 1081344 | tf_op jit(solution)/shard_map/all_to_all | solution.py:143
  130.8 0.8 copy.35
  (51 shorter events, 2.2 us)
Async XLA Ops:
  6.5 4.1 %copy-start = (bf16[1,128,1408]{2,1,0:T(8,128)(2,1)S(1)}, bf16[1,128,1408]{2,1,0:T(8,128)(2,1)}, u32[]{:S(2)}) copy-start(bf16[1,128,1408]{2,1,0:T(8,128)(2,1)} %param.16) | copy-start | bytes 1081348
  6.5 59.5 %all-gather.12.cloned.1.call-start = ((), (), s32[]{:S(2)}) async-start(), calls=%async_computation.3 | async-start | bytes 1802240 | tf_op jit(solution)/shard_map/all_gather | solution.py:80
  7.3 63.7 %all-gather.14.cloned.1.call-start = ((), (), s32[]{:S(2)}) async-start(), calls=%async_computation.4 | async-start | bytes 1802240 | tf_op jit(solution)/shard_map/all_gather | solution.py:81
  8.0 82.0 %all-gather.10.cloned.1.call-start = ((), (), s32[]{:S(2)}) async-start(), calls=%async_computation.2 | async-start | bytes 4460544 | tf_op jit(solution)/shard_map/all_gather | solution.py:89
  8.7 106.7 %all-gather.8.cloned.1.call-start = ((), (), s32[]{:S(2)}) async-start(), calls=%async_computation.1 | async-start | bytes 1216512 | tf_op jit(solution)/shard_map/all_gather | solution.py:111
  10.7 1.9 %copy-start.1 = (bf16[1,128,1408]{2,1,0:T(8,128)(2,1)S(1)}, bf16[1,128,1408]{2,1,0:T(8,128)(2,1)}, u32[]{:S(2)}) copy-start(bf16[1,128,1408]{2,1,0:T(8,128)(2,1)} %param.19) | copy-start | bytes 1081348
  11.6 2.5 %copy-start.10 = (bf16[1,32,384]{2,1,0:T(8,128)(2,1)S(1)}, bf16[1,32,384]{2,1,0:T(8,128)(2,1)}, u32[]{:S(2)}) copy-start(bf16[1,32,384]{2,1,0:T(8,128)(2,1)} %param.22) | copy-start | bytes 73732
  12.5 12.8 %copy-start.6 = (bf16[48,384]{1,0:T(8,128)(2,1)S(1)}, bf16[48,384]{1,0:T(8,128)(2,1)}, u32[]{:S(2)}) copy-start(bf16[48,384]{1,0:T(8,128)(2,1)} %param.24) | copy-start | bytes 110596
  12.5 22.6 %copy-start.7 = (bf16[48,384]{1,0:T(8,128)(2,1)S(1)}, bf16[48,384]{1,0:T(8,128)(2,1)}, u32[]{:S(2)}) copy-start(bf16[48,384]{1,0:T(8,128)(2,1)} %param.23) | copy-start | bytes 110596
  14.1 30.2 %copy-start.5 = (bf16[1,96,384]{2,1,0:T(8,128)(2,1)S(1)}, bf16[1,96,384]{2,1,0:T(8,128)(2,1)}, u32[]{:S(2)}) copy-start(bf16[1,96,384]{2,1,0:T(8,128)(2,1)} %param.21) | copy-start | bytes 221188
  44.5 1.1 copy-start.8
  45.1 10.4 %copy-start.9 = (bf16[48,384]{1,0:T(8,128)(2,1)S(1)}, bf16[48,384]{1,0:T(8,128)(2,1)}, u32[]{:S(2)}) copy-start(bf16[48,384]{1,0:T(8,128)(2,1)} %param.26) | copy-start | bytes 110596
  55.5 10.2 %copy-start.11 = (s32[2,384]{1,0:T(2,128)S(1)}, s32[2,384]{1,0:T(2,128)}, u32[]{:S(2)}) copy-start(s32[2,384]{1,0:T(2,128)} %param.29) | copy-start | bytes 9220
  64.9 0.7 copy-start.3
  73.5 1.4 copy-start.2
  90.1 25.4 %copy-start.4 = (f32[96,384]{1,0:T(8,128)S(1)}, f32[96,384]{1,0:T(8,128)}, u32[]{:S(2)}) copy-start(f32[96,384]{1,0:T(8,128)} %copy-done.3) | copy-start | bytes 442372
Sparse Core Ops, SparseCore 0:
  8.9 22.3 all-gather.11
  32.9 19.4 all-gather.13
  54.3 35.7 all-gather.9
  91.8 23.6 all-gather.7

commit v2 on v1

--- a/solution.py
+++ b/solution.py
@@ -1,12 +1,16 @@
+import functools
 import math
 
 import jax
 import jax.numpy as jnp
 from jax import lax
+from jax.experimental import pallas as pl
+from jax.experimental.pallas import tpu as pltpu
 from jax.sharding import PartitionSpec as P
 
 HEADS = 16
 P_HEADS = 12
+LANES = 128
 
 
 def norm_rows(values_in):
@@ -144,6 +148,343 @@
     return errors.reshape(1, 1, slot_total, model_width)
 
 
+def rows_dot(left, right):
+    return lax.dot_general(
+        left, right, (((1,), (1,)), ((), ())), preferred_element_type=jnp.float32
+    )
+
+
+def dot(left, right):
+    return jnp.dot(left, right, preferred_element_type=jnp.float32)
+
+
+def position():
+    return lax.axis_index("cam"), lax.axis_index("slab")
+
+
+def head_windows(head_count, head_size):
+    windows = []
+    for head in range(head_count):
+        low, high = head * head_size, (head + 1) * head_size
+        start = low // LANES * LANES
+        windows.append((low, high, start, -(-high // LANES) * LANES))
+    return windows
+
+
+def inside(shape, start, low, high):
+    lane = lax.broadcasted_iota(jnp.int32, shape, 1) + start
+    return (lane >= low) & (lane < high)
+
+
+def softmax_terms(scores, scale):
+    peak = jnp.max(scores, axis=1, keepdims=True)
+    terms = jnp.exp2((scores - peak) * scale)
+    return terms.astype(jnp.bfloat16), jnp.sum(terms, axis=1, keepdims=True)
+
+
+def slot_picker(key_row, owner, capacity, slot_total):
+    shape = (2 * capacity, key_row.shape[1])
+    row = lax.broadcasted_iota(jnp.int32, shape, 0)
+    late = row >= capacity
+    wanted = owner * capacity + row + jnp.where(late, slot_total - capacity, 0)
+    return jnp.where(key_row == wanted, 1.0, 0.0).astype(jnp.bfloat16)
+
+
+def pack_kernel(
+    capacity, query, key, value, resid, mask, owners, wq, wk, wv, wo, wp, context,
+    block0, block1, block2, block3, resid_rows, slot_keys, pack, stack, blocks,
+):
+    cam, slab = position()
+    tokens, width = key.shape
+    masked = mask.shape[1]
+    quarter = width // 8
+    token = lax.broadcasted_iota(jnp.int32, (tokens, masked), 0)
+    chosen = jnp.where(token == mask[...], 1.0, 0.0).T.astype(jnp.bfloat16)
+    stack[0:tokens] = key[...]
+    stack[tokens : 2 * tokens] = value[...]
+    stack[2 * tokens :] = dot(chosen, query[...]).astype(jnp.bfloat16)
+    resid_rows[...] = dot(chosen, resid[...]).astype(jnp.bfloat16)
+    row_total = stack.shape[0]
+    pad = blocks.shape[2] - 2 * quarter
+    for other in range(4):
+        first = stack[:, other * quarter : (other + 1) * quarter]
+        second = stack[:, (other + 4) * quarter : (other + 5) * quarter]
+        blocks[other] = jnp.concatenate(
+            [first, second, jnp.zeros((row_total, pad), jnp.bfloat16)], axis=1
+        )
+    for relation, out in enumerate((block0, block1, block2, block3)):
+        out[...] = blocks[slab ^ relation]
+    listed = owners.shape[1]
+    before = lax.broadcasted_iota(jnp.int32, (listed, listed), 0)
+    after = lax.broadcasted_iota(jnp.int32, (listed, listed), 1)
+    group = sum((before >= edge).astype(jnp.int32) for edge in range(masked, listed, masked))
+    group_after = sum((after >= edge).astype(jnp.int32) for edge in range(masked, listed, masked))
+    precedes = jnp.where((before < after) & (group == group_after), 1.0, 0.0)
+    owner_row = owners[pl.ds(cam, 1), :]
+    device = lax.broadcasted_iota(jnp.int32, (8, listed), 0)
+    owned = jnp.where(device == owner_row, 1.0, 0.0)
+    counted = dot(owned.astype(jnp.bfloat16), precedes.astype(jnp.bfloat16))
+    rank = jnp.sum(owned * counted, axis=0, keepdims=True).astype(jnp.int32)
+    lane = lax.broadcasted_iota(jnp.int32, (1, listed), 1)
+    odd = ((lane >= masked) & (lane < 2 * masked)) | (lane >= 3 * masked)
+    keys = owner_row * capacity + rank + jnp.where(odd, 8 * capacity, 0)
+    slot_keys[0:1, :] = keys[:, 0 : 2 * masked]
+    slot_keys[1:2, :] = keys[:, 2 * masked :]
+    at = 0
+    for part in (wq, wk, wv, wo, wp):
+        pack[:, at : at + part.shape[1]] = part[...]
+        at += part.shape[1]
+    pack[0 : context.shape[0], at:] = context[...]
+    pack[context.shape[0] :, at:] = jnp.zeros(
+        (pack.shape[0] - context.shape[0], context.shape[1]), jnp.bfloat16
+    )
+
+
+def ask_kernel(capacity, slot_keys, own_rows, peer_rows, pack, out0, out1, out2, out3, pair):
+    cam, slab = position()
+    rows = own_rows.shape[0]
+    core = slab % 2
+    pair[pl.ds(pl.multiple_of(core * rows, rows), rows)] = own_rows[...]
+    pair[pl.ds(pl.multiple_of((1 - core) * rows, rows), rows)] = peer_rows[...]
+    key_row = slot_keys[pl.ds(slab // 2, 1), :]
+    width = pack.shape[1]
+    for relation, out in enumerate((out0, out1, out2, out3)):
+        owner = (cam * 4 + slab) ^ (relation * 2)
+        picker = slot_picker(key_row, owner, capacity, 8 * capacity)
+        picked = dot(picker, pair[...]).astype(jnp.bfloat16)
+        if relation:
+            out[:, 0:width] = pack[...]
+            out[:, width:] = picked
+        else:
+            out[...] = picked
+
+
+def teacher_kernel(
+    capacity, head_size, tokens, masked, slot_keys, block0, block1, block2, block3,
+    own_core, peer_core, queries, keys, values, attended,
+):
+    cam, slab = position()
+    for relation, block in enumerate((block0, block1, block2, block3)):
+        other = slab ^ relation
+        keys[relation * tokens : (relation + 1) * tokens] = block[0:tokens]
+        values[relation * tokens : (relation + 1) * tokens] = block[tokens : 2 * tokens]
+        queries[pl.ds(pl.multiple_of(other * masked, masked), masked)] = block[2 * tokens :]
+    scale = math.log2(math.e) / math.sqrt(head_size)
+    chunk = 2 * masked
+    for half in range(2):
+        rows = slice(half * chunk, (half + 1) * chunk)
+        total = [jnp.zeros((chunk, LANES), jnp.float32) for _ in range(attended.shape[1] // LANES)]
+        for low, high, start, stop in head_windows(4, head_size):
+            window = inside((chunk, stop - start), start, low, high)
+            picked = jnp.where(window, queries[rows, start:stop].astype(jnp.float32), 0.0)
+            scores = rows_dot(picked.astype(jnp.bfloat16), keys[:, start:stop])
+            terms, weight = softmax_terms(scores, scale)
+            mixed = dot(terms, values[:, start:stop]) / weight
+            mixed = jnp.where(window, mixed, 0.0)
+            for tile in range(start // LANES, stop // LANES):
+                total[tile] += mixed[:, tile * LANES - start : (tile + 1) * LANES - start]
+        attended[rows] = jnp.concatenate(total, axis=1).astype(jnp.bfloat16)
+    for flip, out in enumerate((own_core, peer_core)):
+        for relation in range(4):
+            owner = (cam * 4 + slab) ^ (relation * 2 + flip)
+            for half in range(2):
+                picker = slot_picker(slot_keys[half : half + 1, :], owner, capacity, 8 * capacity)
+                at = (relation * 2 + half) * 2 * capacity
+                out[at : at + 2 * capacity] = dot(
+                    picker, attended[half * chunk : (half + 1) * chunk]
+                ).astype(jnp.bfloat16)
+
+
+def project_kernel(
+    capacity, slot_keys, own_slots, peer_slots, w_own, w_cam, w_core, w_both, resid_own, resid_peer,
+    out0, out1, out2, out3, weight, resid_pair, total,
+):
+    cam, slab = position()
+    core, chip = slab % 2, slab // 2
+    part, width = w_own.shape
+    half = own_slots.shape[1]
+    for base, same, crossed in ((0, w_own, w_cam), (half, w_core, w_both)):
+        weight[pl.ds(pl.multiple_of(base + cam * part, 16), part)] = same[...]
+        weight[pl.ds(pl.multiple_of(base + (1 - cam) * part, 16), part)] = crossed[...]
+        weight[base + 2 * part : base + half] = jnp.zeros((half - 2 * part, width), jnp.bfloat16)
+    rows = resid_own.shape[0]
+    resid_pair[pl.ds(pl.multiple_of(core * rows, rows), rows)] = resid_own[...]
+    resid_pair[pl.ds(pl.multiple_of((1 - core) * rows, rows), rows)] = resid_peer[...]
+    key_row = slot_keys[pl.ds(chip, 1), :]
+    block = out0.shape[0]
+    for relation, out in ((3, out3), (2, out2), (1, out1), (0, out0)):
+        at = relation * block
+        total[...] = dot(own_slots[at : at + block], weight[0:half]) + dot(
+            peer_slots[at : at + block], weight[half:]
+        )
+        owner = (cam * 4 + slab) ^ (relation * 2)
+        picker = slot_picker(key_row, owner, capacity, 8 * capacity)
+        own_rows = pl.ds(pl.multiple_of(chip * 2 * capacity, 8), 2 * capacity)
+        total[own_rows] = total[own_rows] + dot(picker, resid_pair[...])
+        out[...] = total[...].astype(jnp.bfloat16)
+
+
+def predict_kernel(
+    context_rows, ask0, ask1, ask2, ask3, own_pack, peer0, peer1, peer2, peer3, out,
+    queries, weights, context,
+):
+    cam, slab = position()
+    rows, width = ask0.shape
+    own = cam * 4 + slab
+    side = own // 2
+    pieces = ((own_pack, peer0), (ask1, peer1), (ask2, peer2), (ask3, peer3))
+    wide = weights.shape[1]
+    for relation, both in enumerate(pieces):
+        asked = ask0[...] if relation == 0 else both[0][:, wide + width :]
+        queries[pl.ds(pl.multiple_of((side ^ relation) * rows, rows), rows)] = asked
+        for flip, piece in enumerate(both):
+            source = own ^ (relation * 2 + flip)
+            part = piece.shape[0]
+            weights[pl.ds(pl.multiple_of(source * part, part), part)] = piece[:, 0:wide]
+            context[pl.ds(pl.multiple_of(source * context_rows, context_rows), context_rows)] = (
+                piece[0:context_rows, wide : wide + width]
+            )
+    head_size = width // P_HEADS
+    scale = math.log2(math.e) / math.sqrt(head_size)
+    asked = dot(queries[...], weights[:, 0:width]).astype(jnp.bfloat16)
+    seen_keys = dot(context[...], weights[:, width : 2 * width]).astype(jnp.bfloat16)
+    seen_values = dot(context[...], weights[:, 2 * width : 3 * width]).astype(jnp.bfloat16)
+    total = [jnp.zeros((asked.shape[0], LANES), jnp.float32) for _ in range(width // LANES)]
+    for low, high, start, stop in head_windows(P_HEADS, head_size):
+        window = inside((asked.shape[0], stop - start), start, low, high)
+        picked = jnp.where(window, asked[:, start:stop].astype(jnp.float32), 0.0)
+        scores = rows_dot(picked.astype(jnp.bfloat16), seen_keys[:, start:stop])
+        terms, weight = softmax_terms(scores, scale)
+        mixed = dot(terms, seen_values[:, start:stop]) / weight
+        total[start // LANES] += jnp.where(window, mixed, 0.0)
+    attended = jnp.concatenate(total, axis=1).astype(jnp.bfloat16)
+    hidden = queries[...].astype(jnp.float32) + dot(attended, weights[:, 3 * width : 4 * width])
+    predicted = norm_rows(hidden).astype(jnp.bfloat16)
+    out[...] = dot(predicted, weights[:, 4 * width :])
+
+
+def finish_kernel(capacity, masked, owners, predicted, part0, part1, part2, part3, out):
+    cam, slab = position()
+    rows = part0.shape[0]
+    for flip, (near, far) in enumerate(((part0, part1), (part2, part3))):
+        camera = cam ^ flip
+        at = pl.ds(pl.multiple_of(camera * rows, rows), rows)
+        summed = near[...].astype(jnp.float32) + far[...].astype(jnp.float32)
+        shape = (rows, owners.shape[1])
+        row = lax.broadcasted_iota(jnp.int32, shape, 0)
+        lane = lax.broadcasted_iota(jnp.int32, shape, 1)
+        listed = owners[pl.ds(camera, 1), :] == cam * 4 + slab
+        same = jnp.zeros(shape, jnp.bool_)
+        for group in range(4):
+            same = same | (
+                (row >= group * capacity)
+                & (row < (group + 1) * capacity)
+                & (lane >= group * masked)
+                & (lane < (group + 1) * masked)
+            )
+        count = jnp.sum(jnp.where(same & listed, 1.0, 0.0), axis=1, keepdims=True)
+        order = lax.broadcasted_iota(jnp.int32, (rows, 1), 0)
+        order = order - sum(
+            jnp.where(order >= group * capacity, capacity, 0) for group in range(1, 4)
+        )
+        filled = order.astype(jnp.float32) < count
+        goal = norm_rows(summed).astype(jnp.bfloat16).astype(jnp.float32)
+        out[at] = jnp.where(filled, predicted[at] - goal, 0.0).astype(jnp.bfloat16)
+
+
+def call(kernel, outs, scratch, *args):
+    shapes = tuple(jax.ShapeDtypeStruct(shape, dtype) for shape, dtype in outs)
+    return pl.pallas_call(
+        kernel,
+        out_shape=shapes,
+        scratch_shapes=[pltpu.VMEM(shape, dtype) for shape, dtype in scratch],
+        compiler_params=pltpu.CompilerParams(vmem_limit_bytes=40 * 2**20),
+    )(*args)
+
+
+def send(rows, flip):
+    return lax.ppermute(rows, ("cam", "slab"), [(source, source ^ flip) for source in range(8)])
+
+
+def paired_shards(
+    t_query, t_key, t_value, t_resid, w_out_teacher, pred_query, pred_context,
+    w_query, w_key, w_value, w_out, w_proj, mask_list, owners,
+):
+    bf16, f32 = jnp.bfloat16, jnp.float32
+    tokens, width = t_key.shape[1:]
+    masked, pred_width = pred_query.shape[1:]
+    capacity = masked // 4
+    quarter = width // 8
+    head_size = width // HEADS
+    context_rows = pred_context.shape[1]
+    padded = -(-2 * quarter // LANES) * LANES
+    block_rows = 2 * tokens + masked
+    block = ((block_rows, padded), bf16)
+    weight_rows = w_query.shape[0]
+    weight_width = 4 * pred_width + w_proj.shape[1]
+    pack_width = weight_width + pred_width
+    peer_query = send(pred_query[0], 1)
+    w_core = send(w_out_teacher, 1)
+    w_cam = send(w_out_teacher, 4)
+    block0, block1, block2, block3, resid_rows, slot_keys, pack = call(
+        functools.partial(pack_kernel, capacity),
+        [block] * 4
+        + [((masked, width), bf16), ((2, 2 * masked), jnp.int32), ((weight_rows, pack_width), bf16)],
+        [((block_rows, width), bf16), ((4, block_rows, padded), bf16)],
+        t_query[0], t_key[0], t_value[0], t_resid[0], mask_list, owners,
+        w_query, w_key, w_value, w_out, w_proj, pred_context[0],
+    )
+    other2, other3, other1 = send(block2, 2), send(block3, 3), send(block1, 1)
+    w_both = send(w_cam, 1)
+    peer_resid = send(resid_rows, 1)
+    ask_rows = 2 * capacity
+    ask = ((ask_rows, pack_width + pred_width), bf16)
+    ask0, ask1, ask2, ask3 = call(
+        functools.partial(ask_kernel, capacity),
+        [((ask_rows, pred_width), bf16), ask, ask, ask],
+        [((2 * masked, pred_width), bf16)],
+        slot_keys, pred_query[0], peer_query, pack,
+    )
+    asked1, asked2, asked3 = send(ask1, 2), send(ask2, 4), send(ask3, 6)
+    peer_pack = send(pack, 1)
+    slots = ((16 * capacity, padded), bf16)
+    own_slots, away_slots = call(
+        functools.partial(teacher_kernel, capacity, head_size, tokens, masked),
+        [slots, slots],
+        [
+            ((4 * masked, padded), bf16), ((4 * tokens, padded), bf16), ((4 * tokens, padded), bf16),
+            ((4 * masked, padded), bf16),
+        ],
+        slot_keys, block0, other1, other2, other3,
+    )
+    peer_slots = send(away_slots, 1)
+    part = ((4 * capacity, width), bf16)
+    part0, part1, part2, part3 = call(
+        functools.partial(project_kernel, capacity),
+        [part] * 4,
+        [((2 * padded, width), bf16), ((2 * masked, width), bf16), ((4 * capacity, width), f32)],
+        slot_keys, own_slots, peer_slots, w_out_teacher, w_cam, w_core, w_both, resid_rows, peer_resid,
+    )
+    far1, far2, far3 = send(part1, 2), send(part2, 4), send(part3, 6)
+    peer1, peer2, peer3 = send(asked1, 1), send(asked2, 1), send(asked3, 1)
+    (predicted,) = call(
+        functools.partial(predict_kernel, context_rows),
+        [((8 * capacity, width), f32)],
+        [
+            ((8 * capacity, pred_width), bf16), ((8 * weight_rows, weight_width), bf16),
+            ((8 * context_rows, pred_width), bf16),
+        ],
+        ask0, asked1, asked2, asked3, pack, peer_pack, peer1, peer2, peer3,
+    )
+    (errors,) = call(
+        functools.partial(finish_kernel, capacity, masked),
+        [((8 * capacity, width), bf16)],
+        [],
+        owners, predicted, part0, far1, far2, far3,
+    )
+    return errors[None, None]
+
+
 def solution(mesh):
     placed = (
         P(("clip", "cam"), "slab", None),
@@ -161,8 +502,9 @@
         P(("clip", "cam"), "slab"),
         P("clip", None),
     )
+    small = (mesh.shape["cam"], mesh.shape["slab"]) == (2, 4)
     return jax.shard_map(
-        shards,
+        paired_shards if small else shards,
         mesh=mesh,
         in_specs=placed,
         out_specs=P(("clip", "cam"), "slab", None, None),

time: 139 us -> 64.1 us (0.46)
  blocking collectives: 60.3 us -> 0 us
  starting transfers between devices: 0.12 us -> 14.2 us
  between operations: 13.4 us -> 0.07 us
  matrix products: 10.6 us -> 0 us
  Pallas kernels: 0 us -> 9.55 us
  waiting for transfers between devices: 38.2 us -> 29.7 us
  other arithmetic: 3.53 us -> 0 us
  local copies, waits for them, and re-layouts: 12 us -> 10.1 us
    all_gather x5 -> x0, blocking collectives: 47.8 us -> none  [the longest x1 11.3 us: shards(): lax.all_gather(pred_context[0], ('cam', 'slab'), axis=0, tiled=True)]
    all_gather x4 -> x0, waiting for transfers between devices: 35.6 us -> none  [the longest x1 22 us: shards(): lax.all_gather(w_proj, ('cam', 'slab'), axis=0, tiled=True)]
    ppermute x0 -> x19, waiting for transfers between devices: none -> 29.7 us  [send(): lax.ppermute(rows, ('cam', 'slab'), [(source, source ^ flip) for source i...]
    ppermute x0 -> x19, starting transfers between devices: none -> 14.2 us  [send(): lax.ppermute(rows, ('cam', 'slab'), [(source, source ^ flip) for source i...]
    all_to_all x1 -> x0, blocking collectives: 12.5 us -> none  [shards(): lax.all_to_all(sent, ('cam', 'slab'), split_axis=0, concat_axis=0, tiled=...]
    dot_general x10 -> x0, matrix products: 10.6 us -> none  [the longest x1 3.18 us: shards(): jnp.dot(teacher_attended, lax.all_gather(w_out_teacher, ('cam', 'slab'),...]
    pallas_call x0 -> x6, Pallas kernels: none -> 9.55 us  [call(): pl.pallas_call(kernel, out_shape=shapes, scratch_shapes=[pltpu.VMEM(shape...]
    unnamed x25 -> x30, local copies, waits for them, and re-layouts: 1.84 us -> 10.1 us
  transfers between devices with their start and end apart: 4 -> 19, of which waited for: 2 -> 7; matrix products, arithmetic and copies ran while one was open for 16% -> 0% of each run, Pallas kernels for 0% -> 12%
where the time goes in v2:
time: 64.1 us; the launch traced here: 63.5 us
  waiting for transfers between devices  29.7 us (46%)
  starting transfers between devices  14.2 us (22%)
  local copies, waits for them, and re-layouts  10.1 us (16%)
  Pallas kernels  9.55 us (15%)
    ppermute x19, waiting for transfers between devices, send(): lax.ppermute(rows, ('cam', 'slab'), [(source, source ^ flip) for source i...  29.7 us
    ppermute x19, starting transfers between devices, send(): lax.ppermute(rows, ('cam', 'slab'), [(source, source ^ flip) for source i...  14.2 us
    unnamed x30, local copies, waits for them, and re-layouts  10.1 us
    pallas_call x6, Pallas kernels, call(): pl.pallas_call(kernel, out_shape=shapes, scratch_shapes=[pltpu.VMEM(shape...  9.55 us
  transfers between devices with their start and end apart: 19, of which 7 were waited for; matrix products, arithmetic and copies ran while one was open for 0% of the time, Pallas kernels for 12%

profile of v2, /device:TPU:0, one launch (start us, length us, event | category | flops | bytes accessed | tf_op | source)
XLA Modules:
  0.0 63.5 jit_solution(9594700533403660219)
XLA Ops:
  0.0 1.0 %copy-done.1 = bf16[1,128,1408]{2,1,0:T(8,128)(2,1)S(1)} copy-done((bf16[1,128,1408]{2,1,0:T(8,128)(2,1)S(1)}, bf16[1,128,1408]{2,1,0:T(8,128)(2,1)}, u32[]{:S(2)}) %copy-start.1) | copy-done | bytes 360472
  1.0 1.0 %copy-done.2 = bf16[1,128,1408]{2,1,0:T(8,128)(2,1)S(1)} copy-done((bf16[1,128,1408]{2,1,0:T(8,128)(2,1)S(1)}, bf16[1,128,1408]{2,1,0:T(8,128)(2,1)}, u32[]{:S(2)}) %copy-start.2) | copy-done | bytes 360472
  2.0 1.0 %copy-done.3 = bf16[1,128,1408]{2,1,0:T(8,128)(2,1)S(1)} copy-done((bf16[1,128,1408]{2,1,0:T(8,128)(2,1)S(1)}, bf16[1,128,1408]{2,1,0:T(8,128)(2,1)}, u32[]{:S(2)}) %copy-start.3) | copy-done | bytes 360472
  3.0 1.0 %copy-done.4 = bf16[1,128,1408]{2,1,0:T(8,128)(2,1)S(1)} copy-done((bf16[1,128,1408]{2,1,0:T(8,128)(2,1)S(1)}, bf16[1,128,1408]{2,1,0:T(8,128)(2,1)}, u32[]{:S(2)}) %copy-start.4) | copy-done | bytes 360472
  4.0 0.9 %copy-done.5 = bf16[48,1408]{1,0:T(8,128)(2,1)S(1)} copy-done((bf16[48,1408]{1,0:T(8,128)(2,1)S(1)}, bf16[48,1408]{1,0:T(8,128)(2,1)}, u32[]{:S(2)}) %copy-start.5) | copy-done | bytes 135192
  4.9 0.8 %copy-done.7 = bf16[48,384]{1,0:T(8,128)(2,1)S(1)} copy-done((bf16[48,384]{1,0:T(8,128)(2,1)S(1)}, bf16[48,384]{1,0:T(8,128)(2,1)}, u32[]{:S(2)}) %copy-start.7) | copy-done | bytes 36888
  5.7 0.8 %copy-done.8 = bf16[48,384]{1,0:T(8,128)(2,1)S(1)} copy-done((bf16[48,384]{1,0:T(8,128)(2,1)S(1)}, bf16[48,384]{1,0:T(8,128)(2,1)}, u32[]{:S(2)}) %copy-start.8) | copy-done | bytes 36888
  6.4 0.8 %copy-done.9 = bf16[48,384]{1,0:T(8,128)(2,1)S(1)} copy-done((bf16[48,384]{1,0:T(8,128)(2,1)S(1)}, bf16[48,384]{1,0:T(8,128)(2,1)}, u32[]{:S(2)}) %copy-start.9) | copy-done | bytes 36888
  7.2 0.8 %copy-done.10 = bf16[48,384]{1,0:T(8,128)(2,1)S(1)} copy-done((bf16[48,384]{1,0:T(8,128)(2,1)S(1)}, bf16[48,384]{1,0:T(8,128)(2,1)}, u32[]{:S(2)}) %copy-start.10) | copy-done | bytes 36888
  8.0 0.7 %copy-done.11 = bf16[1,32,384]{2,1,0:T(8,128)(2,1)S(1)} copy-done((bf16[1,32,384]{2,1,0:T(8,128)(2,1)S(1)}, bf16[1,32,384]{2,1,0:T(8,128)(2,1)}, u32[]{:S(2)}) %copy-start.11) | copy-done | bytes 24600
  8.7 0.7 %copy-done.12 = s32[2,384]{1,0:T(2,128)S(1)} copy-done((s32[2,384]{1,0:T(2,128)S(1)}, s32[2,384]{1,0:T(2,128)}, u32[]{:S(2)}) %copy-start.12) | copy-done | bytes 3096
  9.4 0.7 %copy-done.14 = s32[1,96]{1,0:T(1,128)S(1)} copy-done((s32[1,96]{1,0:T(1,128)S(1)}, s32[1,96]{1,0:T(1,128)}, u32[]{:S(2)}) %copy-start.14) | copy-done | bytes 408
  10.1 0.7 %shard_map.136 = (bf16[352,384]{1,0:T(8,128)(2,1)S(1)}, bf16[352,384]{1,0:T(8,128)(2,1)S(1)}, bf16[352,384]{1,0:T(8,128)(2,1)S(1)}, bf16[352,384]{1,0:T(8,128)(2...) custom-call(bf16[128,1408]{1,0:T(8,128)(2,1)S(1)} %bitcast.7, ...), custom_call_target="tpu_custom_call" | custom-call | tf_op jit(solution)/shard_map/pallas_call | solution.py:397
  11.3 2.6 %collective-permute-start.12 = (bf16[176,1408]{1,0:T(8,128)(2,1)S(1)}, bf16[176,1408]{1,0:T(8,128)(2,1)S(1)}, u32[]{:S(2)}, u32[]{:S(2)}) collective-permute-start(bf16[176,1408]{1,0:T(8,128)(2,1)S(1)} %copy-done), channel_id=1, source_target_pairs={{0,4},{1,5},{2,6},{3,7},{4,0},{5,1},{6,2},{7,3},{8,12},{9,13},{10,... | collective-permute-start | bytes 1486856 | tf_op jit(solution)/shard_map/ppermute | solution.py:406
  13.9 1.5 %collective-permute-start.9 = (bf16[352,384]{1,0:T(8,128)(2,1)S(1)}, bf16[352,384]{1,0:T(8,128)(2,1)S(1)}, u32[]{:S(2)}, u32[]{:S(2)}) collective-permute-start(bf16[352,384]{1,0:T(8,128)(2,1)S(1)} %get-tuple-element.30), channel_id=1, source_target_pairs={{0,2},{1,3},{2,0},{3,1},{4,6},{5,7},{6,4},{7,5},{8,10},{9,11},{10,... | collective-permute-start | bytes 811016 | tf_op jit(solution)/shard_map/ppermute | solution.py:406
  15.4 0.6 collective-permute-start
  16.0 0.9 %collective-permute-done.peer_rows = bf16[96,384]{1,0:T(8,128)(2,1)S(1)} collective-permute-done((bf16[96,384]{1,0:T(8,128)(2,1)S(1)}, bf16[96,384]{1,0:T(8,128)(2,1)S(1)}, u32[]{:S(2)}, u32[]{:S(2)}) %collective-permute-start) | collective-permute-done | bytes 73760 | tf_op jit(solution)/shard_map/ppermute | solution.py:406
  17.6 1.6 %collective-permute-start.1 = (bf16[48,3712]{1,0:T(8,128)(2,1)S(1)}, bf16[48,3712]{1,0:T(8,128)(2,1)S(1)}, u32[]{:S(2)}, u32[]{:S(2)}) collective-permute-start(bf16[48,3712]{1,0:T(8,128)(2,1)S(1)} %get-tuple-element.25), channel_id=1, source_target_pairs={{0,2},{1,3},{2,0},{3,1},{4,6},{5,7},{6,4},{7,5},{8,10},{9,11},{10,... | collective-permute-start | bytes 1069064 | tf_op jit(solution)/shard_map/ppermute | solution.py:406
  19.1 4.1 %collective-permute-done.9.block2 = bf16[352,384]{1,0:T(8,128)(2,1)S(1)} collective-permute-done((bf16[352,384]{1,0:T(8,128)(2,1)S(1)}, bf16[352,384]{1,0:T(8,128)(2,1)S(1)}, u32[]{:S(2)}, u32[]{:S(2)}) %collective-permute-start.9) | collective-permute-done | bytes 270368 | tf_op jit(solution)/shard_map/ppermute | solution.py:406
  23.2 4.7 %collective-permute-done.10.block3 = bf16[352,384]{1,0:T(8,128)(2,1)S(1)} collective-permute-done((bf16[352,384]{1,0:T(8,128)(2,1)S(1)}, bf16[352,384]{1,0:T(8,128)(2,1)S(1)}, u32[]{:S(2)}, u32[]{:S(2)}) %collective-permute-start.10) | collective-permute-done | bytes 270368 | tf_op jit(solution)/shard_map/ppermute | solution.py:406
  28.0 0.9 %collective-permute-start.3 = (bf16[48,3712]{1,0:T(8,128)(2,1)S(1)}, bf16[48,3712]{1,0:T(8,128)(2,1)S(1)}, u32[]{:S(2)}, u32[]{:S(2)}) collective-permute-start(bf16[48,3712]{1,0:T(8,128)(2,1)S(1)} %get-tuple-element.27), channel_id=1, source_target_pairs={{0,6},{1,7},{2,4},{3,5},{4,2},{5,3},{6,0},{7,1},{8,14},{9,15},{10,... | collective-permute-start | bytes 1069064 | tf_op jit(solution)/shard_map/ppermute | solution.py:406
  28.8 1.4 %collective-permute-start.13 = (bf16[176,1408]{1,0:T(8,128)(2,1)S(1)}, bf16[176,1408]{1,0:T(8,128)(2,1)S(1)}, u32[]{:S(2)}, u32[]{:S(2)}) collective-permute-start(bf16[176,1408]{1,0:T(8,128)(2,1)S(1)} %copy-done), channel_id=1, source_target_pairs={{0,1},{1,0},{2,3},{3,2},{4,5},{5,4},{6,7},{7,6},{8,9},{9,8},{10,11... | collective-permute-start | bytes 1486856 | tf_op jit(solution)/shard_map/ppermute | solution.py:406
  30.3 2.8 %shard_map.139 = (bf16[384,384]{1,0:T(8,128)(2,1)S(1)}, bf16[384,384]{1,0:T(8,128)(2,1)S(1)}) custom-call(s32[2,192]{1,0:T(2,128)S(1)} %get-tuple-element.22.slot_keys, bf16[352,384]{1,0:T(8,128)(2,1)S(1)} %get-tuple-element.28.block0, bf16[352,384]{1,0:T(8,128)(2,1)S(1)} %collective-permute-done.8.block1, ...), custom_call_target="tpu_custom_call" | custom-call | tf_op jit(solution)/shard_map/pallas_call | solution.py:397
  33.1 3.5 %collective-permute-done.1.ask1 = bf16[48,3712]{1,0:T(8,128)(2,1)S(1)} collective-permute-done((bf16[48,3712]{1,0:T(8,128)(2,1)S(1)}, bf16[48,3712]{1,0:T(8,128)(2,1)S(1)}, u32[]{:S(2)}, u32[]{:S(2)}) %collective-permute-start.1) | collective-permute-done | bytes 356384 | tf_op jit(solution)/shard_map/ppermute | solution.py:406
  37.1 6.0 %collective-permute-done.3.ask3 = bf16[48,3712]{1,0:T(8,128)(2,1)S(1)} collective-permute-done((bf16[48,3712]{1,0:T(8,128)(2,1)S(1)}, bf16[48,3712]{1,0:T(8,128)(2,1)S(1)}, u32[]{:S(2)}, u32[]{:S(2)}) %collective-permute-start.3) | collective-permute-done | bytes 356384 | tf_op jit(solution)/shard_map/ppermute | solution.py:406
  43.8 2.3 %shard_map.140 = (bf16[96,1408]{1,0:T(8,128)(2,1)S(1)}, bf16[96,1408]{1,0:T(8,128)(2,1)S(1)}, bf16[96,1408]{1,0:T(8,128)(2,1)S(1)}, bf16[96,1408]{1,0:T(8,128)(2,1)S(1)}) custom-call(s32[2,192]{1,0:T(2,128)S(1)} %get-tuple-element.22.slot_keys, bf16[384,384]{1,0:T(8,128)(2,1)S(1)} %get-tuple-element.32.own_slots, ...), custom_call_target="tpu_custom_call" | custom-call | tf_op jit(solution)/shard_map/pallas_call | solution.py:397
  46.1 1.8 %collective-permute-start.16 = (bf16[96,1408]{1,0:T(8,128)(2,1)S(1)}, bf16[96,1408]{1,0:T(8,128)(2,1)S(1)}, u32[]{:S(2)}, u32[]{:S(2)}) collective-permute-start(bf16[96,1408]{1,0:T(8,128)(2,1)S(1)} %get-tuple-element.36), channel_id=1, source_target_pairs={{0,2},{1,3},{2,0},{3,1},{4,6},{5,7},{6,4},{7,5},{8,10},{9,11},{10,... | collective-permute-start | bytes 811016 | tf_op jit(solution)/shard_map/ppermute | solution.py:406
  47.9 1.5 %collective-permute-start.17 = (bf16[96,1408]{1,0:T(8,128)(2,1)S(1)}, bf16[96,1408]{1,0:T(8,128)(2,1)S(1)}, u32[]{:S(2)}, u32[]{:S(2)}) collective-permute-start(bf16[96,1408]{1,0:T(8,128)(2,1)S(1)} %get-tuple-element.37), channel_id=1, source_target_pairs={{0,4},{1,5},{2,6},{3,7},{4,0},{5,1},{6,2},{7,3},{8,12},{9,13},{10,... | collective-permute-start | bytes 811016 | tf_op jit(solution)/shard_map/ppermute | solution.py:406
  49.7 2.2 %shard_map.138.predicted = f32[192,1408]{1,0:T(8,128)S(1)} custom-call(bf16[48,384]{1,0:T(8,128)(2,1)S(1)} %get-tuple-element.24.ask0, bf16[48,3712]{1,0:T(8,128)(2,1)S(1)} %collective-permute-done.1.ask1, bf16[48,3712]{1,0:T(8,128)(2,1)S(1)} %collective-permute-done.2.ask2, bf16[48,3712]{1,0:T(8,128)(2,1)S(1)} %collective-permute-done.3.ask3, ...), custom_call_target="tpu_custom_call" | custom-call | tf_op jit(solution)/shard_map/pallas_call | solution.py:397
  51.9 3.5 %collective-permute-done.16.part1 = bf16[96,1408]{1,0:T(8,128)(2,1)S(1)} collective-permute-done((bf16[96,1408]{1,0:T(8,128)(2,1)S(1)}, bf16[96,1408]{1,0:T(8,128)(2,1)S(1)}, u32[]{:S(2)}, u32[]{:S(2)}) %collective-permute-start.16) | collective-permute-done | bytes 270368 | tf_op jit(solution)/shard_map/ppermute | solution.py:406
  55.4 6.8 %collective-permute-done.17.part2 = bf16[96,1408]{1,0:T(8,128)(2,1)S(1)} collective-permute-done((bf16[96,1408]{1,0:T(8,128)(2,1)S(1)}, bf16[96,1408]{1,0:T(8,128)(2,1)S(1)}, u32[]{:S(2)}, u32[]{:S(2)}) %collective-permute-start.17) | collective-permute-done | bytes 270368 | tf_op jit(solution)/shard_map/ppermute | solution.py:406
  62.3 1.3 %shard_map.141 = bf16[192,1408]{1,0:T(8,128)(2,1)} custom-call(s32[2,384]{1,0:T(2,128)S(1)} %copy-done.13, f32[192,1408]{1,0:T(8,128)S(1)} %shard_map.138.predicted, bf16[96,1408]{1,0:T(8,128)(2,1)S(1)} %get-tuple-element.35.part0, bf16[96,1408]{1,0:T(8,128)(2,1)S(1)} %collective-permute-done.16.part1, bf16[96,1408]{1,0:T(8,128)(2,1)S(1)} %collective-permute-done.17.part2, ...), custom_call_target="tpu_custom_call" | custom-call | tf_op jit(solution)/shard_map/pallas_call | solution.py:397
  (42 shorter events, 2.7 us)
Async XLA Ops:
  0.0 11.3 %copy-start = (bf16[176,1408]{1,0:T(8,128)(2,1)S(1)}, bf16[176,1408]{1,0:T(8,128)(2,1)}, u32[]{:S(2)}) copy-start(bf16[176,1408]{1,0:T(8,128)(2,1)} %w_own.1) | copy-start | bytes 1486852
  0.0 1.0 %copy-start.1 = (bf16[1,128,1408]{2,1,0:T(8,128)(2,1)S(1)}, bf16[1,128,1408]{2,1,0:T(8,128)(2,1)}, u32[]{:S(2)}) copy-start(bf16[1,128,1408]{2,1,0:T(8,128)(2,1)} %param.14) | copy-start | bytes 1081348
  1.0 1.0 %copy-start.2 = (bf16[1,128,1408]{2,1,0:T(8,128)(2,1)S(1)}, bf16[1,128,1408]{2,1,0:T(8,128)(2,1)}, u32[]{:S(2)}) copy-start(bf16[1,128,1408]{2,1,0:T(8,128)(2,1)} %param.15) | copy-start | bytes 1081348
  2.0 1.0 %copy-start.3 = (bf16[1,128,1408]{2,1,0:T(8,128)(2,1)S(1)}, bf16[1,128,1408]{2,1,0:T(8,128)(2,1)}, u32[]{:S(2)}) copy-start(bf16[1,128,1408]{2,1,0:T(8,128)(2,1)} %param.16) | copy-start | bytes 1081348
  3.0 1.0 %copy-start.4 = (bf16[1,128,1408]{2,1,0:T(8,128)(2,1)S(1)}, bf16[1,128,1408]{2,1,0:T(8,128)(2,1)}, u32[]{:S(2)}) copy-start(bf16[1,128,1408]{2,1,0:T(8,128)(2,1)} %param.17) | copy-start | bytes 1081348
  4.0 0.9 %copy-start.5 = (bf16[48,1408]{1,0:T(8,128)(2,1)S(1)}, bf16[48,1408]{1,0:T(8,128)(2,1)}, u32[]{:S(2)}) copy-start(bf16[48,1408]{1,0:T(8,128)(2,1)} %wp.1) | copy-start | bytes 405508
  4.9 0.8 %copy-start.7 = (bf16[48,384]{1,0:T(8,128)(2,1)S(1)}, bf16[48,384]{1,0:T(8,128)(2,1)}, u32[]{:S(2)}) copy-start(bf16[48,384]{1,0:T(8,128)(2,1)} %wq.1) | copy-start | bytes 110596
  5.7 0.8 %copy-start.8 = (bf16[48,384]{1,0:T(8,128)(2,1)S(1)}, bf16[48,384]{1,0:T(8,128)(2,1)}, u32[]{:S(2)}) copy-start(bf16[48,384]{1,0:T(8,128)(2,1)} %wk.1) | copy-start | bytes 110596
  6.4 0.8 %copy-start.9 = (bf16[48,384]{1,0:T(8,128)(2,1)S(1)}, bf16[48,384]{1,0:T(8,128)(2,1)}, u32[]{:S(2)}) copy-start(bf16[48,384]{1,0:T(8,128)(2,1)} %wv.1) | copy-start | bytes 110596
  7.2 0.8 %copy-start.10 = (bf16[48,384]{1,0:T(8,128)(2,1)S(1)}, bf16[48,384]{1,0:T(8,128)(2,1)}, u32[]{:S(2)}) copy-start(bf16[48,384]{1,0:T(8,128)(2,1)} %wo.1) | copy-start | bytes 110596
  8.0 0.7 %copy-start.11 = (bf16[1,32,384]{2,1,0:T(8,128)(2,1)S(1)}, bf16[1,32,384]{2,1,0:T(8,128)(2,1)}, u32[]{:S(2)}) copy-start(bf16[1,32,384]{2,1,0:T(8,128)(2,1)} %param.20) | copy-start | bytes 73732
  10.1 5.3 %copy-start.6 = (bf16[1,96,384]{2,1,0:T(8,128)(2,1)S(1)}, bf16[1,96,384]{2,1,0:T(8,128)(2,1)}, u32[]{:S(2)}) copy-start(bf16[1,96,384]{2,1,0:T(8,128)(2,1)} %param.19) | copy-start | bytes 221188
  10.7 6.8 %collective-permute-start.8 = (bf16[352,384]{1,0:T(8,128)(2,1)S(1)}, bf16[352,384]{1,0:T(8,128)(2,1)S(1)}, u32[]{:S(2)}, u32[]{:S(2)}) collective-permute-start(bf16[352,384]{1,0:T(8,128)(2,1)S(1)} %get-tuple-element.29), channel_id=1, source_target_pairs={{0,1},{1,0},{2,3},{3,2},{4,5},{5,4},{6,7},{7,6},{8,9},{9,8},{10,11... | collective-permute-start | bytes 811016 | tf_op jit(solution)/shard_map/ppermute | solution.py:406
  11.3 19.0 %collective-permute-start.12 = (bf16[176,1408]{1,0:T(8,128)(2,1)S(1)}, bf16[176,1408]{1,0:T(8,128)(2,1)S(1)}, u32[]{:S(2)}, u32[]{:S(2)}) collective-permute-start(bf16[176,1408]{1,0:T(8,128)(2,1)S(1)} %copy-done), channel_id=1, source_target_pairs={{0,4},{1,5},{2,6},{3,7},{4,0},{5,1},{6,2},{7,3},{8,12},{9,13},{10,... | collective-permute-start | bytes 1486856 | tf_op jit(solution)/shard_map/ppermute | solution.py:406
  13.9 9.3 %collective-permute-start.9 = (bf16[352,384]{1,0:T(8,128)(2,1)S(1)}, bf16[352,384]{1,0:T(8,128)(2,1)S(1)}, u32[]{:S(2)}, u32[]{:S(2)}) collective-permute-start(bf16[352,384]{1,0:T(8,128)(2,1)S(1)} %get-tuple-element.30), channel_id=1, source_target_pairs={{0,2},{1,3},{2,0},{3,1},{4,6},{5,7},{6,4},{7,5},{8,10},{9,11},{10,... | collective-permute-start | bytes 811016 | tf_op jit(solution)/shard_map/ppermute | solution.py:406
  15.3 12.6 %collective-permute-start.10 = (bf16[352,384]{1,0:T(8,128)(2,1)S(1)}, bf16[352,384]{1,0:T(8,128)(2,1)S(1)}, u32[]{:S(2)}, u32[]{:S(2)}) collective-permute-start(bf16[352,384]{1,0:T(8,128)(2,1)S(1)} %get-tuple-element.31), channel_id=1, source_target_pairs={{0,3},{1,2},{2,1},{3,0},{4,7},{5,6},{6,5},{7,4},{8,11},{9,10},{10,... | collective-permute-start | bytes 811016 | tf_op jit(solution)/shard_map/ppermute | solution.py:406
  15.4 1.5 %collective-permute-start = (bf16[96,384]{1,0:T(8,128)(2,1)S(1)}, bf16[96,384]{1,0:T(8,128)(2,1)S(1)}, u32[]{:S(2)}, u32[]{:S(2)}) collective-permute-start(bf16[96,384]{1,0:T(8,128)(2,1)S(1)} %bitcast.11), channel_id=1, source_target_pairs={{0,1},{1,0},{2,3},{3,2},{4,5},{5,4},{6,7},{7,6},{8,9},{9,8},{10,11... | collective-permute-start | bytes 221192 | tf_op jit(solution)/shard_map/ppermute | solution.py:406
  16.9 11.9 %collective-permute-start.15 = (bf16[96,1408]{1,0:T(8,128)(2,1)S(1)}, bf16[96,1408]{1,0:T(8,128)(2,1)S(1)}, u32[]{:S(2)}, u32[]{:S(2)}) collective-permute-start(bf16[96,1408]{1,0:T(8,128)(2,1)S(1)} %get-tuple-element.34.resid_own), channel_id=1, source_target_pairs={{0,1},{1,0},{2,3},{3,2},{4,5},{5,4},{6,7},{7,6},{8,9},{9,8},{10,11... | collective-permute-start | bytes 811016 | tf_op jit(solution)/shard_map/ppermute | solution.py:406
  17.6 19.0 %collective-permute-start.1 = (bf16[48,3712]{1,0:T(8,128)(2,1)S(1)}, bf16[48,3712]{1,0:T(8,128)(2,1)S(1)}, u32[]{:S(2)}, u32[]{:S(2)}) collective-permute-start(bf16[48,3712]{1,0:T(8,128)(2,1)S(1)} %get-tuple-element.25), channel_id=1, source_target_pairs={{0,2},{1,3},{2,0},{3,1},{4,6},{5,7},{6,4},{7,5},{8,10},{9,11},{10,... | collective-permute-start | bytes 1069064 | tf_op jit(solution)/shard_map/ppermute | solution.py:406
  23.2 13.4 %collective-permute-start.2 = (bf16[48,3712]{1,0:T(8,128)(2,1)S(1)}, bf16[48,3712]{1,0:T(8,128)(2,1)S(1)}, u32[]{:S(2)}, u32[]{:S(2)}) collective-permute-start(bf16[48,3712]{1,0:T(8,128)(2,1)S(1)} %get-tuple-element.26), channel_id=1, source_target_pairs={{0,4},{1,5},{2,6},{3,7},{4,0},{5,1},{6,2},{7,3},{8,12},{9,13},{10,... | collective-permute-start | bytes 1069064 | tf_op jit(solution)/shard_map/ppermute | solution.py:406
  28.0 15.2 %collective-permute-start.3 = (bf16[48,3712]{1,0:T(8,128)(2,1)S(1)}, bf16[48,3712]{1,0:T(8,128)(2,1)S(1)}, u32[]{:S(2)}, u32[]{:S(2)}) collective-permute-start(bf16[48,3712]{1,0:T(8,128)(2,1)S(1)} %get-tuple-element.27), channel_id=1, source_target_pairs={{0,6},{1,7},{2,4},{3,5},{4,2},{5,3},{6,0},{7,1},{8,14},{9,15},{10,... | collective-permute-start | bytes 1069064 | tf_op jit(solution)/shard_map/ppermute | solution.py:406
  28.8 14.3 %collective-permute-start.13 = (bf16[176,1408]{1,0:T(8,128)(2,1)S(1)}, bf16[176,1408]{1,0:T(8,128)(2,1)S(1)}, u32[]{:S(2)}, u32[]{:S(2)}) collective-permute-start(bf16[176,1408]{1,0:T(8,128)(2,1)S(1)} %copy-done), channel_id=1, source_target_pairs={{0,1},{1,0},{2,3},{3,2},{4,5},{5,4},{6,7},{7,6},{8,9},{9,8},{10,11... | collective-permute-start | bytes 1486856 | tf_op jit(solution)/shard_map/ppermute | solution.py:406
  30.2 13.5 %collective-permute-start.14 = (bf16[176,1408]{1,0:T(8,128)(2,1)S(1)}, bf16[176,1408]{1,0:T(8,128)(2,1)S(1)}, u32[]{:S(2)}, u32[]{:S(2)}) collective-permute-start(bf16[176,1408]{1,0:T(8,128)(2,1)S(1)} %collective-permute-done.12.w_cam), channel_id=1, source_target_pairs={{0,1},{1,0},{2,3},{3,2},{4,5},{5,4},{6,7},{7,6},{8,9},{9,8},{10,11... | collective-permute-start | bytes 1486856 | tf_op jit(solution)/shard_map/ppermute | solution.py:406
  36.6 7.1 %collective-permute-start.11 = (bf16[384,384]{1,0:T(8,128)(2,1)S(1)}, bf16[384,384]{1,0:T(8,128)(2,1)S(1)}, u32[]{:S(2)}, u32[]{:S(2)}) collective-permute-start(bf16[384,384]{1,0:T(8,128)(2,1)S(1)} %get-tuple-element.33), channel_id=1, source_target_pairs={{0,1},{1,0},{2,3},{3,2},{4,5},{5,4},{6,7},{7,6},{8,9},{9,8},{10,11... | collective-permute-start | bytes 884744 | tf_op jit(solution)/shard_map/ppermute | solution.py:406
  36.6 12.8 %collective-permute-start.5 = (bf16[48,3712]{1,0:T(8,128)(2,1)S(1)}, bf16[48,3712]{1,0:T(8,128)(2,1)S(1)}, u32[]{:S(2)}, u32[]{:S(2)}) collective-permute-start(bf16[48,3712]{1,0:T(8,128)(2,1)S(1)} %collective-permute-done.1.ask1), channel_id=1, source_target_pairs={{0,1},{1,0},{2,3},{3,2},{4,5},{5,4},{6,7},{7,6},{8,9},{9,8},{10,11... | collective-permute-start | bytes 1069064 | tf_op jit(solution)/shard_map/ppermute | solution.py:406
  43.2 4.7 %collective-permute-start.4 = (bf16[48,3328]{1,0:T(8,128)(2,1)S(1)}, bf16[48,3328]{1,0:T(8,128)(2,1)S(1)}, u32[]{:S(2)}, u32[]{:S(2)}) collective-permute-start(bf16[48,3328]{1,0:T(8,128)(2,1)S(1)} %get-tuple-element.23.pack.own_pack), channel_id=1, source_target_pairs={{0,1},{1,0},{2,3},{3,2},{4,5},{5,4},{6,7},{7,6},{8,9},{9,8},{10,11... | collective-permute-start | bytes 958472 | tf_op jit(solution)/shard_map/ppermute | solution.py:406
  43.2 6.5 %collective-permute-start.6 = (bf16[48,3712]{1,0:T(8,128)(2,1)S(1)}, bf16[48,3712]{1,0:T(8,128)(2,1)S(1)}, u32[]{:S(2)}, u32[]{:S(2)}) collective-permute-start(bf16[48,3712]{1,0:T(8,128)(2,1)S(1)} %collective-permute-done.2.ask2), channel_id=1, source_target_pairs={{0,1},{1,0},{2,3},{3,2},{4,5},{5,4},{6,7},{7,6},{8,9},{9,8},{10,11... | collective-permute-start | bytes 1069064 | tf_op jit(solution)/shard_map/ppermute | solution.py:406
  43.7 6.0 %collective-permute-start.7 = (bf16[48,3712]{1,0:T(8,128)(2,1)S(1)}, bf16[48,3712]{1,0:T(8,128)(2,1)S(1)}, u32[]{:S(2)}, u32[]{:S(2)}) collective-permute-start(bf16[48,3712]{1,0:T(8,128)(2,1)S(1)} %collective-permute-done.3.ask3), channel_id=1, source_target_pairs={{0,1},{1,0},{2,3},{3,2},{4,5},{5,4},{6,7},{7,6},{8,9},{9,8},{10,11... | collective-permute-start | bytes 1069064 | tf_op jit(solution)/shard_map/ppermute | solution.py:406
  46.1 9.3 %collective-permute-start.16 = (bf16[96,1408]{1,0:T(8,128)(2,1)S(1)}, bf16[96,1408]{1,0:T(8,128)(2,1)S(1)}, u32[]{:S(2)}, u32[]{:S(2)}) collective-permute-start(bf16[96,1408]{1,0:T(8,128)(2,1)S(1)} %get-tuple-element.36), channel_id=1, source_target_pairs={{0,2},{1,3},{2,0},{3,1},{4,6},{5,7},{6,4},{7,5},{8,10},{9,11},{10,... | collective-permute-start | bytes 811016 | tf_op jit(solution)/shard_map/ppermute | solution.py:406
  47.9 14.3 %collective-permute-start.17 = (bf16[96,1408]{1,0:T(8,128)(2,1)S(1)}, bf16[96,1408]{1,0:T(8,128)(2,1)S(1)}, u32[]{:S(2)}, u32[]{:S(2)}) collective-permute-start(bf16[96,1408]{1,0:T(8,128)(2,1)S(1)} %get-tuple-element.37), channel_id=1, source_target_pairs={{0,4},{1,5},{2,6},{3,7},{4,0},{5,1},{6,2},{7,3},{8,12},{9,13},{10,... | collective-permute-start | bytes 811016 | tf_op jit(solution)/shard_map/ppermute | solution.py:406
  49.4 12.8 %collective-permute-start.18 = (bf16[96,1408]{1,0:T(8,128)(2,1)S(1)}, bf16[96,1408]{1,0:T(8,128)(2,1)S(1)}, u32[]{:S(2)}, u32[]{:S(2)}) collective-permute-start(bf16[96,1408]{1,0:T(8,128)(2,1)S(1)} %get-tuple-element.38), channel_id=1, source_target_pairs={{0,6},{1,7},{2,4},{3,5},{4,2},{5,3},{6,0},{7,1},{8,14},{9,15},{10,... | collective-permute-start | bytes 811016 | tf_op jit(solution)/shard_map/ppermute | solution.py:406
  49.6 12.6 %copy-start.13 = (s32[2,384]{1,0:T(2,128)S(1)}, s32[2,384]{1,0:T(2,128)}, u32[]{:S(2)}) copy-start(s32[2,384]{1,0:T(2,128)} %owners.3) | copy-start | bytes 9220
  (2 other events, 1.3 us)

commit v3 on v2

--- a/solution.py
+++ b/solution.py
@@ -192,18 +192,39 @@
 
 def pack_kernel(
     capacity, query, key, value, resid, mask, owners, wq, wk, wv, wo, wp, context,
-    block0, block1, block2, block3, resid_rows, slot_keys, pack, stack, blocks,
+    block0, block1, block2, block3, resid_rows, slot_keys, pack,
+    stack, blocks, query_here, resid_here, mask_here, owners_here, done,
 ):
     cam, slab = position()
     tokens, width = key.shape
     masked = mask.shape[1]
     quarter = width // 8
+    context_rows, pred_width = context.shape
+    moves = [
+        (mask, mask_here),
+        (query, query_here),
+        (key, stack.at[0:tokens]),
+        (value, stack.at[tokens : 2 * tokens]),
+        (resid, resid_here),
+        (owners, owners_here),
+    ]
+    at = 0
+    for part in (wq, wk, wv, wo, wp):
+        moves.append((part, pack.at[:, at : at + part.shape[1]]))
+        at += part.shape[1]
+    moves.append((context, pack.at[0:context_rows, at:]))
+    copies = [
+        pltpu.make_async_copy(source, target, done.at[number])
+        for number, (source, target) in enumerate(moves)
+    ]
+    for copy in copies:
+        copy.start()
+    pack[context_rows:, at:] = jnp.zeros((pack.shape[0] - context_rows, pred_width), jnp.bfloat16)
     token = lax.broadcasted_iota(jnp.int32, (tokens, masked), 0)
-    chosen = jnp.where(token == mask[...], 1.0, 0.0).T.astype(jnp.bfloat16)
-    stack[0:tokens] = key[...]
-    stack[tokens : 2 * tokens] = value[...]
-    stack[2 * tokens :] = dot(chosen, query[...]).astype(jnp.bfloat16)
-    resid_rows[...] = dot(chosen, resid[...]).astype(jnp.bfloat16)
+    for copy in copies[:4]:
+        copy.wait()
+    chosen = jnp.where(token == mask_here[...], 1.0, 0.0).T.astype(jnp.bfloat16)
+    stack[2 * tokens :] = dot(chosen, query_here[...]).astype(jnp.bfloat16)
     row_total = stack.shape[0]
     pad = blocks.shape[2] - 2 * quarter
     for other in range(4):
@@ -214,6 +235,10 @@
         )
     for relation, out in enumerate((block0, block1, block2, block3)):
         out[...] = blocks[slab ^ relation]
+    for copy in copies[4:]:
+        copy.wait()
+    resid_rows[...] = dot(chosen, resid_here[...]).astype(jnp.bfloat16)
+    owners = owners_here
     listed = owners.shape[1]
     before = lax.broadcasted_iota(jnp.int32, (listed, listed), 0)
     after = lax.broadcasted_iota(jnp.int32, (listed, listed), 1)
@@ -230,33 +255,36 @@
     keys = owner_row * capacity + rank + jnp.where(odd, 8 * capacity, 0)
     slot_keys[0:1, :] = keys[:, 0 : 2 * masked]
     slot_keys[1:2, :] = keys[:, 2 * masked :]
-    at = 0
-    for part in (wq, wk, wv, wo, wp):
-        pack[:, at : at + part.shape[1]] = part[...]
-        at += part.shape[1]
-    pack[0 : context.shape[0], at:] = context[...]
-    pack[context.shape[0] :, at:] = jnp.zeros(
-        (pack.shape[0] - context.shape[0], context.shape[1]), jnp.bfloat16
-    )
-
-
-def ask_kernel(capacity, slot_keys, own_rows, peer_rows, pack, out0, out1, out2, out3, pair):
+
+
+def bundle_kernel(first, second, third, asked1, asked2, asked3, after, weights, contexts):
+    rows = first.shape[0]
+    for number, piece in enumerate((first, second, third)):
+        weights[number * rows : (number + 1) * rows] = piece[...]
+    rows = contexts.shape[0] // 3
+    for number, asked in enumerate((asked1, asked2, asked3)):
+        contexts[number * rows : (number + 1) * rows] = asked[asked.shape[0] - rows :]
+
+
+def ask_kernel(
+    capacity, slot_keys, own_rows, peer_rows, context, out0, out1, out2, out3, pair
+):
     cam, slab = position()
     rows = own_rows.shape[0]
     core = slab % 2
     pair[pl.ds(pl.multiple_of(core * rows, rows), rows)] = own_rows[...]
     pair[pl.ds(pl.multiple_of((1 - core) * rows, rows), rows)] = peer_rows[...]
     key_row = slot_keys[pl.ds(slab // 2, 1), :]
-    width = pack.shape[1]
     for relation, out in enumerate((out0, out1, out2, out3)):
         owner = (cam * 4 + slab) ^ (relation * 2)
         picker = slot_picker(key_row, owner, capacity, 8 * capacity)
-        picked = dot(picker, pair[...]).astype(jnp.bfloat16)
+        out[0 : 2 * capacity] = dot(picker, pair[...]).astype(jnp.bfloat16)
         if relation:
-            out[:, 0:width] = pack[...]
-            out[:, width:] = picked
-        else:
-            out[...] = picked
+            out[2 * capacity :] = context[...]
+
+
+def hold_kernel(pack, after, out):
+    out[...] = pack[:, 0 : out.shape[1]]
 
 
 def teacher_kernel(
@@ -325,25 +353,39 @@
 
 
 def predict_kernel(
-    context_rows, ask0, ask1, ask2, ask3, own_pack, peer0, peer1, peer2, peer3, out,
-    queries, weights, context,
+    ask0, ask1, ask2, ask3, own_pack, first, second, third, peer_pack, peer_weights, peer_contexts,
+    out, queries, weights, context,
 ):
     cam, slab = position()
+    parity = lax.axis_index("clip") % 2
     rows, width = ask0.shape
     own = cam * 4 + slab
-    side = own // 2
-    pieces = ((own_pack, peer0), (ask1, peer1), (ask2, peer2), (ask3, peer3))
-    wide = weights.shape[1]
-    for relation, both in enumerate(pieces):
-        asked = ask0[...] if relation == 0 else both[0][:, wide + width :]
-        queries[pl.ds(pl.multiple_of((side ^ relation) * rows, rows), rows)] = asked
-        for flip, piece in enumerate(both):
-            source = own ^ (relation * 2 + flip)
-            part = piece.shape[0]
-            weights[pl.ds(pl.multiple_of(source * part, part), part)] = piece[:, 0:wide]
-            context[pl.ds(pl.multiple_of(source * context_rows, context_rows), context_rows)] = (
-                piece[0:context_rows, wide : wide + width]
-            )
+    part, wide = first.shape
+    context_rows = peer_contexts.shape[0] // 3
+
+    def place(source, piece):
+        weights[pl.ds(pl.multiple_of(source * part, part), part)] = piece
+
+    def place_context(source, piece):
+        context[pl.ds(pl.multiple_of(source * context_rows, context_rows), context_rows)] = piece
+
+    for flip, piece in enumerate((own_pack, peer_pack)):
+        place(own ^ flip, piece[:, 0:wide])
+        place_context(own ^ flip, piece[0:context_rows, wide:])
+    for number, piece in enumerate((first, second, third)):
+        relation = (1 + parity, 2 - parity, 3)[number] * 2
+        place(own ^ relation, piece[...])
+        place(own ^ (relation + 1), peer_weights[number * part : (number + 1) * part])
+    for number, asked in enumerate((ask1, ask2, ask3)):
+        relation = (number + 1) * 2
+        place_context(own ^ relation, asked[rows:])
+        place_context(
+            own ^ (relation + 1),
+            peer_contexts[number * context_rows : (number + 1) * context_rows],
+        )
+    for relation, asked in enumerate((ask0, ask1, ask2, ask3)):
+        source = (own // 2) ^ relation
+        queries[pl.ds(pl.multiple_of(source * rows, rows), rows)] = asked[0:rows]
     head_size = width // P_HEADS
     scale = math.log2(math.e) / math.sqrt(head_size)
     asked = dot(queries[...], weights[:, 0:width]).astype(jnp.bfloat16)
@@ -392,18 +434,41 @@
         out[at] = jnp.where(filled, predicted[at] - goal, 0.0).astype(jnp.bfloat16)
 
 
-def call(kernel, outs, scratch, *args):
+def call(kernel, outs, scratch, *args, far=0, after=0, light=False):
     shapes = tuple(jax.ShapeDtypeStruct(shape, dtype) for shape, dtype in outs)
+    near = pl.BlockSpec(memory_space=pltpu.VMEM)
+    scratch_shapes = [pltpu.VMEM(shape, dtype) for shape, dtype in scratch]
+    if far:
+        scratch_shapes.append(pltpu.SemaphoreType.DMA((far,)))
+        args = [pltpu.with_memory_space_constraint(arg, pltpu.HBM) for arg in args[:far]] + list(args[far:])
     return pl.pallas_call(
         kernel,
         out_shape=shapes,
-        scratch_shapes=[pltpu.VMEM(shape, dtype) for shape, dtype in scratch],
+        in_specs=[pl.BlockSpec(memory_space=pltpu.HBM)] * far
+        + [near] * (len(args) - far - after)
+        + [pl.BlockSpec(memory_space=pl.ANY)] * after,
+        out_specs=tuple(near for _ in outs),
+        scratch_shapes=scratch_shapes,
         compiler_params=pltpu.CompilerParams(vmem_limit_bytes=40 * 2**20),
+        cost_estimate=pl.CostEstimate(flops=1, bytes_accessed=1, transcendentals=0) if light else None,
     )(*args)
 
 
 def send(rows, flip):
     return lax.ppermute(rows, ("cam", "slab"), [(source, source ^ flip) for source in range(8)])
+
+
+def send_alternating(rows, clips, even, odd):
+    pairs = [
+        (clip * 8 + source, clip * 8 + (source ^ (odd if clip % 2 else even)))
+        for clip in range(clips)
+        for source in range(8)
+    ]
+    return lax.ppermute(rows, ("clip", "cam", "slab"), pairs)
+
+
+def swap_clips(rows, clips):
+    return lax.ppermute(rows, "clip", [(clip, clip ^ 1) for clip in range(clips)])
 
 
 def paired_shards(
@@ -430,23 +495,31 @@
         functools.partial(pack_kernel, capacity),
         [block] * 4
         + [((masked, width), bf16), ((2, 2 * masked), jnp.int32), ((weight_rows, pack_width), bf16)],
-        [((block_rows, width), bf16), ((4, block_rows, padded), bf16)],
+        [
+            ((block_rows, width), bf16), ((4, block_rows, padded), bf16), ((tokens, width), bf16),
+            ((tokens, width), bf16), (mask_list.shape, jnp.int32), (owners.shape, jnp.int32),
+        ],
         t_query[0], t_key[0], t_value[0], t_resid[0], mask_list, owners,
-        w_query, w_key, w_value, w_out, w_proj, pred_context[0],
+        w_query, w_key, w_value, w_out, w_proj, pred_context[0], far=12,
     )
     other2, other3, other1 = send(block2, 2), send(block3, 3), send(block1, 1)
     w_both = send(w_cam, 1)
     peer_resid = send(resid_rows, 1)
-    ask_rows = 2 * capacity
-    ask = ((ask_rows, pack_width + pred_width), bf16)
+    ask = ((2 * capacity + context_rows, pred_width), bf16)
     ask0, ask1, ask2, ask3 = call(
         functools.partial(ask_kernel, capacity),
-        [((ask_rows, pred_width), bf16), ask, ask, ask],
+        [((2 * capacity, pred_width), bf16), ask, ask, ask],
         [((2 * masked, pred_width), bf16)],
-        slot_keys, pred_query[0], peer_query, pack,
+        slot_keys, pred_query[0], peer_query, pred_context[0],
     )
     asked1, asked2, asked3 = send(ask1, 2), send(ask2, 4), send(ask3, 6)
     peer_pack = send(pack, 1)
+    clips = lax.axis_size("clip")
+    shard = ((weight_rows, weight_width), bf16)
+    (held,) = call(hold_kernel, [shard], [], pack, other2, after=1, light=True)
+    first = send_alternating(held, clips, 2, 4)
+    third = send_alternating(first, clips, 4, 2)
+    second = swap_clips(first, clips)
     slots = ((16 * capacity, padded), bf16)
     own_slots, away_slots = call(
         functools.partial(teacher_kernel, capacity, head_size, tokens, masked),
@@ -466,15 +539,23 @@
         slot_keys, own_slots, peer_slots, w_out_teacher, w_cam, w_core, w_both, resid_rows, peer_resid,
     )
     far1, far2, far3 = send(part1, 2), send(part2, 4), send(part3, 6)
-    peer1, peer2, peer3 = send(asked1, 1), send(asked2, 1), send(asked3, 1)
+    bundle, contexts = call(
+        bundle_kernel,
+        [((3 * weight_rows, weight_width), bf16), ((3 * context_rows, pred_width), bf16)],
+        [],
+        first, second, third, asked1, asked2, asked3, part0,
+        after=1, light=True,
+    )
     (predicted,) = call(
-        functools.partial(predict_kernel, context_rows),
+        predict_kernel,
         [((8 * capacity, width), f32)],
         [
             ((8 * capacity, pred_width), bf16), ((8 * weight_rows, weight_width), bf16),
             ((8 * context_rows, pred_width), bf16),
         ],
-        ask0, asked1, asked2, asked3, pack, peer_pack, peer1, peer2, peer3,
+        ask0, asked1, asked2, asked3, pack, first, second, third, peer_pack, send(bundle, 1),
+        send(contexts, 1),
+        light=True,
     )
     (errors,) = call(
         functools.partial(finish_kernel, capacity, masked),
@@ -502,7 +583,7 @@
         P(("clip", "cam"), "slab"),
         P("clip", None),
     )
-    small = (mesh.shape["cam"], mesh.shape["slab"]) == (2, 4)
+    small = (mesh.shape["cam"], mesh.shape["slab"]) == (2, 4) and mesh.shape["clip"] % 2 == 0
     return jax.shard_map(
         paired_shards if small else shards,
         mesh=mesh,

time: 64.1 us -> 52.9 us (0.83)
  local copies, waits for them, and re-layouts: 10.1 us -> 0.02 us
  waiting for transfers between devices: 29.7 us -> 24.8 us
  starting transfers between devices: 14.2 us -> 16.5 us
  Pallas kernels: 9.55 us -> 11.3 us
    unnamed x30 -> x8, local copies, waits for them, and re-layouts: 10.1 us -> 0.02 us
    ppermute x19 -> x18, waiting for transfers between devices: 29.7 us -> 23.4 us  [send(): lax.ppermute(rows, ('cam', 'slab'), [(source, source ^ flip) for source i...]
    ppermute x0 -> x3, starting transfers between devices: none -> 1.86 us  [the longest x2 1.85 us: send_alternating(): return lax.ppermute(rows, ('clip', 'cam', 'slab'), pairs)]
    pallas_call x6 -> x8, Pallas kernels: 9.55 us -> 11.3 us  [call(): pl.pallas_call(kernel, out_shape=shapes, in_specs=[pl.BlockSpec(memory_sp...]
    ppermute x0 -> x3, waiting for transfers between devices: none -> 1.42 us  [the longest x2 1.42 us: send_alternating(): return lax.ppermute(rows, ('clip', 'cam', 'slab'), pairs)]
    ppermute x19 -> x18, starting transfers between devices: 14.2 us -> 14.7 us  [send(): lax.ppermute(rows, ('cam', 'slab'), [(source, source ^ flip) for source i...]
  transfers between devices with their start and end apart: 19 -> 21, of which waited for: 7 -> 7; matrix products, arithmetic and copies ran while one was open for 0% -> 0% of each run, Pallas kernels for 12% -> 19%
where the time goes in v3:
time: 52.9 us; the launch traced here: 52.8 us
  waiting for transfers between devices  24.8 us (47%)
  starting transfers between devices  16.5 us (31%)
  Pallas kernels  11.3 us (21%)
    ppermute x18, waiting for transfers between devices, send(): lax.ppermute(rows, ('cam', 'slab'), [(source, source ^ flip) for source i...  23.4 us
    ppermute x18, starting transfers between devices, send(): lax.ppermute(rows, ('cam', 'slab'), [(source, source ^ flip) for source i...  14.7 us
    pallas_call x8, Pallas kernels, call(): pl.pallas_call(kernel, out_shape=shapes, in_specs=[pl.BlockSpec(memory_sp...  11.3 us
    ppermute x2, starting transfers between devices, send_alternating(): return lax.ppermute(rows, ('clip', 'cam', 'slab'), pairs)  1.85 us
    ppermute x2, waiting for transfers between devices, send_alternating(): return lax.ppermute(rows, ('clip', 'cam', 'slab'), pairs)  1.42 us
  transfers between devices with their start and end apart: 21, of which 7 were waited for; matrix products, arithmetic and copies ran while one was open for 0% of the time, Pallas kernels for 19%

profile of v3, /device:TPU:0, one launch (start us, length us, event | category | flops | bytes accessed | tf_op | source)
XLA Modules:
  0.0 52.8 jit_solution(13185614673587844513)
XLA Ops:
  0.0 3.0 %collective-permute-start.12 = (bf16[176,1408]{1,0:T(8,128)(2,1)}, bf16[176,1408]{1,0:T(8,128)(2,1)S(1)}, u32[]{:S(2)}, u32[]{:S(2)}) collective-permute-start(bf16[176,1408]{1,0:T(8,128)(2,1)} %w_own.1), channel_id=1, source_target_pairs={{0,4},{1,5},{2,6},{3,7},{4,0},{5,1},{6,2},{7,3},{8,12},{9,13},{10,... | collective-permute-start | bytes 1486856 | tf_op jit(solution)/shard_map/ppermute | solution.py:458
  3.0 2.4 %shard_map.136 = (bf16[352,384]{1,0:T(8,128)(2,1)S(1)}, bf16[352,384]{1,0:T(8,128)(2,1)S(1)}, bf16[352,384]{1,0:T(8,128)(2,1)S(1)}, bf16[352,384]{1,0:T(8,128)(2...) custom-call(bf16[128,1408]{1,0:T(8,128)(2,1)} %bitcast.11, ...), custom_call_target="tpu_custom_call" | custom-call | tf_op jit(solution)/shard_map/pallas_call | solution.py:444
  5.3 0.0 copy-start.1
  5.3 1.6 %collective-permute-start.4 = (bf16[352,384]{1,0:T(8,128)(2,1)S(1)}, bf16[352,384]{1,0:T(8,128)(2,1)S(1)}, u32[]{:S(2)}, u32[]{:S(2)}) collective-permute-start(bf16[352,384]{1,0:T(8,128)(2,1)S(1)} %get-tuple-element.30), channel_id=1, source_target_pairs={{0,2},{1,3},{2,0},{3,1},{4,6},{5,7},{6,4},{7,5},{8,10},{9,11},{10,... | collective-permute-start | bytes 811016 | tf_op jit(solution)/shard_map/ppermute | solution.py:458
  6.9 0.6 %collective-permute-start.9 = (bf16[352,384]{1,0:T(8,128)(2,1)S(1)}, bf16[352,384]{1,0:T(8,128)(2,1)S(1)}, u32[]{:S(2)}, u32[]{:S(2)}) collective-permute-start(bf16[352,384]{1,0:T(8,128)(2,1)S(1)} %get-tuple-element.32), channel_id=1, source_target_pairs={{0,1},{1,0},{2,3},{3,2},{4,5},{5,4},{6,7},{7,6},{8,9},{9,8},{10,11... | collective-permute-start | bytes 811016 | tf_op jit(solution)/shard_map/ppermute | solution.py:458
  7.6 7.3 %collective-permute-done.4.after.block2 = bf16[352,384]{1,0:T(8,128)(2,1)S(1)} collective-permute-done((bf16[352,384]{1,0:T(8,128)(2,1)S(1)}, bf16[352,384]{1,0:T(8,128)(2,1)S(1)}, u32[]{:S(2)}, u32[]{:S(2)}) %collective-permute-start.4) | collective-permute-done | bytes 270368 | tf_op jit(solution)/shard_map/ppermute | solution.py:458
  14.8 1.6 %collective-permute-start.5 = (bf16[48,2944]{1,0:T(8,128)(2,1)S(1)}, bf16[48,2944]{1,0:T(8,128)(2,1)S(1)}, u32[]{:S(2)}, u32[]{:S(2)}) collective-permute-start(bf16[48,2944]{1,0:T(8,128)(2,1)S(1)} %shard_map.138), channel_id=1, source_target_pairs={{0,2},{1,3},{2,0},{3,1},{4,6},{5,7},{6,4},{7,5},{8,12},{9,13},{10,... | collective-permute-start | bytes 847880 | tf_op jit(solution)/shard_map/ppermute | solution.py:467
  16.4 0.5 collective-permute-start.14
  16.9 2.7 %collective-permute-done.10.block3 = bf16[352,384]{1,0:T(8,128)(2,1)S(1)} collective-permute-done((bf16[352,384]{1,0:T(8,128)(2,1)S(1)}, bf16[352,384]{1,0:T(8,128)(2,1)S(1)}, u32[]{:S(2)}, u32[]{:S(2)}) %collective-permute-start.10) | collective-permute-done | bytes 270368 | tf_op jit(solution)/shard_map/ppermute | solution.py:458
  19.6 0.8 %collective-permute-start.15 = (bf16[96,1408]{1,0:T(8,128)(2,1)S(1)}, bf16[96,1408]{1,0:T(8,128)(2,1)S(1)}, u32[]{:S(2)}, u32[]{:S(2)}) collective-permute-start(bf16[96,1408]{1,0:T(8,128)(2,1)S(1)} %get-tuple-element.36.resid_own), channel_id=1, source_target_pairs={{0,1},{1,0},{2,3},{3,2},{4,5},{5,4},{6,7},{7,6},{8,9},{9,8},{10,11... | collective-permute-start | bytes 811016 | tf_op jit(solution)/shard_map/ppermute | solution.py:458
  20.4 0.1 collective-permute-start
  20.5 2.8 %shard_map.139 = (bf16[384,384]{1,0:T(8,128)(2,1)S(1)}, bf16[384,384]{1,0:T(8,128)(2,1)S(1)}) custom-call(s32[2,192]{1,0:T(2,128)S(1)} %get-tuple-element.24.slot_keys, bf16[352,384]{1,0:T(8,128)(2,1)S(1)} %get-tuple-element.31.block0, bf16[352,384]{1,0:T(8,128)(2,1)S(1)} %collective-permute-done.9.block1, ...), custom_call_target="tpu_custom_call" | custom-call | tf_op jit(solution)/shard_map/pallas_call | solution.py:444
  23.3 0.5 collective-permute-start.11
  23.8 1.4 %collective-permute-done.5.first = bf16[48,2944]{1,0:T(8,128)(2,1)S(1)} collective-permute-done((bf16[48,2944]{1,0:T(8,128)(2,1)S(1)}, bf16[48,2944]{1,0:T(8,128)(2,1)S(1)}, u32[]{:S(2)}, u32[]{:S(2)}) %collective-permute-start.5) | collective-permute-done | bytes 282656 | tf_op jit(solution)/shard_map/ppermute | solution.py:467
  25.2 0.3 collective-permute-start.7
  25.5 0.3 shard_map.137
  25.8 1.8 %collective-permute-start.1 = (bf16[80,384]{1,0:T(8,128)(2,1)S(1)}, bf16[80,384]{1,0:T(8,128)(2,1)S(1)}, u32[]{:S(2)}, u32[]{:S(2)}) collective-permute-start(bf16[80,384]{1,0:T(8,128)(2,1)S(1)} %get-tuple-element.26), channel_id=1, source_target_pairs={{0,2},{1,3},{2,0},{3,1},{4,6},{5,7},{6,4},{7,5},{8,10},{9,11},{10,... | collective-permute-start | bytes 184328 | tf_op jit(solution)/shard_map/ppermute | solution.py:458
  27.6 1.5 %collective-permute-start.2 = (bf16[80,384]{1,0:T(8,128)(2,1)S(1)}, bf16[80,384]{1,0:T(8,128)(2,1)S(1)}, u32[]{:S(2)}, u32[]{:S(2)}) collective-permute-start(bf16[80,384]{1,0:T(8,128)(2,1)S(1)} %get-tuple-element.27), channel_id=1, source_target_pairs={{0,4},{1,5},{2,6},{3,7},{4,0},{5,1},{6,2},{7,3},{8,12},{9,13},{10,... | collective-permute-start | bytes 184328 | tf_op jit(solution)/shard_map/ppermute | solution.py:458
  29.1 0.3 collective-permute-start.3
  29.4 2.3 %shard_map.140 = (bf16[96,1408]{1,0:T(8,128)(2,1)S(1)}, bf16[96,1408]{1,0:T(8,128)(2,1)S(1)}, bf16[96,1408]{1,0:T(8,128)(2,1)S(1)}, bf16[96,1408]{1,0:T(8,128)(2,1)S(1)}) custom-call(s32[2,192]{1,0:T(2,128)S(1)} %get-tuple-element.24.slot_keys, bf16[384,384]{1,0:T(8,128)(2,1)S(1)} %get-tuple-element.34.own_slots, ...), custom_call_target="tpu_custom_call" | custom-call | tf_op jit(solution)/shard_map/pallas_call | solution.py:444
  31.7 3.6 %collective-permute-done.2.asked2.ask2 = bf16[80,384]{1,0:T(8,128)(2,1)S(1)} collective-permute-done((bf16[80,384]{1,0:T(8,128)(2,1)S(1)}, bf16[80,384]{1,0:T(8,128)(2,1)S(1)}, u32[]{:S(2)}, u32[]{:S(2)}) %collective-permute-start.2) | collective-permute-done | bytes 61472 | tf_op jit(solution)/shard_map/ppermute | solution.py:458
  35.3 0.1 shard_map.141
  35.4 0.1 collective-permute-start.16
  35.5 0.5 collective-permute-start.8
  36.0 1.5 %collective-permute-start.18 = (bf16[96,1408]{1,0:T(8,128)(2,1)S(1)}, bf16[96,1408]{1,0:T(8,128)(2,1)S(1)}, u32[]{:S(2)}, u32[]{:S(2)}) collective-permute-start(bf16[96,1408]{1,0:T(8,128)(2,1)S(1)} %get-tuple-element.40), channel_id=1, source_target_pairs={{0,2},{1,3},{2,0},{3,1},{4,6},{5,7},{6,4},{7,5},{8,10},{9,11},{10,... | collective-permute-start | bytes 811016 | tf_op jit(solution)/shard_map/ppermute | solution.py:458
  37.5 0.5 collective-permute-start.19
  38.0 1.5 %collective-permute-start.20 = (bf16[96,1408]{1,0:T(8,128)(2,1)S(1)}, bf16[96,1408]{1,0:T(8,128)(2,1)S(1)}, u32[]{:S(2)}, u32[]{:S(2)}) collective-permute-start(bf16[96,1408]{1,0:T(8,128)(2,1)S(1)} %get-tuple-element.42), channel_id=1, source_target_pairs={{0,6},{1,7},{2,4},{3,5},{4,2},{5,3},{6,0},{7,1},{8,14},{9,15},{10,... | collective-permute-start | bytes 811016 | tf_op jit(solution)/shard_map/ppermute | solution.py:458
  39.5 1.3 %collective-permute-done.17.peer_contexts = bf16[96,384]{1,0:T(8,128)(2,1)S(1)} collective-permute-done((bf16[96,384]{1,0:T(8,128)(2,1)S(1)}, bf16[96,384]{1,0:T(8,128)(2,1)S(1)}, u32[]{:S(2)}, u32[]{:S(2)}) %collective-permute-start.17) | collective-permute-done | bytes 73760 | tf_op jit(solution)/shard_map/ppermute | solution.py:458
  40.7 2.2 %shard_map.142.predicted = f32[192,1408]{1,0:T(8,128)S(1)} custom-call(bf16[48,384]{1,0:T(8,128)(2,1)S(1)} %get-tuple-element.25.ask0, bf16[80,384]{1,0:T(8,128)(2,1)S(1)} %collective-permute-done.1.asked1.ask1, bf16[80,384]{1,0:T(8,128)(2,1)S(1)} %collective-permute-done.2.asked2.ask2, bf16[80,384]{1,0:T(8,128)(2,1)S(1)} %collective-permute-done.3.asked3.ask3, ...), custom_call_target="tpu_custom_call" | custom-call | flops 1 | bytes 1 | tf_op jit(solution)/shard_map/pallas_call | solution.py:444
  43.0 2.3 %collective-permute-done.18.part1 = bf16[96,1408]{1,0:T(8,128)(2,1)S(1)} collective-permute-done((bf16[96,1408]{1,0:T(8,128)(2,1)S(1)}, bf16[96,1408]{1,0:T(8,128)(2,1)S(1)}, u32[]{:S(2)}, u32[]{:S(2)}) %collective-permute-start.18) | collective-permute-done | bytes 270368 | tf_op jit(solution)/shard_map/ppermute | solution.py:458
  45.3 6.1 %collective-permute-done.19.part2 = bf16[96,1408]{1,0:T(8,128)(2,1)S(1)} collective-permute-done((bf16[96,1408]{1,0:T(8,128)(2,1)S(1)}, bf16[96,1408]{1,0:T(8,128)(2,1)S(1)}, u32[]{:S(2)}, u32[]{:S(2)}) %collective-permute-start.19) | collective-permute-done | bytes 270368 | tf_op jit(solution)/shard_map/ppermute | solution.py:458
  51.5 1.3 %shard_map.143 = bf16[192,1408]{1,0:T(8,128)(2,1)} custom-call(s32[2,384]{1,0:T(2,128)S(1)} %copy-done.3, f32[192,1408]{1,0:T(8,128)S(1)} %shard_map.142.predicted, bf16[96,1408]{1,0:T(8,128)(2,1)S(1)} %get-tuple-element.37.after.part0, bf16[96,1408]{1,0:T(8,128)(2,1)S(1)} %collective-permute-done.18.part1, ...), custom_call_target="tpu_custom_call" | custom-call | tf_op jit(solution)/shard_map/pallas_call | solution.py:444
  (26 shorter events, 0.1 us)
Async XLA Ops:
  0.0 16.4 %collective-permute-start.12 = (bf16[176,1408]{1,0:T(8,128)(2,1)}, bf16[176,1408]{1,0:T(8,128)(2,1)S(1)}, u32[]{:S(2)}, u32[]{:S(2)}) collective-permute-start(bf16[176,1408]{1,0:T(8,128)(2,1)} %w_own.1), channel_id=1, source_target_pairs={{0,4},{1,5},{2,6},{3,7},{4,0},{5,1},{6,2},{7,3},{8,12},{9,13},{10,... | collective-permute-start | bytes 1486856 | tf_op jit(solution)/shard_map/ppermute | solution.py:458
  3.0 13.4 %copy-start = (bf16[176,1408]{1,0:T(8,128)(2,1)S(1)}, bf16[176,1408]{1,0:T(8,128)(2,1)}, u32[]{:S(2)}) copy-start(bf16[176,1408]{1,0:T(8,128)(2,1)} %w_own.1) | copy-start | bytes 1486852
  3.0 17.5 %copy-start.2 = (bf16[1,96,384]{2,1,0:T(8,128)(2,1)S(1)}, bf16[1,96,384]{2,1,0:T(8,128)(2,1)}, u32[]{:S(2)}) copy-start(bf16[1,96,384]{2,1,0:T(8,128)(2,1)} %param.19) | copy-start | bytes 221188
  5.3 20.2 %copy-start.1 = (bf16[1,32,384]{2,1,0:T(8,128)(2,1)S(1)}, bf16[1,32,384]{2,1,0:T(8,128)(2,1)}, u32[]{:S(2)}) copy-start(bf16[1,32,384]{2,1,0:T(8,128)(2,1)} %param.20) | copy-start | bytes 73732
  5.3 9.5 %collective-permute-start.4 = (bf16[352,384]{1,0:T(8,128)(2,1)S(1)}, bf16[352,384]{1,0:T(8,128)(2,1)S(1)}, u32[]{:S(2)}, u32[]{:S(2)}) collective-permute-start(bf16[352,384]{1,0:T(8,128)(2,1)S(1)} %get-tuple-element.30), channel_id=1, source_target_pairs={{0,2},{1,3},{2,0},{3,1},{4,6},{5,7},{6,4},{7,5},{8,10},{9,11},{10,... | collective-permute-start | bytes 811016 | tf_op jit(solution)/shard_map/ppermute | solution.py:458
  6.9 12.7 %collective-permute-start.10 = (bf16[352,384]{1,0:T(8,128)(2,1)S(1)}, bf16[352,384]{1,0:T(8,128)(2,1)S(1)}, u32[]{:S(2)}, u32[]{:S(2)}) collective-permute-start(bf16[352,384]{1,0:T(8,128)(2,1)S(1)} %get-tuple-element.33), channel_id=1, source_target_pairs={{0,3},{1,2},{2,1},{3,0},{4,7},{5,6},{6,5},{7,4},{8,11},{9,10},{10,... | collective-permute-start | bytes 811016 | tf_op jit(solution)/shard_map/ppermute | solution.py:458
  6.9 13.5 %collective-permute-start.9 = (bf16[352,384]{1,0:T(8,128)(2,1)S(1)}, bf16[352,384]{1,0:T(8,128)(2,1)S(1)}, u32[]{:S(2)}, u32[]{:S(2)}) collective-permute-start(bf16[352,384]{1,0:T(8,128)(2,1)S(1)} %get-tuple-element.32), channel_id=1, source_target_pairs={{0,1},{1,0},{2,3},{3,2},{4,5},{5,4},{6,7},{7,6},{8,9},{9,8},{10,11... | collective-permute-start | bytes 811016 | tf_op jit(solution)/shard_map/ppermute | solution.py:458
  14.8 10.4 %collective-permute-start.5 = (bf16[48,2944]{1,0:T(8,128)(2,1)S(1)}, bf16[48,2944]{1,0:T(8,128)(2,1)S(1)}, u32[]{:S(2)}, u32[]{:S(2)}) collective-permute-start(bf16[48,2944]{1,0:T(8,128)(2,1)S(1)} %shard_map.138), channel_id=1, source_target_pairs={{0,2},{1,3},{2,0},{3,1},{4,6},{5,7},{6,4},{7,5},{8,12},{9,13},{10,... | collective-permute-start | bytes 847880 | tf_op jit(solution)/shard_map/ppermute | solution.py:467
  16.4 9.4 %collective-permute-start.13 = (bf16[176,1408]{1,0:T(8,128)(2,1)S(1)}, bf16[176,1408]{1,0:T(8,128)(2,1)S(1)}, u32[]{:S(2)}, u32[]{:S(2)}) collective-permute-start(bf16[176,1408]{1,0:T(8,128)(2,1)S(1)} %copy-done), channel_id=1, source_target_pairs={{0,1},{1,0},{2,3},{3,2},{4,5},{5,4},{6,7},{7,6},{8,9},{9,8},{10,11... | collective-permute-start | bytes 1486856 | tf_op jit(solution)/shard_map/ppermute | solution.py:458
  16.4 12.7 %collective-permute-start.14 = (bf16[176,1408]{1,0:T(8,128)(2,1)S(1)}, bf16[176,1408]{1,0:T(8,128)(2,1)S(1)}, u32[]{:S(2)}, u32[]{:S(2)}) collective-permute-start(bf16[176,1408]{1,0:T(8,128)(2,1)S(1)} %collective-permute-done.12.w_cam), channel_id=1, source_target_pairs={{0,1},{1,0},{2,3},{3,2},{4,5},{5,4},{6,7},{7,6},{8,9},{9,8},{10,11... | collective-permute-start | bytes 1486856 | tf_op jit(solution)/shard_map/ppermute | solution.py:458
  19.6 5.6 %collective-permute-start.15 = (bf16[96,1408]{1,0:T(8,128)(2,1)S(1)}, bf16[96,1408]{1,0:T(8,128)(2,1)S(1)}, u32[]{:S(2)}, u32[]{:S(2)}) collective-permute-start(bf16[96,1408]{1,0:T(8,128)(2,1)S(1)} %get-tuple-element.36.resid_own), channel_id=1, source_target_pairs={{0,1},{1,0},{2,3},{3,2},{4,5},{5,4},{6,7},{7,6},{8,9},{9,8},{10,11... | collective-permute-start | bytes 811016 | tf_op jit(solution)/shard_map/ppermute | solution.py:458
  20.4 2.8 %collective-permute-start = (bf16[96,384]{1,0:T(8,128)(2,1)S(1)}, bf16[96,384]{1,0:T(8,128)(2,1)S(1)}, u32[]{:S(2)}, u32[]{:S(2)}) collective-permute-start(bf16[96,384]{1,0:T(8,128)(2,1)S(1)} %bitcast.9), channel_id=1, source_target_pairs={{0,1},{1,0},{2,3},{3,2},{4,5},{5,4},{6,7},{7,6},{8,9},{9,8},{10,11... | collective-permute-start | bytes 221192 | tf_op jit(solution)/shard_map/ppermute | solution.py:458
  23.3 4.3 %collective-permute-start.11 = (bf16[384,384]{1,0:T(8,128)(2,1)S(1)}, bf16[384,384]{1,0:T(8,128)(2,1)S(1)}, u32[]{:S(2)}, u32[]{:S(2)}) collective-permute-start(bf16[384,384]{1,0:T(8,128)(2,1)S(1)} %get-tuple-element.35), channel_id=1, source_target_pairs={{0,1},{1,0},{2,3},{3,2},{4,5},{5,4},{6,7},{7,6},{8,9},{9,8},{10,11... | collective-permute-start | bytes 884744 | tf_op jit(solution)/shard_map/ppermute | solution.py:458
  25.2 10.1 %collective-permute-start.6 = (bf16[48,2944]{1,0:T(8,128)(2,1)S(1)}, bf16[48,2944]{1,0:T(8,128)(2,1)S(1)}, u32[]{:S(2)}, u32[]{:S(2)}) collective-permute-start(bf16[48,2944]{1,0:T(8,128)(2,1)S(1)} %collective-permute-done.5.first), channel_id=1, source_target_pairs={{0,8},{8,0},{16,24},{24,16},{1,9},{9,1},{17,25},{25,17},{2,10},{10... | collective-permute-start | bytes 847880 | tf_op jit(solution)/shard_map/ppermute | solution.py:471
  25.2 10.1 %collective-permute-start.7 = (bf16[48,2944]{1,0:T(8,128)(2,1)S(1)}, bf16[48,2944]{1,0:T(8,128)(2,1)S(1)}, u32[]{:S(2)}, u32[]{:S(2)}) collective-permute-start(bf16[48,2944]{1,0:T(8,128)(2,1)S(1)} %collective-permute-done.5.first), channel_id=1, source_target_pairs={{0,4},{1,5},{2,6},{3,7},{4,0},{5,1},{6,2},{7,3},{8,10},{9,11},{10,... | collective-permute-start | bytes 847880 | tf_op jit(solution)/shard_map/ppermute | solution.py:467
  25.8 5.9 %collective-permute-start.1 = (bf16[80,384]{1,0:T(8,128)(2,1)S(1)}, bf16[80,384]{1,0:T(8,128)(2,1)S(1)}, u32[]{:S(2)}, u32[]{:S(2)}) collective-permute-start(bf16[80,384]{1,0:T(8,128)(2,1)S(1)} %get-tuple-element.26), channel_id=1, source_target_pairs={{0,2},{1,3},{2,0},{3,1},{4,6},{5,7},{6,4},{7,5},{8,10},{9,11},{10,... | collective-permute-start | bytes 184328 | tf_op jit(solution)/shard_map/ppermute | solution.py:458
  27.6 7.7 %collective-permute-start.2 = (bf16[80,384]{1,0:T(8,128)(2,1)S(1)}, bf16[80,384]{1,0:T(8,128)(2,1)S(1)}, u32[]{:S(2)}, u32[]{:S(2)}) collective-permute-start(bf16[80,384]{1,0:T(8,128)(2,1)S(1)} %get-tuple-element.27), channel_id=1, source_target_pairs={{0,4},{1,5},{2,6},{3,7},{4,0},{5,1},{6,2},{7,3},{8,12},{9,13},{10,... | collective-permute-start | bytes 184328 | tf_op jit(solution)/shard_map/ppermute | solution.py:458
  29.1 6.2 %collective-permute-start.3 = (bf16[80,384]{1,0:T(8,128)(2,1)S(1)}, bf16[80,384]{1,0:T(8,128)(2,1)S(1)}, u32[]{:S(2)}, u32[]{:S(2)}) collective-permute-start(bf16[80,384]{1,0:T(8,128)(2,1)S(1)} %get-tuple-element.28), channel_id=1, source_target_pairs={{0,6},{1,7},{2,4},{3,5},{4,2},{5,3},{6,0},{7,1},{8,14},{9,15},{10,... | collective-permute-start | bytes 184328 | tf_op jit(solution)/shard_map/ppermute | solution.py:458
  35.4 5.3 %collective-permute-start.16 = (bf16[144,2944]{1,0:T(8,128)(2,1)S(1)}, bf16[144,2944]{1,0:T(8,128)(2,1)S(1)}, u32[]{:S(2)}, u32[]{:S(2)}) collective-permute-start(bf16[144,2944]{1,0:T(8,128)(2,1)S(1)} %get-tuple-element.38), channel_id=1, source_target_pairs={{0,1},{1,0},{2,3},{3,2},{4,5},{5,4},{6,7},{7,6},{8,9},{9,8},{10,11... | collective-permute-start | bytes 2543624 | tf_op jit(solution)/shard_map/ppermute | solution.py:458
  35.5 4.0 %collective-permute-start.8 = (bf16[48,3328]{1,0:T(8,128)(2,1)S(1)}, bf16[48,3328]{1,0:T(8,128)(2,1)S(1)}, u32[]{:S(2)}, u32[]{:S(2)}) collective-permute-start(bf16[48,3328]{1,0:T(8,128)(2,1)S(1)} %get-tuple-element.29.pack.own_pack), channel_id=1, source_target_pairs={{0,1},{1,0},{2,3},{3,2},{4,5},{5,4},{6,7},{7,6},{8,9},{9,8},{10,11... | collective-permute-start | bytes 958472 | tf_op jit(solution)/shard_map/ppermute | solution.py:458
  36.0 9.3 %collective-permute-start.18 = (bf16[96,1408]{1,0:T(8,128)(2,1)S(1)}, bf16[96,1408]{1,0:T(8,128)(2,1)S(1)}, u32[]{:S(2)}, u32[]{:S(2)}) collective-permute-start(bf16[96,1408]{1,0:T(8,128)(2,1)S(1)} %get-tuple-element.40), channel_id=1, source_target_pairs={{0,2},{1,3},{2,0},{3,1},{4,6},{5,7},{6,4},{7,5},{8,10},{9,11},{10,... | collective-permute-start | bytes 811016 | tf_op jit(solution)/shard_map/ppermute | solution.py:458
  37.5 14.0 %collective-permute-start.19 = (bf16[96,1408]{1,0:T(8,128)(2,1)S(1)}, bf16[96,1408]{1,0:T(8,128)(2,1)S(1)}, u32[]{:S(2)}, u32[]{:S(2)}) collective-permute-start(bf16[96,1408]{1,0:T(8,128)(2,1)S(1)} %get-tuple-element.41), channel_id=1, source_target_pairs={{0,4},{1,5},{2,6},{3,7},{4,0},{5,1},{6,2},{7,3},{8,12},{9,13},{10,... | collective-permute-start | bytes 811016 | tf_op jit(solution)/shard_map/ppermute | solution.py:458
  38.0 13.5 %collective-permute-start.20 = (bf16[96,1408]{1,0:T(8,128)(2,1)S(1)}, bf16[96,1408]{1,0:T(8,128)(2,1)S(1)}, u32[]{:S(2)}, u32[]{:S(2)}) collective-permute-start(bf16[96,1408]{1,0:T(8,128)(2,1)S(1)} %get-tuple-element.42), channel_id=1, source_target_pairs={{0,6},{1,7},{2,4},{3,5},{4,2},{5,3},{6,0},{7,1},{8,14},{9,15},{10,... | collective-permute-start | bytes 811016 | tf_op jit(solution)/shard_map/ppermute | solution.py:458
  39.5 1.3 %collective-permute-start.17 = (bf16[96,384]{1,0:T(8,128)(2,1)S(1)}, bf16[96,384]{1,0:T(8,128)(2,1)S(1)}, u32[]{:S(2)}, u32[]{:S(2)}) collective-permute-start(bf16[96,384]{1,0:T(8,128)(2,1)S(1)} %get-tuple-element.39), channel_id=1, source_target_pairs={{0,1},{1,0},{2,3},{3,2},{4,5},{5,4},{6,7},{7,6},{8,9},{9,8},{10,11... | collective-permute-start | bytes 221192 | tf_op jit(solution)/shard_map/ppermute | solution.py:458
  40.7 10.7 %copy-start.3 = (s32[2,384]{1,0:T(2,128)S(1)}, s32[2,384]{1,0:T(2,128)}, u32[]{:S(2)}) copy-start(s32[2,384]{1,0:T(2,128)} %owners.3) | copy-start | bytes 9220

commit v4 on v3

--- a/solution.py
+++ b/solution.py
@@ -191,15 +191,17 @@
 
 
 def pack_kernel(
-    capacity, query, key, value, resid, mask, owners, wq, wk, wv, wo, wp, context,
-    block0, block1, block2, block3, resid_rows, slot_keys, pack,
+    capacity, query, key, value, resid, mask, owners, wq, wk, wv, wo, wp, asks, context, w_far,
+    block0, block2, block3, resid_rows, slot_keys, pack, message, w_here,
     stack, blocks, query_here, resid_here, mask_here, owners_here, done,
 ):
     cam, slab = position()
     tokens, width = key.shape
-    masked = mask.shape[1]
+    masked, pred_width = asks.shape
     quarter = width // 8
-    context_rows, pred_width = context.shape
+    context_rows = context.shape[0]
+    row_total = stack.shape[0]
+    part_rows, half = w_far.shape[0], masked // 2
     moves = [
         (mask, mask_here),
         (query, query_here),
@@ -207,25 +209,35 @@
         (value, stack.at[tokens : 2 * tokens]),
         (resid, resid_here),
         (owners, owners_here),
+        (w_far, w_here.at[0:part_rows]),
+        (asks, block2.at[row_total : row_total + masked]),
+        (context, block2.at[row_total + masked :]),
+        (asks.at[0:half], w_here.at[part_rows:, 0:pred_width]),
+        (asks.at[half:], w_here.at[part_rows:, pred_width : 2 * pred_width]),
+        (
+            context,
+            w_here.at[part_rows : part_rows + context_rows, 2 * pred_width : 3 * pred_width],
+        ),
     ]
     at = 0
     for part in (wq, wk, wv, wo, wp):
         moves.append((part, pack.at[:, at : at + part.shape[1]]))
         at += part.shape[1]
-    moves.append((context, pack.at[0:context_rows, at:]))
     copies = [
         pltpu.make_async_copy(source, target, done.at[number])
         for number, (source, target) in enumerate(moves)
     ]
     for copy in copies:
         copy.start()
-    pack[context_rows:, at:] = jnp.zeros((pack.shape[0] - context_rows, pred_width), jnp.bfloat16)
+    w_here[part_rows:, 3 * pred_width :] = jnp.zeros((half, width - 3 * pred_width), jnp.bfloat16)
+    w_here[part_rows + context_rows :, 2 * pred_width : 3 * pred_width] = jnp.zeros(
+        (half - context_rows, pred_width), jnp.bfloat16
+    )
     token = lax.broadcasted_iota(jnp.int32, (tokens, masked), 0)
     for copy in copies[:4]:
         copy.wait()
     chosen = jnp.where(token == mask_here[...], 1.0, 0.0).T.astype(jnp.bfloat16)
     stack[2 * tokens :] = dot(chosen, query_here[...]).astype(jnp.bfloat16)
-    row_total = stack.shape[0]
     pad = blocks.shape[2] - 2 * quarter
     for other in range(4):
         first = stack[:, other * quarter : (other + 1) * quarter]
@@ -233,70 +245,104 @@
         blocks[other] = jnp.concatenate(
             [first, second, jnp.zeros((row_total, pad), jnp.bfloat16)], axis=1
         )
-    for relation, out in enumerate((block0, block1, block2, block3)):
-        out[...] = blocks[slab ^ relation]
+    for relation, out in ((0, block0), (2, block2), (3, block3)):
+        out[0:row_total] = blocks[slab ^ relation]
+    core_block = blocks.at[slab ^ 1]
     for copy in copies[4:]:
         copy.wait()
     resid_rows[...] = dot(chosen, resid_here[...]).astype(jnp.bfloat16)
-    owners = owners_here
+    base = w_here.shape[0]
+    message[0:base] = w_here[...]
+    message[base : base + masked] = resid_rows[...]
+    base += masked
+    count = pack.shape[0]
+    message[base + 2 * count : base + 3 * count] = jnp.zeros((count, width), jnp.bfloat16)
+    for low in range(0, at, width):
+        high = min(low + width, at)
+        message[base : base + count, 0 : high - low] = pack[:, low:high]
+        base += count
+    message[base:] = jnp.zeros((tokens, width), jnp.bfloat16)
+    for number in range(3):
+        low, high = number * tokens, min((number + 1) * tokens, row_total)
+        lanes = slice(number * core_block.shape[1], (number + 1) * core_block.shape[1])
+        message[base : base + high - low, lanes] = core_block[low:high]
     listed = owners.shape[1]
     before = lax.broadcasted_iota(jnp.int32, (listed, listed), 0)
     after = lax.broadcasted_iota(jnp.int32, (listed, listed), 1)
     group = sum((before >= edge).astype(jnp.int32) for edge in range(masked, listed, masked))
     group_after = sum((after >= edge).astype(jnp.int32) for edge in range(masked, listed, masked))
     precedes = jnp.where((before < after) & (group == group_after), 1.0, 0.0)
-    owner_row = owners[pl.ds(cam, 1), :]
-    device = lax.broadcasted_iota(jnp.int32, (8, listed), 0)
-    owned = jnp.where(device == owner_row, 1.0, 0.0)
-    counted = dot(owned.astype(jnp.bfloat16), precedes.astype(jnp.bfloat16))
-    rank = jnp.sum(owned * counted, axis=0, keepdims=True).astype(jnp.int32)
+    precedes = precedes.astype(jnp.bfloat16)
     lane = lax.broadcasted_iota(jnp.int32, (1, listed), 1)
     odd = ((lane >= masked) & (lane < 2 * masked)) | (lane >= 3 * masked)
-    keys = owner_row * capacity + rank + jnp.where(odd, 8 * capacity, 0)
-    slot_keys[0:1, :] = keys[:, 0 : 2 * masked]
-    slot_keys[1:2, :] = keys[:, 2 * masked :]
-
-
-def bundle_kernel(first, second, third, asked1, asked2, asked3, after, weights, contexts):
-    rows = first.shape[0]
-    for number, piece in enumerate((first, second, third)):
-        weights[number * rows : (number + 1) * rows] = piece[...]
-    rows = contexts.shape[0] // 3
-    for number, asked in enumerate((asked1, asked2, asked3)):
-        contexts[number * rows : (number + 1) * rows] = asked[asked.shape[0] - rows :]
-
-
-def ask_kernel(
-    capacity, slot_keys, own_rows, peer_rows, context, out0, out1, out2, out3, pair
+    device = lax.broadcasted_iota(jnp.int32, (8, listed), 0)
+    for camera in range(2):
+        owner_row = owners_here[camera : camera + 1, :]
+        owned = jnp.where(device == owner_row, 1.0, 0.0)
+        counted = dot(owned.astype(jnp.bfloat16), precedes)
+        rank = jnp.sum(owned * counted, axis=0, keepdims=True).astype(jnp.int32)
+        keys = owner_row * capacity + rank + jnp.where(odd, 8 * capacity, 0)
+        slot_keys[2 * camera : 2 * camera + 1, :] = keys[:, 0 : 2 * masked]
+        slot_keys[2 * camera + 1 : 2 * camera + 2, :] = keys[:, 2 * masked :]
+
+
+def hold_kernel(base, pack, block, message, held, passed):
+    core = lax.axis_index("slab") % 2
+    rows, wide = pack.shape
+    width = message.shape[1]
+    held[pl.ds(pl.multiple_of(core * rows, rows), rows)] = pack[...]
+    other = pl.ds(pl.multiple_of((1 - core) * rows, rows), rows)
+    for number, low in enumerate(range(0, wide, width)):
+        high = min(low + width, wide)
+        at = base + number * rows
+        held[other, low:high] = message[at : at + rows, 0 : high - low]
+    passed[...] = block[block.shape[0] - passed.shape[0] :]
+
+
+def bundle_kernel(first, near, far, beside, after, out, forward):
+    rows, wide = first.shape
+    core = lax.axis_index("slab") % 2
+    part = forward.shape[0]
+    forward[...] = first[pl.ds(pl.multiple_of(core * part, part), part)]
+    out[:, 0:wide] = first[...]
+    asked_rows, width = far.shape
+    rest = asked_rows - rows
+    at = wide + 3 * width
+    for number, piece in enumerate((near.at[near.shape[0] - asked_rows :], far)):
+        out[:, wide + number * width : wide + (number + 1) * width] = piece[0:rows]
+        out[number * rest : (number + 1) * rest, at:] = piece[rows:]
+    base = beside.shape[0] - rows // 2
+    out[0 : rows // 2, at - width : at] = beside[base:, 0:width]
+    out[rows // 2 :, at - width : at] = beside[base:, width : 2 * width]
+    out[2 * rest : 3 * rest, at:] = beside[base : base + rest, 2 * width : 3 * width]
+    if 3 * rest < rows:
+        out[3 * rest :, at:] = jnp.zeros((rows - 3 * rest, width), jnp.bfloat16)
+
+
+def split_kernel(piece, after, left, right):
+    left[...] = piece[:, 0 : left.shape[1]]
+    right[...] = piece[:, left.shape[1] :]
+
+
+def teacher_kernel(
+    capacity, head_size, tokens, masked, slot_keys, block0, message, block2, block3, w_cam,
+    own_core, peer_core, w_pass, queries, keys, values, attended,
 ):
     cam, slab = position()
-    rows = own_rows.shape[0]
-    core = slab % 2
-    pair[pl.ds(pl.multiple_of(core * rows, rows), rows)] = own_rows[...]
-    pair[pl.ds(pl.multiple_of((1 - core) * rows, rows), rows)] = peer_rows[...]
-    key_row = slot_keys[pl.ds(slab // 2, 1), :]
-    for relation, out in enumerate((out0, out1, out2, out3)):
-        owner = (cam * 4 + slab) ^ (relation * 2)
-        picker = slot_picker(key_row, owner, capacity, 8 * capacity)
-        out[0 : 2 * capacity] = dot(picker, pair[...]).astype(jnp.bfloat16)
-        if relation:
-            out[2 * capacity :] = context[...]
-
-
-def hold_kernel(pack, after, out):
-    out[...] = pack[:, 0 : out.shape[1]]
-
-
-def teacher_kernel(
-    capacity, head_size, tokens, masked, slot_keys, block0, block1, block2, block3,
-    own_core, peer_core, queries, keys, values, attended,
-):
-    cam, slab = position()
-    for relation, block in enumerate((block0, block1, block2, block3)):
-        other = slab ^ relation
-        keys[relation * tokens : (relation + 1) * tokens] = block[0:tokens]
-        values[relation * tokens : (relation + 1) * tokens] = block[tokens : 2 * tokens]
-        queries[pl.ds(pl.multiple_of(other * masked, masked), masked)] = block[2 * tokens :]
+    w_pass[...] = w_cam[0 : w_pass.shape[0]]
+    wide, base = keys.shape[1], message.shape[0] - tokens
+    pieces = [message.at[base:, number * wide : (number + 1) * wide] for number in range(3)]
+    for relation, block in enumerate((block0, None, block2, block3)):
+        if relation == 1:
+            key_part, value_part, query_part = pieces
+            query_part = query_part.at[0:masked]
+        else:
+            key_part, value_part = block.at[0:tokens], block.at[tokens : 2 * tokens]
+            query_part = block.at[2 * tokens : 2 * tokens + masked]
+        keys[relation * tokens : (relation + 1) * tokens] = key_part[...]
+        values[relation * tokens : (relation + 1) * tokens] = value_part[...]
+        start = pl.multiple_of((slab ^ relation) * masked, masked)
+        queries[pl.ds(start, masked)] = query_part[...]
     scale = math.log2(math.e) / math.sqrt(head_size)
     chunk = 2 * masked
     for half in range(2):
@@ -316,7 +362,7 @@
         for relation in range(4):
             owner = (cam * 4 + slab) ^ (relation * 2 + flip)
             for half in range(2):
-                picker = slot_picker(slot_keys[half : half + 1, :], owner, capacity, 8 * capacity)
+                picker = slot_picker(slot_keys[pl.ds(2 * cam + half, 1), :], owner, capacity, 8 * capacity)
                 at = (relation * 2 + half) * 2 * capacity
                 out[at : at + 2 * capacity] = dot(
                     picker, attended[half * chunk : (half + 1) * chunk]
@@ -324,21 +370,24 @@
 
 
 def project_kernel(
-    capacity, slot_keys, own_slots, peer_slots, w_own, w_cam, w_core, w_both, resid_own, resid_peer,
+    capacity, slot_keys, own_slots, peer_slots, w_own, w_cam, w_core, w_both, resid_own,
     out0, out1, out2, out3, weight, resid_pair, total,
 ):
     cam, slab = position()
     core, chip = slab % 2, slab // 2
-    part, width = w_own.shape
+    width = w_own.shape[1]
+    part = width // 8
     half = own_slots.shape[1]
     for base, same, crossed in ((0, w_own, w_cam), (half, w_core, w_both)):
-        weight[pl.ds(pl.multiple_of(base + cam * part, 16), part)] = same[...]
-        weight[pl.ds(pl.multiple_of(base + (1 - cam) * part, 16), part)] = crossed[...]
+        weight[pl.ds(pl.multiple_of(base + cam * part, 16), part)] = same[0:part]
+        weight[pl.ds(pl.multiple_of(base + (1 - cam) * part, 16), part)] = crossed[0:part]
         weight[base + 2 * part : base + half] = jnp.zeros((half - 2 * part, width), jnp.bfloat16)
     rows = resid_own.shape[0]
     resid_pair[pl.ds(pl.multiple_of(core * rows, rows), rows)] = resid_own[...]
-    resid_pair[pl.ds(pl.multiple_of((1 - core) * rows, rows), rows)] = resid_peer[...]
-    key_row = slot_keys[pl.ds(chip, 1), :]
+    resid_pair[pl.ds(pl.multiple_of((1 - core) * rows, rows), rows)] = w_core[
+        w_own.shape[0] : w_own.shape[0] + rows
+    ]
+    key_row = slot_keys[pl.ds(2 * cam + chip, 1), :]
     block = out0.shape[0]
     for relation, out in ((3, out3), (2, out2), (1, out1), (0, out0)):
         at = relation * block
@@ -353,15 +402,18 @@
 
 
 def predict_kernel(
-    ask0, ask1, ask2, ask3, own_pack, first, second, third, peer_pack, peer_weights, peer_contexts,
-    out, queries, weights, context,
+    capacity, part_rows, slot_keys, w_own, w_core, w_cam, near, far,
+    held, first, third, peer_left, peer_right, peers, out,
+    queries, weights, context, asks,
 ):
     cam, slab = position()
-    parity = lax.axis_index("clip") % 2
-    rows, width = ask0.shape
+    core = slab % 2
     own = cam * 4 + slab
-    part, wide = first.shape
-    context_rows = peer_contexts.shape[0] // 3
+    part, wide = third.shape
+    width = far.shape[1]
+    context_rows = context.shape[0] // 8
+    masked = asks.shape[0] // 8
+    half = masked // 2
 
     def place(source, piece):
         weights[pl.ds(pl.multiple_of(source * part, part), part)] = piece
@@ -369,23 +421,43 @@
     def place_context(source, piece):
         context[pl.ds(pl.multiple_of(source * context_rows, context_rows), context_rows)] = piece
 
-    for flip, piece in enumerate((own_pack, peer_pack)):
-        place(own ^ flip, piece[:, 0:wide])
-        place_context(own ^ flip, piece[0:context_rows, wide:])
-    for number, piece in enumerate((first, second, third)):
-        relation = (1 + parity, 2 - parity, 3)[number] * 2
-        place(own ^ relation, piece[...])
-        place(own ^ (relation + 1), peer_weights[number * part : (number + 1) * part])
-    for number, asked in enumerate((ask1, ask2, ask3)):
-        relation = (number + 1) * 2
-        place_context(own ^ relation, asked[rows:])
+    pair = 2 * part
+    chip = own - core
+    along, across = jnp.where(core == 0, 2, 4), jnp.where(core == 0, 4, 2)
+    for source, piece in (
+        (chip, held.at[0:pair]),
+        (chip ^ along, first.at[0:pair]),
+        (chip ^ across, peers.at[0:pair, 0:wide]),
+    ):
+        weights[pl.ds(pl.multiple_of(source * part, part), pair)] = piece[...]
+    place(own ^ 6, third[...])
+    last = pl.ds(pl.multiple_of((own ^ 7) * part, part), part)
+    weights[last, 0 : peer_left.shape[1]] = peer_left[...]
+    weights[last, peer_left.shape[1] :] = peer_right[...]
+    for flip, piece in ((0, w_own), (1, w_core), (4, w_cam)):
+        source = own ^ flip
+        for number in range(2):
+            start = pl.multiple_of(source * masked + number * half, half)
+            asks[pl.ds(start, half)] = piece[part_rows : part_rows + half, number * width : (number + 1) * width]
         place_context(
-            own ^ (relation + 1),
-            peer_contexts[number * context_rows : (number + 1) * context_rows],
+            source, piece[part_rows : part_rows + context_rows, 2 * width : 3 * width]
         )
-    for relation, asked in enumerate((ask0, ask1, ask2, ask3)):
-        source = (own // 2) ^ relation
-        queries[pl.ds(pl.multiple_of(source * rows, rows), rows)] = asked[0:rows]
+    base = near.shape[0] - masked - context_rows
+    at = wide + 3 * width
+    pieces = [(2, near.at[base : base + masked], near.at[base + masked :])]
+    pieces.append((6, far.at[0:masked], far.at[masked:]))
+    for number, flip in enumerate((3, 7, 5)):
+        rows = peers.at[:, wide + number * width : wide + (number + 1) * width]
+        pieces.append((flip, rows, peers.at[number * context_rows : (number + 1) * context_rows, at:]))
+    for flip, rows, last in pieces:
+        source = own ^ flip
+        asks[pl.ds(pl.multiple_of(source * masked, masked), masked)] = rows[...]
+        place_context(source, last[...])
+    for chip in range(4):
+        picker = slot_picker(slot_keys[chip : chip + 1, :], own, capacity, 8 * capacity)
+        queries[chip * 2 * capacity : (chip + 1) * 2 * capacity] = dot(
+            picker, asks[chip * 2 * masked : (chip + 1) * 2 * masked]
+        ).astype(jnp.bfloat16)
     head_size = width // P_HEADS
     scale = math.log2(math.e) / math.sqrt(head_size)
     asked = dot(queries[...], weights[:, 0:width]).astype(jnp.bfloat16)
@@ -434,12 +506,12 @@
         out[at] = jnp.where(filled, predicted[at] - goal, 0.0).astype(jnp.bfloat16)
 
 
-def call(kernel, outs, scratch, *args, far=0, after=0, light=False):
+def call(kernel, outs, scratch, *args, far=0, copies=0, after=0):
     shapes = tuple(jax.ShapeDtypeStruct(shape, dtype) for shape, dtype in outs)
     near = pl.BlockSpec(memory_space=pltpu.VMEM)
     scratch_shapes = [pltpu.VMEM(shape, dtype) for shape, dtype in scratch]
     if far:
-        scratch_shapes.append(pltpu.SemaphoreType.DMA((far,)))
+        scratch_shapes.append(pltpu.SemaphoreType.DMA((copies,)))
         args = [pltpu.with_memory_space_constraint(arg, pltpu.HBM) for arg in args[:far]] + list(args[far:])
     return pl.pallas_call(
         kernel,
@@ -450,7 +522,6 @@
         out_specs=tuple(near for _ in outs),
         scratch_shapes=scratch_shapes,
         compiler_params=pltpu.CompilerParams(vmem_limit_bytes=40 * 2**20),
-        cost_estimate=pl.CostEstimate(flops=1, bytes_accessed=1, transcendentals=0) if light else None,
     )(*args)
 
 
@@ -458,17 +529,9 @@
     return lax.ppermute(rows, ("cam", "slab"), [(source, source ^ flip) for source in range(8)])
 
 
-def send_alternating(rows, clips, even, odd):
-    pairs = [
-        (clip * 8 + source, clip * 8 + (source ^ (odd if clip % 2 else even)))
-        for clip in range(clips)
-        for source in range(8)
-    ]
-    return lax.ppermute(rows, ("clip", "cam", "slab"), pairs)
-
-
-def swap_clips(rows, clips):
-    return lax.ppermute(rows, "clip", [(clip, clip ^ 1) for clip in range(clips)])
+def send_by_core(rows, even, odd):
+    pairs = [(source, source ^ (odd if source % 2 else even)) for source in range(8)]
+    return lax.ppermute(rows, ("cam", "slab"), pairs)
 
 
 def paired_shards(
@@ -487,75 +550,78 @@
     block = ((block_rows, padded), bf16)
     weight_rows = w_query.shape[0]
     weight_width = 4 * pred_width + w_proj.shape[1]
-    pack_width = weight_width + pred_width
-    peer_query = send(pred_query[0], 1)
-    w_core = send(w_out_teacher, 1)
-    w_cam = send(w_out_teacher, 4)
-    block0, block1, block2, block3, resid_rows, slot_keys, pack = call(
+    asked_rows = masked + context_rows
+    message_rows = quarter + masked // 2 + masked + tokens - weight_width // -width * weight_rows
+    shard = ((weight_rows, weight_width), bf16)
+    block0, block2, block3, resid_rows, slot_keys, pack, message, w_here = call(
         functools.partial(pack_kernel, capacity),
-        [block] * 4
-        + [((masked, width), bf16), ((2, 2 * masked), jnp.int32), ((weight_rows, pack_width), bf16)],
+        [
+            block, ((block_rows + asked_rows, padded), bf16), block,
+            ((masked, width), bf16), ((4, 2 * masked), jnp.int32), shard,
+            ((message_rows, width), bf16),
+            ((quarter + masked // 2, width), bf16),
+        ],
         [
             ((block_rows, width), bf16), ((4, block_rows, padded), bf16), ((tokens, width), bf16),
             ((tokens, width), bf16), (mask_list.shape, jnp.int32), (owners.shape, jnp.int32),
         ],
         t_query[0], t_key[0], t_value[0], t_resid[0], mask_list, owners,
-        w_query, w_key, w_value, w_out, w_proj, pred_context[0], far=12,
-    )
-    other2, other3, other1 = send(block2, 2), send(block3, 3), send(block1, 1)
-    w_both = send(w_cam, 1)
-    peer_resid = send(resid_rows, 1)
-    ask = ((2 * capacity + context_rows, pred_width), bf16)
-    ask0, ask1, ask2, ask3 = call(
-        functools.partial(ask_kernel, capacity),
-        [((2 * capacity, pred_width), bf16), ask, ask, ask],
-        [((2 * masked, pred_width), bf16)],
-        slot_keys, pred_query[0], peer_query, pred_context[0],
-    )
-    asked1, asked2, asked3 = send(ask1, 2), send(ask2, 4), send(ask3, 6)
-    peer_pack = send(pack, 1)
-    clips = lax.axis_size("clip")
-    shard = ((weight_rows, weight_width), bf16)
-    (held,) = call(hold_kernel, [shard], [], pack, other2, after=1, light=True)
-    first = send_alternating(held, clips, 2, 4)
-    third = send_alternating(first, clips, 4, 2)
-    second = swap_clips(first, clips)
+        w_query, w_key, w_value, w_out, w_proj, pred_query[0], pred_context[0], w_out_teacher,
+        far=14, copies=17,
+    )
+    other2, other3, w_cam = send(block2, 2), send(block3, 3), send(w_here, 4)
+    peer_message = send(message, 1)
+    held, passed = call(
+        functools.partial(hold_kernel, quarter + masked // 2 + masked),
+        [((2 * weight_rows, weight_width), bf16), ((asked_rows, pred_width), bf16)],
+        [],
+        pack, other2, peer_message,
+    )
+    first = send_by_core(held, 2, 4)
+    far = send(passed, 4)
     slots = ((16 * capacity, padded), bf16)
-    own_slots, away_slots = call(
+    own_slots, away_slots, w_pass = call(
         functools.partial(teacher_kernel, capacity, head_size, tokens, masked),
-        [slots, slots],
+        [slots, slots, (w_out_teacher.shape, bf16)],
         [
             ((4 * masked, padded), bf16), ((4 * tokens, padded), bf16), ((4 * tokens, padded), bf16),
             ((4 * masked, padded), bf16),
         ],
-        slot_keys, block0, other1, other2, other3,
-    )
-    peer_slots = send(away_slots, 1)
+        slot_keys, block0, peer_message, other2, other3, w_cam,
+    )
+    peer_slots, w_both = send(away_slots, 1), send(w_pass, 1)
     part = ((4 * capacity, width), bf16)
     part0, part1, part2, part3 = call(
         functools.partial(project_kernel, capacity),
         [part] * 4,
         [((2 * padded, width), bf16), ((2 * masked, width), bf16), ((4 * capacity, width), f32)],
-        slot_keys, own_slots, peer_slots, w_out_teacher, w_cam, w_core, w_both, resid_rows, peer_resid,
+        slot_keys, own_slots, peer_slots, w_here, w_cam, peer_message, w_both, resid_rows,
     )
     far1, far2, far3 = send(part1, 2), send(part2, 4), send(part3, 6)
-    bundle, contexts = call(
+    bundle, forward = call(
         bundle_kernel,
-        [((3 * weight_rows, weight_width), bf16), ((3 * context_rows, pred_width), bf16)],
+        [((2 * weight_rows, weight_width + 4 * pred_width), bf16), shard],
         [],
-        first, second, third, asked1, asked2, asked3, part0,
-        after=1, light=True,
+        first, other2, far, w_cam, part0,
+        after=1,
+    )
+    peers, third = send(bundle, 1), send_by_core(forward, 4, 2)
+    left, right = call(
+        split_kernel,
+        [((weight_rows, 4 * pred_width), bf16), ((weight_rows, width), bf16)],
+        [],
+        third, peers,
+        after=1,
     )
     (predicted,) = call(
-        predict_kernel,
+        functools.partial(predict_kernel, capacity, quarter),
         [((8 * capacity, width), f32)],
         [
             ((8 * capacity, pred_width), bf16), ((8 * weight_rows, weight_width), bf16),
-            ((8 * context_rows, pred_width), bf16),
+            ((8 * context_rows, pred_width), bf16), ((8 * masked, pred_width), bf16),
         ],
-        ask0, asked1, asked2, asked3, pack, first, second, third, peer_pack, send(bundle, 1),
-        send(contexts, 1),
-        light=True,
+        slot_keys, w_here, peer_message, w_cam, other2, far,
+        held, first, third, send(left, 1), send(right, 1), peers,
     )
     (errors,) = call(
         functools.partial(finish_kernel, capacity, masked),

time: 52.9 us -> 49.8 us (0.941)
  starting transfers between devices: 16.5 us -> 13.1 us
    ppermute x18 -> x13, starting transfers between devices: 14.7 us -> 10.7 us  [send(): lax.ppermute(rows, ('cam', 'slab'), [(source, source ^ flip) for source i...]
    ppermute x3 -> x2, waiting for transfers between devices: 1.42 us -> 4.42 us  [send_by_core(): return lax.ppermute(rows, ('cam', 'slab'), pairs)]
    ppermute x18 -> x13, waiting for transfers between devices: 23.4 us -> 20.6 us  [send(): lax.ppermute(rows, ('cam', 'slab'), [(source, source ^ flip) for source i...]
    ppermute x3 -> x2, starting transfers between devices: 1.86 us -> 2.42 us  [send_by_core(): return lax.ppermute(rows, ('cam', 'slab'), pairs)]
  transfers between devices with their start and end apart: 21 -> 15, of which waited for: 7 -> 7; matrix products, arithmetic and copies ran while one was open for 0% -> 0% of each run, Pallas kernels for 19% -> 15%
where the time goes in v4:
time: 49.8 us; the launch traced here: 49.7 us
  waiting for transfers between devices  25.1 us (50%)
  starting transfers between devices  13.1 us (26%)
  Pallas kernels  11.4 us (23%)
    ppermute x13, waiting for transfers between devices, send(): lax.ppermute(rows, ('cam', 'slab'), [(source, source ^ flip) for source i...  20.6 us
    pallas_call x8, Pallas kernels, call(): pl.pallas_call(kernel, out_shape=shapes, in_specs=[pl.BlockSpec(memory_sp...  11.4 us
    ppermute x13, starting transfers between devices, send(): lax.ppermute(rows, ('cam', 'slab'), [(source, source ^ flip) for source i...  10.7 us
    ppermute x2, waiting for transfers between devices, send_by_core(): return lax.ppermute(rows, ('cam', 'slab'), pairs)  4.42 us
    ppermute x2, starting transfers between devices, send_by_core(): return lax.ppermute(rows, ('cam', 'slab'), pairs)  2.42 us
  transfers between devices with their start and end apart: 15, of which 7 were waited for; matrix products, arithmetic and copies ran while one was open for 0% of the time, Pallas kernels for 15%

profile of v4, /device:TPU:0, one launch (start us, length us, event | category | flops | bytes accessed | tf_op | source)
XLA Modules:
  0.0 49.7 jit_solution(18142503709023821369)
XLA Ops:
  0.0 2.5 %shard_map.136 = (bf16[352,384]{1,0:T(8,128)(2,1)S(1)}, bf16[480,384]{1,0:T(8,128)(2,1)S(1)}, bf16[352,384]{1,0:T(8,128)(2,1)S(1)}, bf16[96,1408]{1,0:T(8,128)(2...) custom-call(bf16[128,1408]{1,0:T(8,128)(2,1)} %bitcast.7, ...), custom_call_target="tpu_custom_call" | custom-call | tf_op jit(solution)/shard_map/pallas_call | solution.py:516
  2.5 0.5 %collective-permute-start = (bf16[592,1408]{1,0:T(8,128)(2,1)S(1)}, bf16[592,1408]{1,0:T(8,128)(2,1)S(1)}, u32[]{:S(2)}, u32[]{:S(2)}) collective-permute-start(bf16[592,1408]{1,0:T(8,128)(2,1)S(1)} %get-tuple-element.28), channel_id=1, source_target_pairs={{0,1},{1,0},{2,3},{3,2},{4,5},{5,4},{6,7},{7,6},{8,9},{9,8},{10,11... | collective-permute-start | bytes 5001224 | tf_op jit(solution)/shard_map/ppermute | solution.py:529
  3.0 2.6 %collective-permute-start.1 = (bf16[224,1408]{1,0:T(8,128)(2,1)S(1)}, bf16[224,1408]{1,0:T(8,128)(2,1)S(1)}, u32[]{:S(2)}, u32[]{:S(2)}) collective-permute-start(bf16[224,1408]{1,0:T(8,128)(2,1)S(1)} %get-tuple-element.27.w_own), channel_id=1, source_target_pairs={{0,4},{1,5},{2,6},{3,7},{4,0},{5,1},{6,2},{7,3},{8,12},{9,13},{10,... | collective-permute-start | bytes 1892360 | tf_op jit(solution)/shard_map/ppermute | solution.py:529
  5.6 1.5 %collective-permute-start.2 = (bf16[480,384]{1,0:T(8,128)(2,1)S(1)}, bf16[480,384]{1,0:T(8,128)(2,1)S(1)}, u32[]{:S(2)}, u32[]{:S(2)}) collective-permute-start(bf16[480,384]{1,0:T(8,128)(2,1)S(1)} %get-tuple-element.29), channel_id=1, source_target_pairs={{0,2},{1,3},{2,0},{3,1},{4,6},{5,7},{6,4},{7,5},{8,10},{9,11},{10,... | collective-permute-start | bytes 1105928 | tf_op jit(solution)/shard_map/ppermute | solution.py:529
  7.1 0.0 collective-permute-start.5
  7.1 9.9 %collective-permute-done.2.block.block2.near = bf16[480,384]{1,0:T(8,128)(2,1)S(1)} collective-permute-done((bf16[480,384]{1,0:T(8,128)(2,1)S(1)}, bf16[480,384]{1,0:T(8,128)(2,1)S(1)}, u32[]{:S(2)}, u32[]{:S(2)}) %collective-permute-start.2) | collective-permute-done | bytes 368672 | tf_op jit(solution)/shard_map/ppermute | solution.py:529
  17.0 0.0 collective-permute-done.message.w_core
  17.0 0.1 shard_map.137
  17.1 1.6 %collective-permute-start.4 = (bf16[96,2944]{1,0:T(8,128)(2,1)S(1)}, bf16[96,2944]{1,0:T(8,128)(2,1)S(1)}, u32[]{:S(2)}, u32[]{:S(2)}) collective-permute-start(bf16[96,2944]{1,0:T(8,128)(2,1)S(1)} %get-tuple-element.32.held), channel_id=1, source_target_pairs={{0,2},{1,5},{2,0},{3,7},{4,6},{5,1},{6,4},{7,3},{8,10},{9,13},{10,... | collective-permute-start | bytes 1695752 | tf_op jit(solution)/shard_map/ppermute | solution.py:534
  18.6 2.6 %collective-permute-done.5.block3 = bf16[352,384]{1,0:T(8,128)(2,1)S(1)} collective-permute-done((bf16[352,384]{1,0:T(8,128)(2,1)S(1)}, bf16[352,384]{1,0:T(8,128)(2,1)S(1)}, u32[]{:S(2)}, u32[]{:S(2)}) %collective-permute-start.5) | collective-permute-done | bytes 270368 | tf_op jit(solution)/shard_map/ppermute | solution.py:529
  21.3 0.0 collective-permute-done.1.w_cam.beside
  21.3 2.8 %shard_map.138 = (bf16[384,384]{1,0:T(8,128)(2,1)S(1)}, bf16[384,384]{1,0:T(8,128)(2,1)S(1)}, bf16[176,1408]{1,0:T(8,128)(2,1)S(1)}) custom-call(s32[4,192]{1,0:T(4,128)S(1)} %get-tuple-element.26.slot_keys, bf16[352,384]{1,0:T(8,128)(2,1)S(1)} %get-tuple-element.33.block0, bf16[592,1408]{1,0:T(8,128)(2,1)S(1)} %collective-permute-done.message.w_core, ...), custom_call_target="tpu_custom_call" | custom-call | tf_op jit(solution)/shard_map/pallas_call | solution.py:516
  24.1 0.7 %collective-permute-start.7 = (bf16[176,1408]{1,0:T(8,128)(2,1)S(1)}, bf16[176,1408]{1,0:T(8,128)(2,1)S(1)}, u32[]{:S(2)}, u32[]{:S(2)}) collective-permute-start(bf16[176,1408]{1,0:T(8,128)(2,1)S(1)} %get-tuple-element.37), channel_id=1, source_target_pairs={{0,1},{1,0},{2,3},{3,2},{4,5},{5,4},{6,7},{7,6},{8,9},{9,8},{10,11... | collective-permute-start | bytes 1486856 | tf_op jit(solution)/shard_map/ppermute | solution.py:529
  24.7 0.1 collective-permute-start.6
  24.8 1.2 %collective-permute-start.3 = (bf16[128,384]{1,0:T(8,128)(2,1)S(1)}, bf16[128,384]{1,0:T(8,128)(2,1)S(1)}, u32[]{:S(2)}, u32[]{:S(2)}) collective-permute-start(bf16[128,384]{1,0:T(8,128)(2,1)S(1)} %get-tuple-element.31), channel_id=1, source_target_pairs={{0,4},{1,5},{2,6},{3,7},{4,0},{5,1},{6,2},{7,3},{8,12},{9,13},{10,... | collective-permute-start | bytes 294920 | tf_op jit(solution)/shard_map/ppermute | solution.py:529
  26.0 0.7 %collective-permute-done.6.peer_slots = bf16[384,384]{1,0:T(8,128)(2,1)S(1)} collective-permute-done((bf16[384,384]{1,0:T(8,128)(2,1)S(1)}, bf16[384,384]{1,0:T(8,128)(2,1)S(1)}, u32[]{:S(2)}, u32[]{:S(2)}) %collective-permute-start.6) | collective-permute-done | bytes 294944 | tf_op jit(solution)/shard_map/ppermute | solution.py:529
  26.6 2.3 %shard_map.139 = (bf16[96,1408]{1,0:T(8,128)(2,1)S(1)}, bf16[96,1408]{1,0:T(8,128)(2,1)S(1)}, bf16[96,1408]{1,0:T(8,128)(2,1)S(1)}, bf16[96,1408]{1,0:T(8,128)(2,1)S(1)}) custom-call(s32[4,192]{1,0:T(4,128)S(1)} %get-tuple-element.26.slot_keys, bf16[384,384]{1,0:T(8,128)(2,1)S(1)} %get-tuple-element.35.own_slots, ...), custom_call_target="tpu_custom_call" | custom-call | tf_op jit(solution)/shard_map/pallas_call | solution.py:516
  29.0 1.0 %collective-permute-done.3.far = bf16[128,384]{1,0:T(8,128)(2,1)S(1)} collective-permute-done((bf16[128,384]{1,0:T(8,128)(2,1)S(1)}, bf16[128,384]{1,0:T(8,128)(2,1)S(1)}, u32[]{:S(2)}, u32[]{:S(2)}) %collective-permute-start.3) | collective-permute-done | bytes 98336 | tf_op jit(solution)/shard_map/ppermute | solution.py:529
  29.9 0.1 shard_map.140
  30.0 0.1 collective-permute-start.9
  30.1 0.9 %collective-permute-start.8 = (bf16[48,2944]{1,0:T(8,128)(2,1)S(1)}, bf16[48,2944]{1,0:T(8,128)(2,1)S(1)}, u32[]{:S(2)}, u32[]{:S(2)}) collective-permute-start(bf16[48,2944]{1,0:T(8,128)(2,1)S(1)} %get-tuple-element.40), channel_id=1, source_target_pairs={{0,4},{1,3},{2,6},{3,1},{4,0},{5,7},{6,2},{7,5},{8,12},{9,11},{10,... | collective-permute-start | bytes 847880 | tf_op jit(solution)/shard_map/ppermute | solution.py:534
  31.0 1.5 %collective-permute-start.12 = (bf16[96,1408]{1,0:T(8,128)(2,1)S(1)}, bf16[96,1408]{1,0:T(8,128)(2,1)S(1)}, u32[]{:S(2)}, u32[]{:S(2)}) collective-permute-start(bf16[96,1408]{1,0:T(8,128)(2,1)S(1)} %get-tuple-element.44), channel_id=1, source_target_pairs={{0,2},{1,3},{2,0},{3,1},{4,6},{5,7},{6,4},{7,5},{8,10},{9,11},{10,... | collective-permute-start | bytes 811016 | tf_op jit(solution)/shard_map/ppermute | solution.py:529
  32.5 1.2 %collective-permute-start.13 = (bf16[96,1408]{1,0:T(8,128)(2,1)S(1)}, bf16[96,1408]{1,0:T(8,128)(2,1)S(1)}, u32[]{:S(2)}, u32[]{:S(2)}) collective-permute-start(bf16[96,1408]{1,0:T(8,128)(2,1)S(1)} %get-tuple-element.45), channel_id=1, source_target_pairs={{0,4},{1,5},{2,6},{3,7},{4,0},{5,1},{6,2},{7,3},{8,12},{9,13},{10,... | collective-permute-start | bytes 811016 | tf_op jit(solution)/shard_map/ppermute | solution.py:529
  33.7 0.8 %collective-permute-start.14 = (bf16[96,1408]{1,0:T(8,128)(2,1)S(1)}, bf16[96,1408]{1,0:T(8,128)(2,1)S(1)}, u32[]{:S(2)}, u32[]{:S(2)}) collective-permute-start(bf16[96,1408]{1,0:T(8,128)(2,1)S(1)} %get-tuple-element.46), channel_id=1, source_target_pairs={{0,6},{1,7},{2,4},{3,5},{4,2},{5,3},{6,0},{7,1},{8,14},{9,15},{10,... | collective-permute-start | bytes 811016 | tf_op jit(solution)/shard_map/ppermute | solution.py:529
  34.5 4.4 %collective-permute-done.8.piece.third = bf16[48,2944]{1,0:T(8,128)(2,1)S(1)} collective-permute-done((bf16[48,2944]{1,0:T(8,128)(2,1)S(1)}, bf16[48,2944]{1,0:T(8,128)(2,1)S(1)}, u32[]{:S(2)}, u32[]{:S(2)}) %collective-permute-start.8) | collective-permute-done | bytes 282656 | tf_op jit(solution)/shard_map/ppermute | solution.py:534
  38.9 0.1 collective-permute-start.10
  39.0 0.0 copy-start
  39.0 0.5 collective-permute-start.11
  39.5 1.1 %collective-permute-done.11.peer_right = bf16[48,1408]{1,0:T(8,128)(2,1)S(1)} collective-permute-done((bf16[48,1408]{1,0:T(8,128)(2,1)S(1)}, bf16[48,1408]{1,0:T(8,128)(2,1)S(1)}, u32[]{:S(2)}, u32[]{:S(2)}) %collective-permute-start.11) | collective-permute-done | bytes 135200 | tf_op jit(solution)/shard_map/ppermute | solution.py:529
  40.5 2.4 %shard_map.142.predicted = f32[192,1408]{1,0:T(8,128)S(1)} custom-call(s32[4,192]{1,0:T(4,128)S(1)} %get-tuple-element.26.slot_keys, bf16[224,1408]{1,0:T(8,128)(2,1)S(1)} %get-tuple-element.27.w_own, bf16[592,1408]{1,0:T(8,128)(2,1)S(1)} %collective-permute-done.message.w_core, bf16[224,1408]{1,0:T(8,128)(2,1)S(1)} %collective-permute-done.1.w_cam.beside, ...), custom_call_target="tpu_custom_call" | custom-call | tf_op jit(solution)/shard_map/pallas_call | solution.py:516
  43.0 5.4 %collective-permute-done.13.part2 = bf16[96,1408]{1,0:T(8,128)(2,1)S(1)} collective-permute-done((bf16[96,1408]{1,0:T(8,128)(2,1)S(1)}, bf16[96,1408]{1,0:T(8,128)(2,1)S(1)}, u32[]{:S(2)}, u32[]{:S(2)}) %collective-permute-start.13) | collective-permute-done | bytes 270368 | tf_op jit(solution)/shard_map/ppermute | solution.py:529
  48.4 1.3 %shard_map.143 = bf16[192,1408]{1,0:T(8,128)(2,1)} custom-call(s32[2,384]{1,0:T(2,128)S(1)} %copy-done, f32[192,1408]{1,0:T(8,128)S(1)} %shard_map.142.predicted, bf16[96,1408]{1,0:T(8,128)(2,1)S(1)} %get-tuple-element.39.after.part0, bf16[96,1408]{1,0:T(8,128)(2,1)S(1)} %collective-permute-done.12.part1, ...), custom_call_target="tpu_custom_call" | custom-call | tf_op jit(solution)/shard_map/pallas_call | solution.py:516
  (8 shorter events, 0.0 us)
Async XLA Ops:
  2.5 14.5 %collective-permute-start = (bf16[592,1408]{1,0:T(8,128)(2,1)S(1)}, bf16[592,1408]{1,0:T(8,128)(2,1)S(1)}, u32[]{:S(2)}, u32[]{:S(2)}) collective-permute-start(bf16[592,1408]{1,0:T(8,128)(2,1)S(1)} %get-tuple-element.28), channel_id=1, source_target_pairs={{0,1},{1,0},{2,3},{3,2},{4,5},{5,4},{6,7},{7,6},{8,9},{9,8},{10,11... | collective-permute-start | bytes 5001224 | tf_op jit(solution)/shard_map/ppermute | solution.py:529
  3.0 18.3 %collective-permute-start.1 = (bf16[224,1408]{1,0:T(8,128)(2,1)S(1)}, bf16[224,1408]{1,0:T(8,128)(2,1)S(1)}, u32[]{:S(2)}, u32[]{:S(2)}) collective-permute-start(bf16[224,1408]{1,0:T(8,128)(2,1)S(1)} %get-tuple-element.27.w_own), channel_id=1, source_target_pairs={{0,4},{1,5},{2,6},{3,7},{4,0},{5,1},{6,2},{7,3},{8,12},{9,13},{10,... | collective-permute-start | bytes 1892360 | tf_op jit(solution)/shard_map/ppermute | solution.py:529
  5.6 11.4 %collective-permute-start.2 = (bf16[480,384]{1,0:T(8,128)(2,1)S(1)}, bf16[480,384]{1,0:T(8,128)(2,1)S(1)}, u32[]{:S(2)}, u32[]{:S(2)}) collective-permute-start(bf16[480,384]{1,0:T(8,128)(2,1)S(1)} %get-tuple-element.29), channel_id=1, source_target_pairs={{0,2},{1,3},{2,0},{3,1},{4,6},{5,7},{6,4},{7,5},{8,10},{9,11},{10,... | collective-permute-start | bytes 1105928 | tf_op jit(solution)/shard_map/ppermute | solution.py:529
  7.1 14.2 %collective-permute-start.5 = (bf16[352,384]{1,0:T(8,128)(2,1)S(1)}, bf16[352,384]{1,0:T(8,128)(2,1)S(1)}, u32[]{:S(2)}, u32[]{:S(2)}) collective-permute-start(bf16[352,384]{1,0:T(8,128)(2,1)S(1)} %get-tuple-element.34), channel_id=1, source_target_pairs={{0,3},{1,2},{2,1},{3,0},{4,7},{5,6},{6,5},{7,4},{8,11},{9,10},{10,... | collective-permute-start | bytes 811016 | tf_op jit(solution)/shard_map/ppermute | solution.py:529
  17.1 12.9 %collective-permute-start.4 = (bf16[96,2944]{1,0:T(8,128)(2,1)S(1)}, bf16[96,2944]{1,0:T(8,128)(2,1)S(1)}, u32[]{:S(2)}, u32[]{:S(2)}) collective-permute-start(bf16[96,2944]{1,0:T(8,128)(2,1)S(1)} %get-tuple-element.32.held), channel_id=1, source_target_pairs={{0,2},{1,5},{2,0},{3,7},{4,6},{5,1},{6,4},{7,3},{8,10},{9,13},{10,... | collective-permute-start | bytes 1695752 | tf_op jit(solution)/shard_map/ppermute | solution.py:534
  24.1 2.6 %collective-permute-start.7 = (bf16[176,1408]{1,0:T(8,128)(2,1)S(1)}, bf16[176,1408]{1,0:T(8,128)(2,1)S(1)}, u32[]{:S(2)}, u32[]{:S(2)}) collective-permute-start(bf16[176,1408]{1,0:T(8,128)(2,1)S(1)} %get-tuple-element.37), channel_id=1, source_target_pairs={{0,1},{1,0},{2,3},{3,2},{4,5},{5,4},{6,7},{7,6},{8,9},{9,8},{10,11... | collective-permute-start | bytes 1486856 | tf_op jit(solution)/shard_map/ppermute | solution.py:529
  24.7 1.9 %collective-permute-start.6 = (bf16[384,384]{1,0:T(8,128)(2,1)S(1)}, bf16[384,384]{1,0:T(8,128)(2,1)S(1)}, u32[]{:S(2)}, u32[]{:S(2)}) collective-permute-start(bf16[384,384]{1,0:T(8,128)(2,1)S(1)} %get-tuple-element.36), channel_id=1, source_target_pairs={{0,1},{1,0},{2,3},{3,2},{4,5},{5,4},{6,7},{7,6},{8,9},{9,8},{10,11... | collective-permute-start | bytes 884744 | tf_op jit(solution)/shard_map/ppermute | solution.py:529
  24.8 5.1 %collective-permute-start.3 = (bf16[128,384]{1,0:T(8,128)(2,1)S(1)}, bf16[128,384]{1,0:T(8,128)(2,1)S(1)}, u32[]{:S(2)}, u32[]{:S(2)}) collective-permute-start(bf16[128,384]{1,0:T(8,128)(2,1)S(1)} %get-tuple-element.31), channel_id=1, source_target_pairs={{0,4},{1,5},{2,6},{3,7},{4,0},{5,1},{6,2},{7,3},{8,12},{9,13},{10,... | collective-permute-start | bytes 294920 | tf_op jit(solution)/shard_map/ppermute | solution.py:529
  30.0 8.8 %collective-permute-start.9 = (bf16[96,4480]{1,0:T(8,128)(2,1)S(1)}, bf16[96,4480]{1,0:T(8,128)(2,1)S(1)}, u32[]{:S(2)}, u32[]{:S(2)}) collective-permute-start(bf16[96,4480]{1,0:T(8,128)(2,1)S(1)} %get-tuple-element.41), channel_id=1, source_target_pairs={{0,1},{1,0},{2,3},{3,2},{4,5},{5,4},{6,7},{7,6},{8,9},{9,8},{10,11... | collective-permute-start | bytes 2580488 | tf_op jit(solution)/shard_map/ppermute | solution.py:529
  30.1 8.8 %collective-permute-start.8 = (bf16[48,2944]{1,0:T(8,128)(2,1)S(1)}, bf16[48,2944]{1,0:T(8,128)(2,1)S(1)}, u32[]{:S(2)}, u32[]{:S(2)}) collective-permute-start(bf16[48,2944]{1,0:T(8,128)(2,1)S(1)} %get-tuple-element.40), channel_id=1, source_target_pairs={{0,4},{1,3},{2,6},{3,1},{4,0},{5,7},{6,2},{7,5},{8,12},{9,11},{10,... | collective-permute-start | bytes 847880 | tf_op jit(solution)/shard_map/ppermute | solution.py:534
  31.0 12.0 %collective-permute-start.12 = (bf16[96,1408]{1,0:T(8,128)(2,1)S(1)}, bf16[96,1408]{1,0:T(8,128)(2,1)S(1)}, u32[]{:S(2)}, u32[]{:S(2)}) collective-permute-start(bf16[96,1408]{1,0:T(8,128)(2,1)S(1)} %get-tuple-element.44), channel_id=1, source_target_pairs={{0,2},{1,3},{2,0},{3,1},{4,6},{5,7},{6,4},{7,5},{8,10},{9,11},{10,... | collective-permute-start | bytes 811016 | tf_op jit(solution)/shard_map/ppermute | solution.py:529
  32.5 15.9 %collective-permute-start.13 = (bf16[96,1408]{1,0:T(8,128)(2,1)S(1)}, bf16[96,1408]{1,0:T(8,128)(2,1)S(1)}, u32[]{:S(2)}, u32[]{:S(2)}) collective-permute-start(bf16[96,1408]{1,0:T(8,128)(2,1)S(1)} %get-tuple-element.45), channel_id=1, source_target_pairs={{0,4},{1,5},{2,6},{3,7},{4,0},{5,1},{6,2},{7,3},{8,12},{9,13},{10,... | collective-permute-start | bytes 811016 | tf_op jit(solution)/shard_map/ppermute | solution.py:529
  33.7 14.7 %collective-permute-start.14 = (bf16[96,1408]{1,0:T(8,128)(2,1)S(1)}, bf16[96,1408]{1,0:T(8,128)(2,1)S(1)}, u32[]{:S(2)}, u32[]{:S(2)}) collective-permute-start(bf16[96,1408]{1,0:T(8,128)(2,1)S(1)} %get-tuple-element.46), channel_id=1, source_target_pairs={{0,6},{1,7},{2,4},{3,5},{4,2},{5,3},{6,0},{7,1},{8,14},{9,15},{10,... | collective-permute-start | bytes 811016 | tf_op jit(solution)/shard_map/ppermute | solution.py:529
  38.9 1.6 %collective-permute-start.10 = (bf16[48,1536]{1,0:T(8,128)(2,1)S(1)}, bf16[48,1536]{1,0:T(8,128)(2,1)S(1)}, u32[]{:S(2)}, u32[]{:S(2)}) collective-permute-start(bf16[48,1536]{1,0:T(8,128)(2,1)S(1)} %get-tuple-element.42), channel_id=1, source_target_pairs={{0,1},{1,0},{2,3},{3,2},{4,5},{5,4},{6,7},{7,6},{8,9},{9,8},{10,11... | collective-permute-start | bytes 442376 | tf_op jit(solution)/shard_map/ppermute | solution.py:529
  39.0 9.4 %copy-start = (s32[2,384]{1,0:T(2,128)S(1)}, s32[2,384]{1,0:T(2,128)}, u32[]{:S(2)}) copy-start(s32[2,384]{1,0:T(2,128)} %owners.3) | copy-start | bytes 9220
  39.0 1.5 %collective-permute-start.11 = (bf16[48,1408]{1,0:T(8,128)(2,1)S(1)}, bf16[48,1408]{1,0:T(8,128)(2,1)S(1)}, u32[]{:S(2)}, u32[]{:S(2)}) collective-permute-start(bf16[48,1408]{1,0:T(8,128)(2,1)S(1)} %get-tuple-element.43), channel_id=1, source_target_pairs={{0,1},{1,0},{2,3},{3,2},{4,5},{5,4},{6,7},{7,6},{8,9},{9,8},{10,11... | collective-permute-start | bytes 405512 | tf_op jit(solution)/shard_map/ppermute | solution.py:529

commit v5 on v4

--- a/solution.py
+++ b/solution.py
@@ -201,71 +201,43 @@
     quarter = width // 8
     context_rows = context.shape[0]
     row_total = stack.shape[0]
-    part_rows, half = w_far.shape[0], masked // 2
+    half = masked // 2
     moves = [
         (mask, mask_here),
+        (owners, owners_here),
         (query, query_here),
         (key, stack.at[0:tokens]),
         (value, stack.at[tokens : 2 * tokens]),
         (resid, resid_here),
-        (owners, owners_here),
-        (w_far, w_here.at[0:part_rows]),
-        (asks, block2.at[row_total : row_total + masked]),
-        (context, block2.at[row_total + masked :]),
-        (asks.at[0:half], w_here.at[part_rows:, 0:pred_width]),
-        (asks.at[half:], w_here.at[part_rows:, pred_width : 2 * pred_width]),
-        (
-            context,
-            w_here.at[part_rows : part_rows + context_rows, 2 * pred_width : 3 * pred_width],
-        ),
+        (w_far, w_here),
     ]
     at = 0
     for part in (wq, wk, wv, wo, wp):
         moves.append((part, pack.at[:, at : at + part.shape[1]]))
         at += part.shape[1]
+    moves.append((asks.at[0:half], pack.at[:, at : at + pred_width]))
+    moves.append((asks.at[half:], pack.at[:, at + pred_width : at + 2 * pred_width]))
+    at += 2 * pred_width
+    split, rest = pack.shape[1] - at, half - context_rows
+    moves.append((context.at[:, 0:split], pack.at[0:context_rows, at:]))
+    for number in range(context_rows // rest):
+        lanes = slice(at + number * (pred_width - split), at + (number + 1) * (pred_width - split))
+        moves.append(
+            (
+                context.at[number * rest : (number + 1) * rest, split:],
+                pack.at[context_rows:, lanes],
+            )
+        )
     copies = [
         pltpu.make_async_copy(source, target, done.at[number])
         for number, (source, target) in enumerate(moves)
     ]
     for copy in copies:
         copy.start()
-    w_here[part_rows:, 3 * pred_width :] = jnp.zeros((half, width - 3 * pred_width), jnp.bfloat16)
-    w_here[part_rows + context_rows :, 2 * pred_width : 3 * pred_width] = jnp.zeros(
-        (half - context_rows, pred_width), jnp.bfloat16
-    )
     token = lax.broadcasted_iota(jnp.int32, (tokens, masked), 0)
-    for copy in copies[:4]:
-        copy.wait()
+    copies[0].wait()
     chosen = jnp.where(token == mask_here[...], 1.0, 0.0).T.astype(jnp.bfloat16)
-    stack[2 * tokens :] = dot(chosen, query_here[...]).astype(jnp.bfloat16)
-    pad = blocks.shape[2] - 2 * quarter
-    for other in range(4):
-        first = stack[:, other * quarter : (other + 1) * quarter]
-        second = stack[:, (other + 4) * quarter : (other + 5) * quarter]
-        blocks[other] = jnp.concatenate(
-            [first, second, jnp.zeros((row_total, pad), jnp.bfloat16)], axis=1
-        )
-    for relation, out in ((0, block0), (2, block2), (3, block3)):
-        out[0:row_total] = blocks[slab ^ relation]
-    core_block = blocks.at[slab ^ 1]
-    for copy in copies[4:]:
-        copy.wait()
-    resid_rows[...] = dot(chosen, resid_here[...]).astype(jnp.bfloat16)
-    base = w_here.shape[0]
-    message[0:base] = w_here[...]
-    message[base : base + masked] = resid_rows[...]
-    base += masked
-    count = pack.shape[0]
-    message[base + 2 * count : base + 3 * count] = jnp.zeros((count, width), jnp.bfloat16)
-    for low in range(0, at, width):
-        high = min(low + width, at)
-        message[base : base + count, 0 : high - low] = pack[:, low:high]
-        base += count
-    message[base:] = jnp.zeros((tokens, width), jnp.bfloat16)
-    for number in range(3):
-        low, high = number * tokens, min((number + 1) * tokens, row_total)
-        lanes = slice(number * core_block.shape[1], (number + 1) * core_block.shape[1])
-        message[base : base + high - low, lanes] = core_block[low:high]
+    copies[1].wait()
     listed = owners.shape[1]
     before = lax.broadcasted_iota(jnp.int32, (listed, listed), 0)
     after = lax.broadcasted_iota(jnp.int32, (listed, listed), 1)
@@ -284,9 +256,41 @@
         keys = owner_row * capacity + rank + jnp.where(odd, 8 * capacity, 0)
         slot_keys[2 * camera : 2 * camera + 1, :] = keys[:, 0 : 2 * masked]
         slot_keys[2 * camera + 1 : 2 * camera + 2, :] = keys[:, 2 * masked :]
-
-
-def hold_kernel(base, pack, block, message, held, passed):
+    for copy in copies[2:5]:
+        copy.wait()
+    stack[2 * tokens :] = dot(chosen, query_here[...]).astype(jnp.bfloat16)
+    pad = blocks.shape[2] - 2 * quarter
+    for other in range(4):
+        first = stack[:, other * quarter : (other + 1) * quarter]
+        second = stack[:, (other + 4) * quarter : (other + 5) * quarter]
+        blocks[other] = jnp.concatenate(
+            [first, second, jnp.zeros((row_total, pad), jnp.bfloat16)], axis=1
+        )
+    for relation, out in ((0, block0), (2, block2), (3, block3)):
+        out[0:row_total] = blocks[slab ^ relation]
+    core_block = blocks.at[slab ^ 1]
+    for copy in copies[5:]:
+        copy.wait()
+    resid_rows[...] = dot(chosen, resid_here[...]).astype(jnp.bfloat16)
+    base = w_here.shape[0]
+    message[0:base] = w_here[...]
+    message[base : base + masked] = resid_rows[...]
+    base += masked
+    count = pack.shape[0]
+    total = pack.shape[1]
+    message[base + 2 * count : base + 3 * count] = jnp.zeros((count, width), jnp.bfloat16)
+    for low in range(0, total, width):
+        high = min(low + width, total)
+        message[base : base + count, 0 : high - low] = pack[:, low:high]
+        base += count
+    message[base:] = jnp.zeros((tokens, width), jnp.bfloat16)
+    for number in range(3):
+        low, high = number * tokens, min((number + 1) * tokens, row_total)
+        lanes = slice(number * core_block.shape[1], (number + 1) * core_block.shape[1])
+        message[base : base + high - low, lanes] = core_block[low:high]
+
+
+def hold_kernel(base, pack, message, after, held):
     core = lax.axis_index("slab") % 2
     rows, wide = pack.shape
     width = message.shape[1]
@@ -296,27 +300,13 @@
         high = min(low + width, wide)
         at = base + number * rows
         held[other, low:high] = message[at : at + rows, 0 : high - low]
-    passed[...] = block[block.shape[0] - passed.shape[0] :]
-
-
-def bundle_kernel(first, near, far, beside, after, out, forward):
-    rows, wide = first.shape
+
+
+def bundle_kernel(first, after, out, forward):
     core = lax.axis_index("slab") % 2
     part = forward.shape[0]
     forward[...] = first[pl.ds(pl.multiple_of(core * part, part), part)]
-    out[:, 0:wide] = first[...]
-    asked_rows, width = far.shape
-    rest = asked_rows - rows
-    at = wide + 3 * width
-    for number, piece in enumerate((near.at[near.shape[0] - asked_rows :], far)):
-        out[:, wide + number * width : wide + (number + 1) * width] = piece[0:rows]
-        out[number * rest : (number + 1) * rest, at:] = piece[rows:]
-    base = beside.shape[0] - rows // 2
-    out[0 : rows // 2, at - width : at] = beside[base:, 0:width]
-    out[rows // 2 :, at - width : at] = beside[base:, width : 2 * width]
-    out[2 * rest : 3 * rest, at:] = beside[base : base + rest, 2 * width : 3 * width]
-    if 3 * rest < rows:
-        out[3 * rest :, at:] = jnp.zeros((rows - 3 * rest, width), jnp.bfloat16)
+    out[...] = first[...]
 
 
 def split_kernel(piece, after, left, right):
@@ -325,11 +315,10 @@
 
 
 def teacher_kernel(
-    capacity, head_size, tokens, masked, slot_keys, block0, message, block2, block3, w_cam,
-    own_core, peer_core, w_pass, queries, keys, values, attended,
+    capacity, head_size, tokens, masked, slot_keys, block0, message, block2, block3,
+    own_core, peer_core, queries, keys, values, attended,
 ):
     cam, slab = position()
-    w_pass[...] = w_cam[0 : w_pass.shape[0]]
     wide, base = keys.shape[1], message.shape[0] - tokens
     pieces = [message.at[base:, number * wide : (number + 1) * wide] for number in range(3)]
     for relation, block in enumerate((block0, None, block2, block3)):
@@ -369,6 +358,10 @@
                 ).astype(jnp.bfloat16)
 
 
+def pass_kernel(rows, after, out):
+    out[...] = rows[...]
+
+
 def project_kernel(
     capacity, slot_keys, own_slots, peer_slots, w_own, w_cam, w_core, w_both, resid_own,
     out0, out1, out2, out3, weight, resid_pair, total,
@@ -402,57 +395,49 @@
 
 
 def predict_kernel(
-    capacity, part_rows, slot_keys, w_own, w_core, w_cam, near, far,
-    held, first, third, peer_left, peer_right, peers, out,
-    queries, weights, context, asks,
+    capacity, base, slot_keys, message, own_pack, first, third, peer_left, peer_right, peers, out,
+    queries, weights, context, asks, peer_pack,
 ):
     cam, slab = position()
     core = slab % 2
     own = cam * 4 + slab
-    part, wide = third.shape
-    width = far.shape[1]
+    part, total = third.shape
+    wide = weights.shape[1]
+    width = context.shape[1]
     context_rows = context.shape[0] // 8
     masked = asks.shape[0] // 8
-    half = masked // 2
 
     def place(source, piece):
-        weights[pl.ds(pl.multiple_of(source * part, part), part)] = piece
-
-    def place_context(source, piece):
-        context[pl.ds(pl.multiple_of(source * context_rows, context_rows), context_rows)] = piece
-
-    pair = 2 * part
+        weights[pl.ds(pl.multiple_of(source * part, part), part)] = piece[:, 0:wide]
+        for number in range(2):
+            start = pl.multiple_of(source * masked + number * part, part)
+            low = wide + number * width
+            asks[pl.ds(start, part)] = piece[:, low : low + width]
+        low = wide + 2 * width
+        split, rest = total - low, part - context_rows
+        start = pl.multiple_of(source * context_rows, context_rows)
+        context[pl.ds(start, context_rows), 0:split] = piece[0:context_rows, low:]
+        for number in range(context_rows // rest):
+            at = low + number * (width - split)
+            context[pl.ds(pl.multiple_of(start + number * rest, rest), rest), split:] = piece[
+                context_rows:, at : at + width - split
+            ]
+
+    place(own, own_pack)
+    for number, low in enumerate(range(0, total, message.shape[1])):
+        high = min(low + message.shape[1], total)
+        at = base + number * part
+        peer_pack[:, low:high] = message[at : at + part, 0 : high - low]
+    place(own ^ 1, peer_pack)
     chip = own - core
     along, across = jnp.where(core == 0, 2, 4), jnp.where(core == 0, 4, 2)
-    for source, piece in (
-        (chip, held.at[0:pair]),
-        (chip ^ along, first.at[0:pair]),
-        (chip ^ across, peers.at[0:pair, 0:wide]),
-    ):
-        weights[pl.ds(pl.multiple_of(source * part, part), pair)] = piece[...]
-    place(own ^ 6, third[...])
-    last = pl.ds(pl.multiple_of((own ^ 7) * part, part), part)
-    weights[last, 0 : peer_left.shape[1]] = peer_left[...]
-    weights[last, peer_left.shape[1] :] = peer_right[...]
-    for flip, piece in ((0, w_own), (1, w_core), (4, w_cam)):
-        source = own ^ flip
-        for number in range(2):
-            start = pl.multiple_of(source * masked + number * half, half)
-            asks[pl.ds(start, half)] = piece[part_rows : part_rows + half, number * width : (number + 1) * width]
-        place_context(
-            source, piece[part_rows : part_rows + context_rows, 2 * width : 3 * width]
-        )
-    base = near.shape[0] - masked - context_rows
-    at = wide + 3 * width
-    pieces = [(2, near.at[base : base + masked], near.at[base + masked :])]
-    pieces.append((6, far.at[0:masked], far.at[masked:]))
-    for number, flip in enumerate((3, 7, 5)):
-        rows = peers.at[:, wide + number * width : wide + (number + 1) * width]
-        pieces.append((flip, rows, peers.at[number * context_rows : (number + 1) * context_rows, at:]))
-    for flip, rows, last in pieces:
-        source = own ^ flip
-        asks[pl.ds(pl.multiple_of(source * masked, masked), masked)] = rows[...]
-        place_context(source, last[...])
+    for flip in range(2):
+        place((chip ^ along) + flip, first.at[flip * part : (flip + 1) * part])
+        place((chip ^ across) + flip, peers.at[flip * part : (flip + 1) * part])
+    place(own ^ 6, third)
+    peer_pack[:, 0 : peer_left.shape[1]] = peer_left[...]
+    peer_pack[:, peer_left.shape[1] :] = peer_right[...]
+    place(own ^ 7, peer_pack)
     for chip in range(4):
         picker = slot_picker(slot_keys[chip : chip + 1, :], own, capacity, 8 * capacity)
         queries[chip * 2 * capacity : (chip + 1) * 2 * capacity] = dot(
@@ -477,41 +462,62 @@
     out[...] = dot(predicted, weights[:, 4 * width :])
 
 
-def finish_kernel(capacity, masked, owners, predicted, part0, part1, part2, part3, out):
+def error_rows(capacity, masked, owner, listed, predicted, near, far):
+    rows = near.shape[0]
+    summed = near[...].astype(jnp.float32) + far[...].astype(jnp.float32)
+    shape = (rows, listed.shape[1])
+    row = lax.broadcasted_iota(jnp.int32, shape, 0)
+    lane = lax.broadcasted_iota(jnp.int32, shape, 1)
+    same = jnp.zeros(shape, jnp.bool_)
+    for group in range(4):
+        same = same | (
+            (row >= group * capacity)
+            & (row < (group + 1) * capacity)
+            & (lane >= group * masked)
+            & (lane < (group + 1) * masked)
+        )
+    count = jnp.sum(jnp.where(same & (listed == owner), 1.0, 0.0), axis=1, keepdims=True)
+    order = lax.broadcasted_iota(jnp.int32, (rows, 1), 0)
+    order = order - sum(
+        jnp.where(order >= group * capacity, capacity, 0) for group in range(1, 4)
+    )
+    filled = order.astype(jnp.float32) < count
+    goal = norm_rows(summed).astype(jnp.bfloat16).astype(jnp.float32)
+    return jnp.where(filled, predicted - goal, 0.0).astype(jnp.bfloat16)
+
+
+def own_camera_kernel(capacity, masked, owners, predicted, near, far, out):
     cam, slab = position()
-    rows = part0.shape[0]
-    for flip, (near, far) in enumerate(((part0, part1), (part2, part3))):
-        camera = cam ^ flip
-        at = pl.ds(pl.multiple_of(camera * rows, rows), rows)
-        summed = near[...].astype(jnp.float32) + far[...].astype(jnp.float32)
-        shape = (rows, owners.shape[1])
-        row = lax.broadcasted_iota(jnp.int32, shape, 0)
-        lane = lax.broadcasted_iota(jnp.int32, shape, 1)
-        listed = owners[pl.ds(camera, 1), :] == cam * 4 + slab
-        same = jnp.zeros(shape, jnp.bool_)
-        for group in range(4):
-            same = same | (
-                (row >= group * capacity)
-                & (row < (group + 1) * capacity)
-                & (lane >= group * masked)
-                & (lane < (group + 1) * masked)
-            )
-        count = jnp.sum(jnp.where(same & listed, 1.0, 0.0), axis=1, keepdims=True)
-        order = lax.broadcasted_iota(jnp.int32, (rows, 1), 0)
-        order = order - sum(
-            jnp.where(order >= group * capacity, capacity, 0) for group in range(1, 4)
-        )
-        filled = order.astype(jnp.float32) < count
-        goal = norm_rows(summed).astype(jnp.bfloat16).astype(jnp.float32)
-        out[at] = jnp.where(filled, predicted[at] - goal, 0.0).astype(jnp.bfloat16)
-
-
-def call(kernel, outs, scratch, *args, far=0, copies=0, after=0):
+    rows = near.shape[0]
+    at = pl.ds(pl.multiple_of(cam * rows, rows), rows)
+    listed = owners[pl.ds(cam, 1), :]
+    out[...] = error_rows(capacity, masked, cam * 4 + slab, listed, predicted[at], near, far)
+
+
+def other_camera_kernel(
+    capacity, masked, owners, predicted, first_rows, near, far, out, here, done
+):
+    cam, slab = position()
+    rows = near.shape[0]
+    own = pl.ds(pl.multiple_of(cam * rows, rows), rows)
+    at = pl.ds(pl.multiple_of((1 - cam) * rows, rows), rows)
+    early = pltpu.make_async_copy(first_rows, out.at[own], done.at[0])
+    early.start()
+    listed = owners[pl.ds(1 - cam, 1), :]
+    here[...] = error_rows(capacity, masked, cam * 4 + slab, listed, predicted[at], near, far)
+    late = pltpu.make_async_copy(here, out.at[at], done.at[1])
+    late.start()
+    early.wait()
+    late.wait()
+
+
+def call(kernel, outs, scratch, *args, far=0, copies=0, after=0, out_space=pltpu.VMEM):
     shapes = tuple(jax.ShapeDtypeStruct(shape, dtype) for shape, dtype in outs)
     near = pl.BlockSpec(memory_space=pltpu.VMEM)
     scratch_shapes = [pltpu.VMEM(shape, dtype) for shape, dtype in scratch]
+    if copies:
+        scratch_shapes.append(pltpu.SemaphoreType.DMA((copies,)))
     if far:
-        scratch_shapes.append(pltpu.SemaphoreType.DMA((copies,)))
         args = [pltpu.with_memory_space_constraint(arg, pltpu.HBM) for arg in args[:far]] + list(args[far:])
     return pl.pallas_call(
         kernel,
@@ -519,7 +525,7 @@
         in_specs=[pl.BlockSpec(memory_space=pltpu.HBM)] * far
         + [near] * (len(args) - far - after)
         + [pl.BlockSpec(memory_space=pl.ANY)] * after,
-        out_specs=tuple(near for _ in outs),
+        out_specs=tuple(pl.BlockSpec(memory_space=out_space) for _ in outs),
         scratch_shapes=scratch_shapes,
         compiler_params=pltpu.CompilerParams(vmem_limit_bytes=40 * 2**20),
     )(*args)
@@ -550,16 +556,15 @@
     block = ((block_rows, padded), bf16)
     weight_rows = w_query.shape[0]
     weight_width = 4 * pred_width + w_proj.shape[1]
-    asked_rows = masked + context_rows
-    message_rows = quarter + masked // 2 + masked + tokens - weight_width // -width * weight_rows
-    shard = ((weight_rows, weight_width), bf16)
+    pack_width = weight_width + 2 * pred_width + context_rows * pred_width // weight_rows
+    pack_at = quarter + masked
+    message_rows = pack_at - pack_width // -width * weight_rows + tokens
+    shard = ((weight_rows, pack_width), bf16)
     block0, block2, block3, resid_rows, slot_keys, pack, message, w_here = call(
         functools.partial(pack_kernel, capacity),
         [
-            block, ((block_rows + asked_rows, padded), bf16), block,
-            ((masked, width), bf16), ((4, 2 * masked), jnp.int32), shard,
-            ((message_rows, width), bf16),
-            ((quarter + masked // 2, width), bf16),
+            block, block, block, ((masked, width), bf16), ((4, 2 * masked), jnp.int32), shard,
+            ((message_rows, width), bf16), ((quarter, width), bf16),
         ],
         [
             ((block_rows, width), bf16), ((4, block_rows, padded), bf16), ((tokens, width), bf16),
@@ -569,65 +574,64 @@
         w_query, w_key, w_value, w_out, w_proj, pred_query[0], pred_context[0], w_out_teacher,
         far=14, copies=17,
     )
-    other2, other3, w_cam = send(block2, 2), send(block3, 3), send(w_here, 4)
+    other2, other3 = send(block2, 2), send(block3, 3)
+    w_cam = send(w_here, 4)
     peer_message = send(message, 1)
-    held, passed = call(
-        functools.partial(hold_kernel, quarter + masked // 2 + masked),
-        [((2 * weight_rows, weight_width), bf16), ((asked_rows, pred_width), bf16)],
-        [],
-        pack, other2, peer_message,
+    pair = ((2 * weight_rows, pack_width), bf16)
+    (held,) = call(
+        functools.partial(hold_kernel, pack_at), [pair], [], pack, peer_message, other2, after=1
     )
     first = send_by_core(held, 2, 4)
-    far = send(passed, 4)
     slots = ((16 * capacity, padded), bf16)
-    own_slots, away_slots, w_pass = call(
+    own_slots, away_slots = call(
         functools.partial(teacher_kernel, capacity, head_size, tokens, masked),
-        [slots, slots, (w_out_teacher.shape, bf16)],
+        [slots, slots],
         [
             ((4 * masked, padded), bf16), ((4 * tokens, padded), bf16), ((4 * tokens, padded), bf16),
             ((4 * masked, padded), bf16),
         ],
-        slot_keys, block0, peer_message, other2, other3, w_cam,
-    )
-    peer_slots, w_both = send(away_slots, 1), send(w_pass, 1)
+        slot_keys, block0, peer_message, other2, other3,
+    )
+    peer_slots = send(away_slots, 1)
+    (w_pass,) = call(pass_kernel, [((quarter, width), bf16)], [], w_cam, own_slots, after=1)
+    w_both = send(w_pass, 1)
     part = ((4 * capacity, width), bf16)
     part0, part1, part2, part3 = call(
         functools.partial(project_kernel, capacity),
         [part] * 4,
         [((2 * padded, width), bf16), ((2 * masked, width), bf16), ((4 * capacity, width), f32)],
-        slot_keys, own_slots, peer_slots, w_here, w_cam, peer_message, w_both, resid_rows,
+        slot_keys, own_slots, peer_slots, w_here, w_cam, peer_message,
+        w_both, resid_rows,
     )
     far1, far2, far3 = send(part1, 2), send(part2, 4), send(part3, 6)
-    bundle, forward = call(
-        bundle_kernel,
-        [((2 * weight_rows, weight_width + 4 * pred_width), bf16), shard],
-        [],
-        first, other2, far, w_cam, part0,
-        after=1,
-    )
+    bundle, forward = call(bundle_kernel, [pair, shard], [], first, part0, after=1)
     peers, third = send(bundle, 1), send_by_core(forward, 4, 2)
+    left_width = pack_width // 2 // LANES * LANES
+    halves = [((weight_rows, lanes), bf16) for lanes in (left_width, pack_width - left_width)]
     left, right = call(
-        split_kernel,
-        [((weight_rows, 4 * pred_width), bf16), ((weight_rows, width), bf16)],
-        [],
-        third, peers,
-        after=1,
+        split_kernel, halves, [], third, peers, after=1
     )
     (predicted,) = call(
-        functools.partial(predict_kernel, capacity, quarter),
+        functools.partial(predict_kernel, capacity, pack_at),
         [((8 * capacity, width), f32)],
         [
             ((8 * capacity, pred_width), bf16), ((8 * weight_rows, weight_width), bf16),
-            ((8 * context_rows, pred_width), bf16), ((8 * masked, pred_width), bf16),
+            ((8 * context_rows, pred_width), bf16), ((8 * masked, pred_width), bf16), shard,
         ],
-        slot_keys, w_here, peer_message, w_cam, other2, far,
-        held, first, third, send(left, 1), send(right, 1), peers,
+        slot_keys, peer_message, pack, first, third, send(left, 1), send(right, 1), peers,
+    )
+    (first_rows,) = call(
+        functools.partial(own_camera_kernel, capacity, masked),
+        [part],
+        [],
+        owners, predicted, part0, far1,
     )
     (errors,) = call(
-        functools.partial(finish_kernel, capacity, masked),
+        functools.partial(other_camera_kernel, capacity, masked),
         [((8 * capacity, width), bf16)],
-        [],
-        owners, predicted, part0, far1, far2, far3,
+        [part],
+        owners, predicted, first_rows, far2, far3,
+        copies=2, out_space=pltpu.HBM,
     )
     return errors[None, None]
 

time: 49.8 us -> 47.1 us (0.946); the launches traced: 49.7 us -> 46.3 us
  waiting for transfers between devices: 25.1 us -> 21.6 us
    ppermute x13 -> x12, waiting for transfers between devices: 20.6 us -> 15.2 us  [send(): lax.ppermute(rows, ('cam', 'slab'), [(source, source ^ flip) for source i...]
    ppermute x2, waiting for transfers between devices: 4.42 us -> 6.42 us  [send_by_core(): return lax.ppermute(rows, ('cam', 'slab'), pairs)]
    ppermute x2, starting transfers between devices: 2.42 us -> 3.58 us  [send_by_core(): return lax.ppermute(rows, ('cam', 'slab'), pairs)]
    ppermute x13 -> x12, starting transfers between devices: 10.7 us -> 9.65 us  [send(): lax.ppermute(rows, ('cam', 'slab'), [(source, source ^ flip) for source i...]
    pallas_call x8 -> x10, Pallas kernels: 11.4 us -> 11.3 us  [call(): pl.pallas_call(kernel, out_shape=shapes, in_specs=[pl.BlockSpec(memory_sp...]
  transfers between devices with their start and end apart: 15 -> 14, of which waited for: 7 -> 7; matrix products, arithmetic and copies ran while one was open for 0% -> 0% of each run, Pallas kernels for 15% -> 17%
where the time goes in v5:
time: 47.1 us; the launch traced here: 46.3 us
  waiting for transfers between devices  21.6 us (46%)
  starting transfers between devices  13.2 us (28%)
  Pallas kernels  11.3 us (24%)
    ppermute x12, waiting for transfers between devices, send(): lax.ppermute(rows, ('cam', 'slab'), [(source, source ^ flip) for source i...  15.2 us
    pallas_call x10, Pallas kernels, call(): pl.pallas_call(kernel, out_shape=shapes, in_specs=[pl.BlockSpec(memory_sp...  11.3 us
    ppermute x12, starting transfers between devices, send(): lax.ppermute(rows, ('cam', 'slab'), [(source, source ^ flip) for source i...  9.65 us
    ppermute x2, waiting for transfers between devices, send_by_core(): return lax.ppermute(rows, ('cam', 'slab'), pairs)  6.42 us
    ppermute x2, starting transfers between devices, send_by_core(): return lax.ppermute(rows, ('cam', 'slab'), pairs)  3.58 us
  transfers between devices with their start and end apart: 14, of which 7 were waited for; matrix products, arithmetic and copies ran while one was open for 0% of the time, Pallas kernels for 17%

profile of v5, /device:TPU:0, one launch (start us, length us, event | category | flops | bytes accessed | tf_op | source)
XLA Modules:
  0.0 46.3 jit_solution(6893125141848785708)
XLA Ops:
  0.0 2.3 %shard_map.136 = (bf16[352,384]{1,0:T(8,128)(2,1)S(1)}, bf16[352,384]{1,0:T(8,128)(2,1)S(1)}, bf16[352,384]{1,0:T(8,128)(2,1)S(1)}, bf16[96,1408]{1,0:T(8,128)(2...) custom-call(bf16[128,1408]{1,0:T(8,128)(2,1)} %bitcast.7, ...), custom_call_target="tpu_custom_call" | custom-call | tf_op jit(solution)/shard_map/pallas_call | solution.py:522
  2.3 0.5 %collective-permute-start = (bf16[544,1408]{1,0:T(8,128)(2,1)S(1)}, bf16[544,1408]{1,0:T(8,128)(2,1)S(1)}, u32[]{:S(2)}, u32[]{:S(2)}) collective-permute-start(bf16[544,1408]{1,0:T(8,128)(2,1)S(1)} %get-tuple-element.24), channel_id=1, source_target_pairs={{0,1},{1,0},{2,3},{3,2},{4,5},{5,4},{6,7},{7,6},{8,9},{9,8},{10,11... | collective-permute-start | bytes 4595720 | tf_op jit(solution)/shard_map/ppermute | solution.py:535
  2.8 2.6 %collective-permute-start.1 = (bf16[352,384]{1,0:T(8,128)(2,1)S(1)}, bf16[352,384]{1,0:T(8,128)(2,1)S(1)}, u32[]{:S(2)}, u32[]{:S(2)}) collective-permute-start(bf16[352,384]{1,0:T(8,128)(2,1)S(1)} %get-tuple-element.26), channel_id=1, source_target_pairs={{0,2},{1,3},{2,0},{3,1},{4,6},{5,7},{6,4},{7,5},{8,10},{9,11},{10,... | collective-permute-start | bytes 811016 | tf_op jit(solution)/shard_map/ppermute | solution.py:535
  5.4 1.5 %collective-permute-start.5 = (bf16[176,1408]{1,0:T(8,128)(2,1)S(1)}, bf16[176,1408]{1,0:T(8,128)(2,1)S(1)}, u32[]{:S(2)}, u32[]{:S(2)}) collective-permute-start(bf16[176,1408]{1,0:T(8,128)(2,1)S(1)} %get-tuple-element.31.w_own), channel_id=1, source_target_pairs={{0,4},{1,5},{2,6},{3,7},{4,0},{5,1},{6,2},{7,3},{8,12},{9,13},{10,... | collective-permute-start | bytes 1486856 | tf_op jit(solution)/shard_map/ppermute | solution.py:535
  6.9 0.0 collective-permute-start.3
  7.0 5.8 %collective-permute-done.1.after.block2 = bf16[352,384]{1,0:T(8,128)(2,1)S(1)} collective-permute-done((bf16[352,384]{1,0:T(8,128)(2,1)S(1)}, bf16[352,384]{1,0:T(8,128)(2,1)S(1)}, u32[]{:S(2)}, u32[]{:S(2)}) %collective-permute-start.1) | collective-permute-done | bytes 270368 | tf_op jit(solution)/shard_map/ppermute | solution.py:535
  12.7 0.0 collective-permute-done.message.w_core
  12.8 0.1 shard_map.137
  12.8 2.0 %collective-permute-start.2 = (bf16[96,3968]{1,0:T(8,128)(2,1)S(1)}, bf16[96,3968]{1,0:T(8,128)(2,1)S(1)}, u32[]{:S(2)}, u32[]{:S(2)}) collective-permute-start(bf16[96,3968]{1,0:T(8,128)(2,1)S(1)} %shard_map.137), channel_id=1, source_target_pairs={{0,2},{1,5},{2,0},{3,7},{4,6},{5,1},{6,4},{7,3},{8,10},{9,13},{10,... | collective-permute-start | bytes 2285576 | tf_op jit(solution)/shard_map/ppermute | solution.py:540
  14.8 3.2 %collective-permute-done.3.block3 = bf16[352,384]{1,0:T(8,128)(2,1)S(1)} collective-permute-done((bf16[352,384]{1,0:T(8,128)(2,1)S(1)}, bf16[352,384]{1,0:T(8,128)(2,1)S(1)}, u32[]{:S(2)}, u32[]{:S(2)}) %collective-permute-start.3) | collective-permute-done | bytes 270368 | tf_op jit(solution)/shard_map/ppermute | solution.py:535
  18.0 2.8 %shard_map.138 = (bf16[384,384]{1,0:T(8,128)(2,1)S(1)}, bf16[384,384]{1,0:T(8,128)(2,1)S(1)}) custom-call(s32[4,192]{1,0:T(4,128)S(1)} %get-tuple-element.23.slot_keys, bf16[352,384]{1,0:T(8,128)(2,1)S(1)} %get-tuple-element.27.block0, bf16[544,1408]{1,0:T(8,128)(2,1)S(1)} %collective-permute-done.message.w_core, ...), custom_call_target="tpu_custom_call" | custom-call | tf_op jit(solution)/shard_map/pallas_call | solution.py:522
  20.8 0.0 collective-permute-done.5.rows.w_cam
  20.8 0.4 collective-permute-start.6
  21.3 0.1 collective-permute-start.4
  21.4 1.8 %collective-permute-done.4.peer_slots = bf16[384,384]{1,0:T(8,128)(2,1)S(1)} collective-permute-done((bf16[384,384]{1,0:T(8,128)(2,1)S(1)}, bf16[384,384]{1,0:T(8,128)(2,1)S(1)}, u32[]{:S(2)}, u32[]{:S(2)}) %collective-permute-start.4) | collective-permute-done | bytes 294944 | tf_op jit(solution)/shard_map/ppermute | solution.py:535
  23.2 2.3 %shard_map.140 = (bf16[96,1408]{1,0:T(8,128)(2,1)S(1)}, bf16[96,1408]{1,0:T(8,128)(2,1)S(1)}, bf16[96,1408]{1,0:T(8,128)(2,1)S(1)}, bf16[96,1408]{1,0:T(8,128)(2,1)S(1)}) custom-call(s32[4,192]{1,0:T(4,128)S(1)} %get-tuple-element.23.slot_keys, bf16[384,384]{1,0:T(8,128)(2,1)S(1)} %get-tuple-element.29.after.own_slots, ...), custom_call_target="tpu_custom_call" | custom-call | tf_op jit(solution)/shard_map/pallas_call | solution.py:522
  25.5 0.9 %collective-permute-done.2.first = bf16[96,3968]{1,0:T(8,128)(2,1)S(1)} collective-permute-done((bf16[96,3968]{1,0:T(8,128)(2,1)S(1)}, bf16[96,3968]{1,0:T(8,128)(2,1)S(1)}, u32[]{:S(2)}, u32[]{:S(2)}) %collective-permute-start.2) | collective-permute-done | bytes 761888 | tf_op jit(solution)/shard_map/ppermute | solution.py:540
  26.4 0.1 shard_map.141
  26.5 0.4 collective-permute-start.8
  26.9 1.6 %collective-permute-start.7 = (bf16[48,3968]{1,0:T(8,128)(2,1)S(1)}, bf16[48,3968]{1,0:T(8,128)(2,1)S(1)}, u32[]{:S(2)}, u32[]{:S(2)}) collective-permute-start(bf16[48,3968]{1,0:T(8,128)(2,1)S(1)} %get-tuple-element.34), channel_id=1, source_target_pairs={{0,4},{1,3},{2,6},{3,1},{4,0},{5,7},{6,2},{7,5},{8,12},{9,11},{10,... | collective-permute-start | bytes 1142792 | tf_op jit(solution)/shard_map/ppermute | solution.py:540
  28.5 1.5 %collective-permute-start.11 = (bf16[96,1408]{1,0:T(8,128)(2,1)S(1)}, bf16[96,1408]{1,0:T(8,128)(2,1)S(1)}, u32[]{:S(2)}, u32[]{:S(2)}) collective-permute-start(bf16[96,1408]{1,0:T(8,128)(2,1)S(1)} %get-tuple-element.38), channel_id=1, source_target_pairs={{0,2},{1,3},{2,0},{3,1},{4,6},{5,7},{6,4},{7,5},{8,10},{9,11},{10,... | collective-permute-start | bytes 811016 | tf_op jit(solution)/shard_map/ppermute | solution.py:535
  29.9 0.5 %collective-permute-start.12 = (bf16[96,1408]{1,0:T(8,128)(2,1)S(1)}, bf16[96,1408]{1,0:T(8,128)(2,1)S(1)}, u32[]{:S(2)}, u32[]{:S(2)}) collective-permute-start(bf16[96,1408]{1,0:T(8,128)(2,1)S(1)} %get-tuple-element.39), channel_id=1, source_target_pairs={{0,4},{1,5},{2,6},{3,7},{4,0},{5,1},{6,2},{7,3},{8,12},{9,13},{10,... | collective-permute-start | bytes 811016 | tf_op jit(solution)/shard_map/ppermute | solution.py:535
  30.5 1.5 %collective-permute-start.13 = (bf16[96,1408]{1,0:T(8,128)(2,1)S(1)}, bf16[96,1408]{1,0:T(8,128)(2,1)S(1)}, u32[]{:S(2)}, u32[]{:S(2)}) collective-permute-start(bf16[96,1408]{1,0:T(8,128)(2,1)S(1)} %get-tuple-element.40), channel_id=1, source_target_pairs={{0,6},{1,7},{2,4},{3,5},{4,2},{5,3},{6,0},{7,1},{8,14},{9,15},{10,... | collective-permute-start | bytes 811016 | tf_op jit(solution)/shard_map/ppermute | solution.py:535
  32.0 5.5 %collective-permute-done.7.piece.third = bf16[48,3968]{1,0:T(8,128)(2,1)S(1)} collective-permute-done((bf16[48,3968]{1,0:T(8,128)(2,1)S(1)}, bf16[48,3968]{1,0:T(8,128)(2,1)S(1)}, u32[]{:S(2)}, u32[]{:S(2)}) %collective-permute-start.7) | collective-permute-done | bytes 380960 | tf_op jit(solution)/shard_map/ppermute | solution.py:540
  37.5 0.1 collective-permute-start.10
  37.6 0.0 copy-start
  37.6 0.5 %collective-permute-start.9 = (bf16[48,1920]{1,0:T(8,128)(2,1)S(1)}, bf16[48,1920]{1,0:T(8,128)(2,1)S(1)}, u32[]{:S(2)}, u32[]{:S(2)}) collective-permute-start(bf16[48,1920]{1,0:T(8,128)(2,1)S(1)} %get-tuple-element.36), channel_id=1, source_target_pairs={{0,1},{1,0},{2,3},{3,2},{4,5},{5,4},{6,7},{7,6},{8,9},{9,8},{10,11... | collective-permute-start | bytes 552968 | tf_op jit(solution)/shard_map/ppermute | solution.py:535
  38.1 1.2 %collective-permute-done.9.peer_left = bf16[48,1920]{1,0:T(8,128)(2,1)S(1)} collective-permute-done((bf16[48,1920]{1,0:T(8,128)(2,1)S(1)}, bf16[48,1920]{1,0:T(8,128)(2,1)S(1)}, u32[]{:S(2)}, u32[]{:S(2)}) %collective-permute-start.9) | collective-permute-done | bytes 184352 | tf_op jit(solution)/shard_map/ppermute | solution.py:535
  39.3 2.4 %shard_map.143.predicted = f32[192,1408]{1,0:T(8,128)S(1)} custom-call(s32[4,192]{1,0:T(4,128)S(1)} %get-tuple-element.23.slot_keys, bf16[544,1408]{1,0:T(8,128)(2,1)S(1)} %collective-permute-done.message.w_core, bf16[48,3968]{1,0:T(8,128)(2,1)S(1)} %get-tuple-element.25.pack.own_pack, bf16[96,3968]{1,0:T(8,128)(2,1)S(1)} %collective-permute-done.2.first, ...), custom_call_target="tpu_custom_call" | custom-call | tf_op jit(solution)/shard_map/pallas_call | solution.py:522
  41.7 0.3 shard_map.144.first_rows
  42.0 3.2 %collective-permute-done.12.near = bf16[96,1408]{1,0:T(8,128)(2,1)S(1)} collective-permute-done((bf16[96,1408]{1,0:T(8,128)(2,1)S(1)}, bf16[96,1408]{1,0:T(8,128)(2,1)S(1)}, u32[]{:S(2)}, u32[]{:S(2)}) %collective-permute-start.12) | collective-permute-done | bytes 270368 | tf_op jit(solution)/shard_map/ppermute | solution.py:535
  45.2 1.0 %shard_map.145 = bf16[192,1408]{1,0:T(8,128)(2,1)} custom-call(s32[2,384]{1,0:T(2,128)S(1)} %copy-done, f32[192,1408]{1,0:T(8,128)S(1)} %shard_map.143.predicted, bf16[96,1408]{1,0:T(8,128)(2,1)S(1)} %shard_map.144.first_rows, bf16[96,1408]{1,0:T(8,128)(2,1)S(1)} %collective-permute-done.12.near, bf16[96,1408]{1,0:T(8,128)(2,1)S(1)} %collective-permute-done.13.far), custom_call_target="tpu_custom_call" | custom-call | tf_op jit(solution)/shard_map/pallas_call | solution.py:522
  (8 shorter events, 0.1 us)
Async XLA Ops:
  2.3 10.4 %collective-permute-start = (bf16[544,1408]{1,0:T(8,128)(2,1)S(1)}, bf16[544,1408]{1,0:T(8,128)(2,1)S(1)}, u32[]{:S(2)}, u32[]{:S(2)}) collective-permute-start(bf16[544,1408]{1,0:T(8,128)(2,1)S(1)} %get-tuple-element.24), channel_id=1, source_target_pairs={{0,1},{1,0},{2,3},{3,2},{4,5},{5,4},{6,7},{7,6},{8,9},{9,8},{10,11... | collective-permute-start | bytes 4595720 | tf_op jit(solution)/shard_map/ppermute | solution.py:535
  2.8 9.9 %collective-permute-start.1 = (bf16[352,384]{1,0:T(8,128)(2,1)S(1)}, bf16[352,384]{1,0:T(8,128)(2,1)S(1)}, u32[]{:S(2)}, u32[]{:S(2)}) collective-permute-start(bf16[352,384]{1,0:T(8,128)(2,1)S(1)} %get-tuple-element.26), channel_id=1, source_target_pairs={{0,2},{1,3},{2,0},{3,1},{4,6},{5,7},{6,4},{7,5},{8,10},{9,11},{10,... | collective-permute-start | bytes 811016 | tf_op jit(solution)/shard_map/ppermute | solution.py:535
  5.4 15.4 %collective-permute-start.5 = (bf16[176,1408]{1,0:T(8,128)(2,1)S(1)}, bf16[176,1408]{1,0:T(8,128)(2,1)S(1)}, u32[]{:S(2)}, u32[]{:S(2)}) collective-permute-start(bf16[176,1408]{1,0:T(8,128)(2,1)S(1)} %get-tuple-element.31.w_own), channel_id=1, source_target_pairs={{0,4},{1,5},{2,6},{3,7},{4,0},{5,1},{6,2},{7,3},{8,12},{9,13},{10,... | collective-permute-start | bytes 1486856 | tf_op jit(solution)/shard_map/ppermute | solution.py:535
  6.9 11.1 %collective-permute-start.3 = (bf16[352,384]{1,0:T(8,128)(2,1)S(1)}, bf16[352,384]{1,0:T(8,128)(2,1)S(1)}, u32[]{:S(2)}, u32[]{:S(2)}) collective-permute-start(bf16[352,384]{1,0:T(8,128)(2,1)S(1)} %get-tuple-element.28), channel_id=1, source_target_pairs={{0,3},{1,2},{2,1},{3,0},{4,7},{5,6},{6,5},{7,4},{8,11},{9,10},{10,... | collective-permute-start | bytes 811016 | tf_op jit(solution)/shard_map/ppermute | solution.py:535
  12.8 13.6 %collective-permute-start.2 = (bf16[96,3968]{1,0:T(8,128)(2,1)S(1)}, bf16[96,3968]{1,0:T(8,128)(2,1)S(1)}, u32[]{:S(2)}, u32[]{:S(2)}) collective-permute-start(bf16[96,3968]{1,0:T(8,128)(2,1)S(1)} %shard_map.137), channel_id=1, source_target_pairs={{0,2},{1,5},{2,0},{3,7},{4,6},{5,1},{6,4},{7,3},{8,10},{9,13},{10,... | collective-permute-start | bytes 2285576 | tf_op jit(solution)/shard_map/ppermute | solution.py:540
  20.8 2.4 %collective-permute-start.6 = (bf16[176,1408]{1,0:T(8,128)(2,1)S(1)}, bf16[176,1408]{1,0:T(8,128)(2,1)S(1)}, u32[]{:S(2)}, u32[]{:S(2)}) collective-permute-start(bf16[176,1408]{1,0:T(8,128)(2,1)S(1)} %shard_map.139), channel_id=1, source_target_pairs={{0,1},{1,0},{2,3},{3,2},{4,5},{5,4},{6,7},{7,6},{8,9},{9,8},{10,11... | collective-permute-start | bytes 1486856 | tf_op jit(solution)/shard_map/ppermute | solution.py:535
  21.3 1.9 %collective-permute-start.4 = (bf16[384,384]{1,0:T(8,128)(2,1)S(1)}, bf16[384,384]{1,0:T(8,128)(2,1)S(1)}, u32[]{:S(2)}, u32[]{:S(2)}) collective-permute-start(bf16[384,384]{1,0:T(8,128)(2,1)S(1)} %get-tuple-element.30), channel_id=1, source_target_pairs={{0,1},{1,0},{2,3},{3,2},{4,5},{5,4},{6,7},{7,6},{8,9},{9,8},{10,11... | collective-permute-start | bytes 884744 | tf_op jit(solution)/shard_map/ppermute | solution.py:535
  26.5 10.9 %collective-permute-start.8 = (bf16[96,3968]{1,0:T(8,128)(2,1)S(1)}, bf16[96,3968]{1,0:T(8,128)(2,1)S(1)}, u32[]{:S(2)}, u32[]{:S(2)}) collective-permute-start(bf16[96,3968]{1,0:T(8,128)(2,1)S(1)} %get-tuple-element.35), channel_id=1, source_target_pairs={{0,1},{1,0},{2,3},{3,2},{4,5},{5,4},{6,7},{7,6},{8,9},{9,8},{10,11... | collective-permute-start | bytes 2285576 | tf_op jit(solution)/shard_map/ppermute | solution.py:535
  26.9 10.5 %collective-permute-start.7 = (bf16[48,3968]{1,0:T(8,128)(2,1)S(1)}, bf16[48,3968]{1,0:T(8,128)(2,1)S(1)}, u32[]{:S(2)}, u32[]{:S(2)}) collective-permute-start(bf16[48,3968]{1,0:T(8,128)(2,1)S(1)} %get-tuple-element.34), channel_id=1, source_target_pairs={{0,4},{1,3},{2,6},{3,1},{4,0},{5,7},{6,2},{7,5},{8,12},{9,11},{10,... | collective-permute-start | bytes 1142792 | tf_op jit(solution)/shard_map/ppermute | solution.py:540
  28.5 13.2 %collective-permute-start.11 = (bf16[96,1408]{1,0:T(8,128)(2,1)S(1)}, bf16[96,1408]{1,0:T(8,128)(2,1)S(1)}, u32[]{:S(2)}, u32[]{:S(2)}) collective-permute-start(bf16[96,1408]{1,0:T(8,128)(2,1)S(1)} %get-tuple-element.38), channel_id=1, source_target_pairs={{0,2},{1,3},{2,0},{3,1},{4,6},{5,7},{6,4},{7,5},{8,10},{9,11},{10,... | collective-permute-start | bytes 811016 | tf_op jit(solution)/shard_map/ppermute | solution.py:535
  29.9 15.3 %collective-permute-start.12 = (bf16[96,1408]{1,0:T(8,128)(2,1)S(1)}, bf16[96,1408]{1,0:T(8,128)(2,1)S(1)}, u32[]{:S(2)}, u32[]{:S(2)}) collective-permute-start(bf16[96,1408]{1,0:T(8,128)(2,1)S(1)} %get-tuple-element.39), channel_id=1, source_target_pairs={{0,4},{1,5},{2,6},{3,7},{4,0},{5,1},{6,2},{7,3},{8,12},{9,13},{10,... | collective-permute-start | bytes 811016 | tf_op jit(solution)/shard_map/ppermute | solution.py:535
  30.5 14.8 %collective-permute-start.13 = (bf16[96,1408]{1,0:T(8,128)(2,1)S(1)}, bf16[96,1408]{1,0:T(8,128)(2,1)S(1)}, u32[]{:S(2)}, u32[]{:S(2)}) collective-permute-start(bf16[96,1408]{1,0:T(8,128)(2,1)S(1)} %get-tuple-element.40), channel_id=1, source_target_pairs={{0,6},{1,7},{2,4},{3,5},{4,2},{5,3},{6,0},{7,1},{8,14},{9,15},{10,... | collective-permute-start | bytes 811016 | tf_op jit(solution)/shard_map/ppermute | solution.py:535
  37.5 1.8 %collective-permute-start.10 = (bf16[48,2048]{1,0:T(8,128)(2,1)S(1)}, bf16[48,2048]{1,0:T(8,128)(2,1)S(1)}, u32[]{:S(2)}, u32[]{:S(2)}) collective-permute-start(bf16[48,2048]{1,0:T(8,128)(2,1)S(1)} %get-tuple-element.37), channel_id=1, source_target_pairs={{0,1},{1,0},{2,3},{3,2},{4,5},{5,4},{6,7},{7,6},{8,9},{9,8},{10,11... | collective-permute-start | bytes 589832 | tf_op jit(solution)/shard_map/ppermute | solution.py:535
  37.6 4.1 %copy-start = (s32[2,384]{1,0:T(2,128)S(1)}, s32[2,384]{1,0:T(2,128)}, u32[]{:S(2)}) copy-start(s32[2,384]{1,0:T(2,128)} %owners.5) | copy-start | bytes 9220
  37.6 1.7 %collective-permute-start.9 = (bf16[48,1920]{1,0:T(8,128)(2,1)S(1)}, bf16[48,1920]{1,0:T(8,128)(2,1)S(1)}, u32[]{:S(2)}, u32[]{:S(2)}) collective-permute-start(bf16[48,1920]{1,0:T(8,128)(2,1)S(1)} %get-tuple-element.36), channel_id=1, source_target_pairs={{0,1},{1,0},{2,3},{3,2},{4,5},{5,4},{6,7},{7,6},{8,9},{9,8},{10,11... | collective-permute-start | bytes 552968 | tf_op jit(solution)/shard_map/ppermute | solution.py:535

commit v6 on v5

--- a/solution.py
+++ b/solution.py
@@ -210,6 +210,7 @@
         (value, stack.at[tokens : 2 * tokens]),
         (resid, resid_here),
         (w_far, w_here),
+        (w_far, message.at[0:quarter]),
     ]
     at = 0
     for part in (wq, wk, wv, wo, wp):
@@ -271,42 +272,125 @@
     core_block = blocks.at[slab ^ 1]
     for copy in copies[5:]:
         copy.wait()
-    resid_rows[...] = dot(chosen, resid_here[...]).astype(jnp.bfloat16)
-    base = w_here.shape[0]
-    message[0:base] = w_here[...]
-    message[base : base + masked] = resid_rows[...]
-    base += masked
-    count = pack.shape[0]
-    total = pack.shape[1]
-    message[base + 2 * count : base + 3 * count] = jnp.zeros((count, width), jnp.bfloat16)
+    picked = dot(chosen, resid_here[...]).astype(jnp.bfloat16)
+    resid_rows[...] = picked
+    base = quarter + masked
+    message[quarter:base] = picked
+    count, total = pack.shape
     for low in range(0, total, width):
         high = min(low + width, total)
         message[base : base + count, 0 : high - low] = pack[:, low:high]
+        if high - low < width:
+            message[base : base + count, high - low :] = jnp.zeros(
+                (count, width - high + low), jnp.bfloat16
+            )
         base += count
-    message[base:] = jnp.zeros((tokens, width), jnp.bfloat16)
+    wide = core_block.shape[1]
     for number in range(3):
         low, high = number * tokens, min((number + 1) * tokens, row_total)
-        lanes = slice(number * core_block.shape[1], (number + 1) * core_block.shape[1])
+        lanes = slice(number * wide, (number + 1) * wide)
         message[base : base + high - low, lanes] = core_block[low:high]
-
-
-def hold_kernel(base, pack, message, after, held):
-    core = lax.axis_index("slab") % 2
-    rows, wide = pack.shape
-    width = message.shape[1]
-    held[pl.ds(pl.multiple_of(core * rows, rows), rows)] = pack[...]
-    other = pl.ds(pl.multiple_of((1 - core) * rows, rows), rows)
-    for number, low in enumerate(range(0, wide, width)):
-        high = min(low + width, wide)
-        at = base + number * rows
-        held[other, low:high] = message[at : at + rows, 0 : high - low]
-
-
-def bundle_kernel(first, after, out, forward):
+    message[base + masked :, 2 * wide : 3 * wide] = jnp.zeros((tokens - masked, wide), jnp.bfloat16)
+    message[base:, 3 * wide :] = jnp.zeros((tokens, width - 3 * wide), jnp.bfloat16)
+
+
+def hold_kernel(
+    capacity, base, width, context_rows, slot_keys, pack, message, after, held, own_asks,
+    peer, pair,
+):
+    cam, slab = position()
+    core = slab % 2
+    chip = cam * 4 + slab - core
+    part, total = pack.shape
+    lanes = message.shape[1]
+    for number, low in enumerate(range(0, total, lanes)):
+        high = min(low + lanes, total)
+        at = base + number * part
+        peer[:, low:high] = message[at : at + part, 0 : high - low]
+    wide = total - 2 * width - context_rows * width // part
+    low, tail = wide + width, wide + 2 * width
+    rest = part - context_rows
+
+    def fill(source, packs):
+        held[pl.ds(pl.multiple_of(source * part, part), part), 0:wide] = packs[:, 0:wide]
+        for number in range(2):
+            start = pl.multiple_of((2 * source + number) * part, part)
+            pair[pl.ds(start, part)] = packs[:, wide + number * width : wide + (number + 1) * width]
+
+    fill(core, pack)
+    fill(1 - core, peer)
+    held[part:, low:] = jnp.zeros((part, held.shape[1] - low), jnp.bfloat16)
+
+    def contexts(first, second):
+        split = 2 * LANES
+        held[0:context_rows, tail:] = first[0:context_rows, tail : tail + LANES]
+        held[part : part + context_rows, tail:] = first[0:context_rows, tail + LANES :]
+        held[context_rows:part, tail:] = first[context_rows:, tail : tail + LANES]
+        held[part + context_rows :, tail:] = first[context_rows:, tail + LANES :]
+        held[part : part + context_rows, low : low + split] = second[0:context_rows, tail:]
+        for number in range(2):
+            at = part + number * rest
+            source = slice(tail + number * LANES, tail + (number + 1) * LANES)
+            held[at : at + rest, low + split : tail] = second[context_rows:, source]
+
+    @pl.when(core == 0)
+    def _():
+        contexts(pack, peer)
+
+    @pl.when(core == 1)
+    def _():
+        contexts(peer, pack)
+
+    key_row = slot_keys[pl.ds(2 * cam + slab // 2, 1), :]
+
+    def slots(owner):
+        picker = slot_picker(key_row, owner, capacity, 8 * capacity)
+        return dot(picker, pair[...]).astype(jnp.bfloat16)
+
+    beside = chip ^ jnp.where(core == 0, 2, 4)
+    held[0:part, wide:low] = slots(beside)
+    held[part:, wide:low] = slots(beside + 1)
+    held[0:part, low:tail] = slots((chip ^ 6) + core)
+    own_asks[...] = slots(chip + core)
+
+
+def context_pieces(packs, part, context_rows, low, tail):
+    rest = part - context_rows
+    first = (
+        (0, context_rows, 0, packs.at[0:context_rows, tail:]),
+        (0, context_rows, LANES, packs.at[part : part + context_rows, tail:]),
+        (0, rest, 2 * LANES, packs.at[context_rows:part, tail:]),
+        (rest, rest, 2 * LANES, packs.at[part + context_rows :, tail:]),
+    )
+    return first, ((0, context_rows, 0, packs.at[part : part + context_rows, low:tail]),)
+
+
+def bundle_kernel(width, context_rows, first, after, out, forward):
     core = lax.axis_index("slab") % 2
     part = forward.shape[0]
-    forward[...] = first[pl.ds(pl.multiple_of(core * part, part), part)]
+    rest = part - context_rows
+    total = first.shape[1]
+    low, tail = total - LANES - width, total - LANES
+    wide = low - width
+    forward[:, 0:wide] = first[pl.ds(pl.multiple_of(core * part, part), part), 0:wide]
+    forward[:, wide:low] = first[0:part, low:tail]
     out[...] = first[...]
+    pieces = context_pieces(first, part, context_rows, low, tail)
+
+    @pl.when(core == 0)
+    def _():
+        left, middle, upper, lower = (piece[3] for piece in pieces[0])
+        forward[0:context_rows, low : low + LANES] = left[...]
+        forward[0:context_rows, low + LANES :] = middle[...]
+        forward[context_rows:, low : low + LANES] = upper[...]
+        forward[context_rows:, low + LANES :] = lower[...]
+
+    @pl.when(core == 1)
+    def _():
+        whole = pieces[1][0][3]
+        forward[0:context_rows, low:] = whole[:, 0 : 2 * LANES]
+        forward[context_rows:, low : low + LANES] = whole[0:rest, 2 * LANES :]
+        forward[context_rows:, low + LANES :] = whole[rest:, 2 * LANES :]
 
 
 def split_kernel(piece, after, left, right):
@@ -395,54 +479,57 @@
 
 
 def predict_kernel(
-    capacity, base, slot_keys, message, own_pack, first, third, peer_left, peer_right, peers, out,
-    queries, weights, context, asks, peer_pack,
+    base, context_rows, message, own_pack, own_asks, first, third, peer_left, peer_right, peers, out,
+    queries, weights, context, peer_pack, peer_third,
 ):
     cam, slab = position()
     core = slab % 2
     own = cam * 4 + slab
-    part, total = third.shape
-    wide = weights.shape[1]
+    chip = own - core
+    part, wide = third.shape[0], weights.shape[1]
     width = context.shape[1]
-    context_rows = context.shape[0] // 8
-    masked = asks.shape[0] // 8
-
-    def place(source, piece):
-        weights[pl.ds(pl.multiple_of(source * part, part), part)] = piece[:, 0:wide]
+    rest = part - context_rows
+    low, tail = wide + width, wide + 2 * width
+
+    def place(source, packs, at):
+        weights[pl.ds(pl.multiple_of(source * part, part), part)] = packs[:, 0:wide]
+        start = pl.multiple_of(source * context_rows, context_rows)
+        context[pl.ds(start, context_rows), 0 : 2 * LANES] = packs[0:context_rows, at:]
         for number in range(2):
-            start = pl.multiple_of(source * masked + number * part, part)
-            low = wide + number * width
-            asks[pl.ds(start, part)] = piece[:, low : low + width]
-        low = wide + 2 * width
-        split, rest = total - low, part - context_rows
-        start = pl.multiple_of(source * context_rows, context_rows)
-        context[pl.ds(start, context_rows), 0:split] = piece[0:context_rows, low:]
-        for number in range(context_rows // rest):
-            at = low + number * (width - split)
-            context[pl.ds(pl.multiple_of(start + number * rest, rest), rest), split:] = piece[
-                context_rows:, at : at + width - split
-            ]
-
-    place(own, own_pack)
-    for number, low in enumerate(range(0, total, message.shape[1])):
-        high = min(low + message.shape[1], total)
+            lanes = slice(at + number * LANES, at + (number + 1) * LANES)
+            rows = pl.ds(pl.multiple_of(start + number * rest, rest), rest)
+            context[rows, 2 * LANES :] = packs[context_rows:, lanes]
+
+    def place_pair(source, packs):
+        for flip, pieces in enumerate(context_pieces(packs, part, context_rows, low, tail)):
+            rows = pl.ds(pl.multiple_of((source + flip) * part, part), part)
+            weights[rows] = packs[flip * part : (flip + 1) * part, 0:wide]
+            start = pl.multiple_of((source + flip) * context_rows, context_rows)
+            for skip, count, lane, piece in pieces:
+                rows = pl.ds(pl.multiple_of(start + skip, rest), count)
+                context[rows, lane : lane + piece.shape[1]] = piece[...]
+
+    def place_asks(source, asked):
+        queries[pl.ds(pl.multiple_of(source // 2 * part, part), part)] = asked
+
+    for number, start in enumerate(range(0, own_pack.shape[1], message.shape[1])):
+        stop = min(start + message.shape[1], own_pack.shape[1])
         at = base + number * part
-        peer_pack[:, low:high] = message[at : at + part, 0 : high - low]
-    place(own ^ 1, peer_pack)
-    chip = own - core
+        peer_pack[:, start:stop] = message[at : at + part, 0 : stop - start]
+    peer_third[:, 0 : peer_left.shape[1]] = peer_left[...]
+    peer_third[:, peer_left.shape[1] :] = peer_right[...]
+    place(own, own_pack, tail)
+    place(own ^ 1, peer_pack, tail)
+    place(own ^ 6, third, low)
+    place(own ^ 7, peer_third, low)
     along, across = jnp.where(core == 0, 2, 4), jnp.where(core == 0, 4, 2)
-    for flip in range(2):
-        place((chip ^ along) + flip, first.at[flip * part : (flip + 1) * part])
-        place((chip ^ across) + flip, peers.at[flip * part : (flip + 1) * part])
-    place(own ^ 6, third)
-    peer_pack[:, 0 : peer_left.shape[1]] = peer_left[...]
-    peer_pack[:, peer_left.shape[1] :] = peer_right[...]
-    place(own ^ 7, peer_pack)
-    for chip in range(4):
-        picker = slot_picker(slot_keys[chip : chip + 1, :], own, capacity, 8 * capacity)
-        queries[chip * 2 * capacity : (chip + 1) * 2 * capacity] = dot(
-            picker, asks[chip * 2 * masked : (chip + 1) * 2 * masked]
-        ).astype(jnp.bfloat16)
+    place_pair(chip ^ along, first)
+    place_pair(chip ^ across, peers)
+    mine = pl.ds(pl.multiple_of(core * part, part), part)
+    place_asks(chip, own_asks[...])
+    place_asks(chip ^ 6, third[:, wide:low])
+    place_asks(chip ^ along, first[mine, wide:low])
+    place_asks(chip ^ across, peers[mine, wide:low])
     head_size = width // P_HEADS
     scale = math.log2(math.e) / math.sqrt(head_size)
     asked = dot(queries[...], weights[:, 0:width]).astype(jnp.bfloat16)
@@ -572,14 +659,20 @@
         ],
         t_query[0], t_key[0], t_value[0], t_resid[0], mask_list, owners,
         w_query, w_key, w_value, w_out, w_proj, pred_query[0], pred_context[0], w_out_teacher,
-        far=14, copies=17,
+        far=14, copies=18,
     )
     other2, other3 = send(block2, 2), send(block3, 3)
     w_cam = send(w_here, 4)
     peer_message = send(message, 1)
-    pair = ((2 * weight_rows, pack_width), bf16)
-    (held,) = call(
-        functools.partial(hold_kernel, pack_at), [pair], [], pack, peer_message, other2, after=1
+    pair = ((2 * weight_rows, weight_width + 2 * pred_width + LANES), bf16)
+    forwarded = ((weight_rows, weight_width + pred_width + 2 * LANES), bf16)
+    asked = ((2 * capacity, pred_width), bf16)
+    held, own_asks = call(
+        functools.partial(hold_kernel, capacity, pack_at, pred_width, context_rows),
+        [pair, asked],
+        [shard, ((2 * masked, pred_width), bf16)],
+        slot_keys, pack, peer_message, other2,
+        after=1,
     )
     first = send_by_core(held, 2, 4)
     slots = ((16 * capacity, padded), bf16)
@@ -604,21 +697,26 @@
         w_both, resid_rows,
     )
     far1, far2, far3 = send(part1, 2), send(part2, 4), send(part3, 6)
-    bundle, forward = call(bundle_kernel, [pair, shard], [], first, part0, after=1)
+    bundle, forward = call(
+        functools.partial(bundle_kernel, pred_width, context_rows),
+        [pair, forwarded], [], first, part0,
+        after=1,
+    )
     peers, third = send(bundle, 1), send_by_core(forward, 4, 2)
-    left_width = pack_width // 2 // LANES * LANES
-    halves = [((weight_rows, lanes), bf16) for lanes in (left_width, pack_width - left_width)]
+    whole = forwarded[0][1]
+    left_width = whole // 2 // LANES * LANES
+    halves = [((weight_rows, lanes), bf16) for lanes in (left_width, whole - left_width)]
     left, right = call(
         split_kernel, halves, [], third, peers, after=1
     )
     (predicted,) = call(
-        functools.partial(predict_kernel, capacity, pack_at),
+        functools.partial(predict_kernel, pack_at, context_rows),
         [((8 * capacity, width), f32)],
         [
             ((8 * capacity, pred_width), bf16), ((8 * weight_rows, weight_width), bf16),
-            ((8 * context_rows, pred_width), bf16), ((8 * masked, pred_width), bf16), shard,
+            ((8 * context_rows, pred_width), bf16), shard, forwarded,
         ],
-        slot_keys, peer_message, pack, first, third, send(left, 1), send(right, 1), peers,
+        peer_message, pack, own_asks, first, third, send(left, 1), send(right, 1), peers,
     )
     (first_rows,) = call(
         functools.partial(own_camera_kernel, capacity, masked),
@@ -630,7 +728,7 @@
         functools.partial(other_camera_kernel, capacity, masked),
         [((8 * capacity, width), bf16)],
         [part],
-        owners, predicted, first_rows, far2, far3,
+        owners, predicted, first_rows, far3, far2,
         copies=2, out_space=pltpu.HBM,
     )
     return errors[None, None]

time: 47.1 us -> 46.4 us (0.985)
  waiting for transfers between devices: 21.6 us -> 20.8 us
    ppermute x2, waiting for transfers between devices: 6.42 us -> 3.49 us  [send_by_core(): return lax.ppermute(rows, ('cam', 'slab'), pairs)]
    ppermute x12, waiting for transfers between devices: 15.2 us -> 17.3 us  [send(): lax.ppermute(rows, ('cam', 'slab'), [(source, source ^ flip) for source i...]
  transfers between devices with their start and end apart: 14 -> 14, of which waited for: 7 -> 9; matrix products, arithmetic and copies ran while one was open for 0% -> 0% of each run, Pallas kernels for 17% -> 18%
where the time goes in v6:
time: 46.4 us; the launch traced here: 45.6 us
  waiting for transfers between devices  20.8 us (45%)
  starting transfers between devices  13.2 us (28%)
  Pallas kernels  11.4 us (25%)
    ppermute x12, waiting for transfers between devices, send(): lax.ppermute(rows, ('cam', 'slab'), [(source, source ^ flip) for source i...  17.3 us
    pallas_call x10, Pallas kernels, call(): pl.pallas_call(kernel, out_shape=shapes, in_specs=[pl.BlockSpec(memory_sp...  11.4 us
    ppermute x12, starting transfers between devices, send(): lax.ppermute(rows, ('cam', 'slab'), [(source, source ^ flip) for source i...  9.65 us
    ppermute x2, starting transfers between devices, send_by_core(): return lax.ppermute(rows, ('cam', 'slab'), pairs)  3.58 us
    ppermute x2, waiting for transfers between devices, send_by_core(): return lax.ppermute(rows, ('cam', 'slab'), pairs)  3.49 us
  transfers between devices with their start and end apart: 14, of which 9 were waited for; matrix products, arithmetic and copies ran while one was open for 0% of the time, Pallas kernels for 18%

profile of v6, /device:TPU:0, one launch (start us, length us, event | category | flops | bytes accessed | tf_op | source)
XLA Modules:
  0.0 45.6 jit_solution(16489269414354854396)
XLA Ops:
  0.0 2.3 %shard_map.136 = (bf16[352,384]{1,0:T(8,128)(2,1)S(1)}, bf16[352,384]{1,0:T(8,128)(2,1)S(1)}, bf16[352,384]{1,0:T(8,128)(2,1)S(1)}, bf16[96,1408]{1,0:T(8,128)(2...) custom-call(bf16[128,1408]{1,0:T(8,128)(2,1)} %bitcast.7, ...), custom_call_target="tpu_custom_call" | custom-call | tf_op jit(solution)/shard_map/pallas_call | solution.py:609
  2.3 0.5 %collective-permute-start = (bf16[544,1408]{1,0:T(8,128)(2,1)S(1)}, bf16[544,1408]{1,0:T(8,128)(2,1)S(1)}, u32[]{:S(2)}, u32[]{:S(2)}) collective-permute-start(bf16[544,1408]{1,0:T(8,128)(2,1)S(1)} %get-tuple-element.25), channel_id=1, source_target_pairs={{0,1},{1,0},{2,3},{3,2},{4,5},{5,4},{6,7},{7,6},{8,9},{9,8},{10,11... | collective-permute-start | bytes 4595720 | tf_op jit(solution)/shard_map/ppermute | solution.py:622
  2.8 2.6 %collective-permute-start.1 = (bf16[352,384]{1,0:T(8,128)(2,1)S(1)}, bf16[352,384]{1,0:T(8,128)(2,1)S(1)}, u32[]{:S(2)}, u32[]{:S(2)}) collective-permute-start(bf16[352,384]{1,0:T(8,128)(2,1)S(1)} %get-tuple-element.28), channel_id=1, source_target_pairs={{0,2},{1,3},{2,0},{3,1},{4,6},{5,7},{6,4},{7,5},{8,10},{9,11},{10,... | collective-permute-start | bytes 811016 | tf_op jit(solution)/shard_map/ppermute | solution.py:622
  5.4 1.5 %collective-permute-start.5 = (bf16[176,1408]{1,0:T(8,128)(2,1)S(1)}, bf16[176,1408]{1,0:T(8,128)(2,1)S(1)}, u32[]{:S(2)}, u32[]{:S(2)}) collective-permute-start(bf16[176,1408]{1,0:T(8,128)(2,1)S(1)} %get-tuple-element.35.w_own), channel_id=1, source_target_pairs={{0,4},{1,5},{2,6},{3,7},{4,0},{5,1},{6,2},{7,3},{8,12},{9,13},{10,... | collective-permute-start | bytes 1486856 | tf_op jit(solution)/shard_map/ppermute | solution.py:622
  6.9 0.0 collective-permute-start.3
  6.9 5.8 %collective-permute-done.1.after.block2 = bf16[352,384]{1,0:T(8,128)(2,1)S(1)} collective-permute-done((bf16[352,384]{1,0:T(8,128)(2,1)S(1)}, bf16[352,384]{1,0:T(8,128)(2,1)S(1)}, u32[]{:S(2)}, u32[]{:S(2)}) %collective-permute-start.1) | collective-permute-done | bytes 270368 | tf_op jit(solution)/shard_map/ppermute | solution.py:622
  12.7 0.0 collective-permute-done.message.w_core
  12.7 0.3 shard_map.137
  13.1 2.0 %collective-permute-start.2 = (bf16[96,3840]{1,0:T(8,128)(2,1)S(1)}, bf16[96,3840]{1,0:T(8,128)(2,1)S(1)}, u32[]{:S(2)}, u32[]{:S(2)}) collective-permute-start(bf16[96,3840]{1,0:T(8,128)(2,1)S(1)} %get-tuple-element.30), channel_id=1, source_target_pairs={{0,2},{1,5},{2,0},{3,7},{4,6},{5,1},{6,4},{7,3},{8,10},{9,13},{10,... | collective-permute-start | bytes 2211848 | tf_op jit(solution)/shard_map/ppermute | solution.py:627
  15.1 2.9 %collective-permute-done.3.block3 = bf16[352,384]{1,0:T(8,128)(2,1)S(1)} collective-permute-done((bf16[352,384]{1,0:T(8,128)(2,1)S(1)}, bf16[352,384]{1,0:T(8,128)(2,1)S(1)}, u32[]{:S(2)}, u32[]{:S(2)}) %collective-permute-start.3) | collective-permute-done | bytes 270368 | tf_op jit(solution)/shard_map/ppermute | solution.py:622
  18.0 2.8 %shard_map.138 = (bf16[384,384]{1,0:T(8,128)(2,1)S(1)}, bf16[384,384]{1,0:T(8,128)(2,1)S(1)}) custom-call(s32[4,192]{1,0:T(4,128)S(1)} %get-tuple-element.27.slot_keys, bf16[352,384]{1,0:T(8,128)(2,1)S(1)} %get-tuple-element.31.block0, bf16[544,1408]{1,0:T(8,128)(2,1)S(1)} %collective-permute-done.message.w_core, ...), custom_call_target="tpu_custom_call" | custom-call | tf_op jit(solution)/shard_map/pallas_call | solution.py:609
  20.8 0.4 collective-permute-start.6
  21.3 0.1 collective-permute-start.4
  21.4 1.8 %collective-permute-done.4.peer_slots = bf16[384,384]{1,0:T(8,128)(2,1)S(1)} collective-permute-done((bf16[384,384]{1,0:T(8,128)(2,1)S(1)}, bf16[384,384]{1,0:T(8,128)(2,1)S(1)}, u32[]{:S(2)}, u32[]{:S(2)}) %collective-permute-start.4) | collective-permute-done | bytes 294944 | tf_op jit(solution)/shard_map/ppermute | solution.py:622
  23.2 2.3 %shard_map.140 = (bf16[96,1408]{1,0:T(8,128)(2,1)S(1)}, bf16[96,1408]{1,0:T(8,128)(2,1)S(1)}, bf16[96,1408]{1,0:T(8,128)(2,1)S(1)}, bf16[96,1408]{1,0:T(8,128)(2,1)S(1)}) custom-call(s32[4,192]{1,0:T(4,128)S(1)} %get-tuple-element.27.slot_keys, bf16[384,384]{1,0:T(8,128)(2,1)S(1)} %get-tuple-element.33.after.own_slots, ...), custom_call_target="tpu_custom_call" | custom-call | tf_op jit(solution)/shard_map/pallas_call | solution.py:609
  25.5 0.6 %collective-permute-done.2.first = bf16[96,3840]{1,0:T(8,128)(2,1)S(1)} collective-permute-done((bf16[96,3840]{1,0:T(8,128)(2,1)S(1)}, bf16[96,3840]{1,0:T(8,128)(2,1)S(1)}, u32[]{:S(2)}, u32[]{:S(2)}) %collective-permute-start.2) | collective-permute-done | bytes 737312 | tf_op jit(solution)/shard_map/ppermute | solution.py:627
  26.1 0.1 shard_map.141
  26.2 0.4 collective-permute-start.8
  26.6 1.6 %collective-permute-start.7 = (bf16[48,3584]{1,0:T(8,128)(2,1)S(1)}, bf16[48,3584]{1,0:T(8,128)(2,1)S(1)}, u32[]{:S(2)}, u32[]{:S(2)}) collective-permute-start(bf16[48,3584]{1,0:T(8,128)(2,1)S(1)} %get-tuple-element.38), channel_id=1, source_target_pairs={{0,4},{1,3},{2,6},{3,1},{4,0},{5,7},{6,2},{7,5},{8,12},{9,11},{10,... | collective-permute-start | bytes 1032200 | tf_op jit(solution)/shard_map/ppermute | solution.py:627
  28.2 1.5 %collective-permute-start.11 = (bf16[96,1408]{1,0:T(8,128)(2,1)S(1)}, bf16[96,1408]{1,0:T(8,128)(2,1)S(1)}, u32[]{:S(2)}, u32[]{:S(2)}) collective-permute-start(bf16[96,1408]{1,0:T(8,128)(2,1)S(1)} %get-tuple-element.42), channel_id=1, source_target_pairs={{0,2},{1,3},{2,0},{3,1},{4,6},{5,7},{6,4},{7,5},{8,10},{9,11},{10,... | collective-permute-start | bytes 811016 | tf_op jit(solution)/shard_map/ppermute | solution.py:622
  29.7 0.5 %collective-permute-start.12 = (bf16[96,1408]{1,0:T(8,128)(2,1)S(1)}, bf16[96,1408]{1,0:T(8,128)(2,1)S(1)}, u32[]{:S(2)}, u32[]{:S(2)}) collective-permute-start(bf16[96,1408]{1,0:T(8,128)(2,1)S(1)} %get-tuple-element.43), channel_id=1, source_target_pairs={{0,6},{1,7},{2,4},{3,5},{4,2},{5,3},{6,0},{7,1},{8,14},{9,15},{10,... | collective-permute-start | bytes 811016 | tf_op jit(solution)/shard_map/ppermute | solution.py:622
  30.1 1.6 %collective-permute-start.13 = (bf16[96,1408]{1,0:T(8,128)(2,1)S(1)}, bf16[96,1408]{1,0:T(8,128)(2,1)S(1)}, u32[]{:S(2)}, u32[]{:S(2)}) collective-permute-start(bf16[96,1408]{1,0:T(8,128)(2,1)S(1)} %get-tuple-element.44), channel_id=1, source_target_pairs={{0,4},{1,5},{2,6},{3,7},{4,0},{5,1},{6,2},{7,3},{8,12},{9,13},{10,... | collective-permute-start | bytes 811016 | tf_op jit(solution)/shard_map/ppermute | solution.py:622
  31.7 2.8 %collective-permute-done.7.piece.third = bf16[48,3584]{1,0:T(8,128)(2,1)S(1)} collective-permute-done((bf16[48,3584]{1,0:T(8,128)(2,1)S(1)}, bf16[48,3584]{1,0:T(8,128)(2,1)S(1)}, u32[]{:S(2)}, u32[]{:S(2)}) %collective-permute-start.7) | collective-permute-done | bytes 344096 | tf_op jit(solution)/shard_map/ppermute | solution.py:627
  34.6 0.1 collective-permute-start.9
  34.6 0.5 %collective-permute-start.10 = (bf16[48,1792]{1,0:T(8,128)(2,1)S(1)}, bf16[48,1792]{1,0:T(8,128)(2,1)S(1)}, u32[]{:S(2)}, u32[]{:S(2)}) collective-permute-start(bf16[48,1792]{1,0:T(8,128)(2,1)S(1)} %get-tuple-element.41), channel_id=1, source_target_pairs={{0,1},{1,0},{2,3},{3,2},{4,5},{5,4},{6,7},{7,6},{8,9},{9,8},{10,11... | collective-permute-start | bytes 516104 | tf_op jit(solution)/shard_map/ppermute | solution.py:622
  35.1 0.9 %collective-permute-done.9.peer_left = bf16[48,1792]{1,0:T(8,128)(2,1)S(1)} collective-permute-done((bf16[48,1792]{1,0:T(8,128)(2,1)S(1)}, bf16[48,1792]{1,0:T(8,128)(2,1)S(1)}, u32[]{:S(2)}, u32[]{:S(2)}) %collective-permute-start.9) | collective-permute-done | bytes 172064 | tf_op jit(solution)/shard_map/ppermute | solution.py:622
  36.0 0.2 collective-permute-done.10.peer_right
  36.3 2.2 %shard_map.143.predicted = f32[192,1408]{1,0:T(8,128)S(1)} custom-call(bf16[544,1408]{1,0:T(8,128)(2,1)S(1)} %collective-permute-done.message.w_core, bf16[48,3968]{1,0:T(8,128)(2,1)S(1)} %get-tuple-element.26.pack.own_pack, bf16[48,384]{1,0:T(8,128)(2,1)S(1)} %get-tuple-element.29.own_asks, bf16[96,3840]{1,0:T(8,128)(2,1)S(1)} %collective-permute-done.2.first, ...), custom_call_target="tpu_custom_call" | custom-call | tf_op jit(solution)/shard_map/pallas_call | solution.py:609
  38.5 0.3 shard_map.144.first_rows
  38.9 4.4 %collective-permute-done.12.near = bf16[96,1408]{1,0:T(8,128)(2,1)S(1)} collective-permute-done((bf16[96,1408]{1,0:T(8,128)(2,1)S(1)}, bf16[96,1408]{1,0:T(8,128)(2,1)S(1)}, u32[]{:S(2)}, u32[]{:S(2)}) %collective-permute-start.12) | collective-permute-done | bytes 270368 | tf_op jit(solution)/shard_map/ppermute | solution.py:622
  43.2 1.3 %collective-permute-done.13.far = bf16[96,1408]{1,0:T(8,128)(2,1)S(1)} collective-permute-done((bf16[96,1408]{1,0:T(8,128)(2,1)S(1)}, bf16[96,1408]{1,0:T(8,128)(2,1)S(1)}, u32[]{:S(2)}, u32[]{:S(2)}) %collective-permute-start.13) | collective-permute-done | bytes 270368 | tf_op jit(solution)/shard_map/ppermute | solution.py:622
  44.5 1.0 %shard_map.145 = bf16[192,1408]{1,0:T(8,128)(2,1)} custom-call(s32[2,384]{1,0:T(2,128)S(1)} %copy-done, f32[192,1408]{1,0:T(8,128)S(1)} %shard_map.143.predicted, bf16[96,1408]{1,0:T(8,128)(2,1)S(1)} %shard_map.144.first_rows, bf16[96,1408]{1,0:T(8,128)(2,1)S(1)} %collective-permute-done.12.near, bf16[96,1408]{1,0:T(8,128)(2,1)S(1)} %collective-permute-done.13.far), custom_call_target="tpu_custom_call" | custom-call | tf_op jit(solution)/shard_map/pallas_call | solution.py:609
  (8 shorter events, 0.1 us)
Async XLA Ops:
  2.3 10.4 %collective-permute-start = (bf16[544,1408]{1,0:T(8,128)(2,1)S(1)}, bf16[544,1408]{1,0:T(8,128)(2,1)S(1)}, u32[]{:S(2)}, u32[]{:S(2)}) collective-permute-start(bf16[544,1408]{1,0:T(8,128)(2,1)S(1)} %get-tuple-element.25), channel_id=1, source_target_pairs={{0,1},{1,0},{2,3},{3,2},{4,5},{5,4},{6,7},{7,6},{8,9},{9,8},{10,11... | collective-permute-start | bytes 4595720 | tf_op jit(solution)/shard_map/ppermute | solution.py:622
  2.8 9.9 %collective-permute-start.1 = (bf16[352,384]{1,0:T(8,128)(2,1)S(1)}, bf16[352,384]{1,0:T(8,128)(2,1)S(1)}, u32[]{:S(2)}, u32[]{:S(2)}) collective-permute-start(bf16[352,384]{1,0:T(8,128)(2,1)S(1)} %get-tuple-element.28), channel_id=1, source_target_pairs={{0,2},{1,3},{2,0},{3,1},{4,6},{5,7},{6,4},{7,5},{8,10},{9,11},{10,... | collective-permute-start | bytes 811016 | tf_op jit(solution)/shard_map/ppermute | solution.py:622
  5.4 15.4 %collective-permute-start.5 = (bf16[176,1408]{1,0:T(8,128)(2,1)S(1)}, bf16[176,1408]{1,0:T(8,128)(2,1)S(1)}, u32[]{:S(2)}, u32[]{:S(2)}) collective-permute-start(bf16[176,1408]{1,0:T(8,128)(2,1)S(1)} %get-tuple-element.35.w_own), channel_id=1, source_target_pairs={{0,4},{1,5},{2,6},{3,7},{4,0},{5,1},{6,2},{7,3},{8,12},{9,13},{10,... | collective-permute-start | bytes 1486856 | tf_op jit(solution)/shard_map/ppermute | solution.py:622
  6.9 11.1 %collective-permute-start.3 = (bf16[352,384]{1,0:T(8,128)(2,1)S(1)}, bf16[352,384]{1,0:T(8,128)(2,1)S(1)}, u32[]{:S(2)}, u32[]{:S(2)}) collective-permute-start(bf16[352,384]{1,0:T(8,128)(2,1)S(1)} %get-tuple-element.32), channel_id=1, source_target_pairs={{0,3},{1,2},{2,1},{3,0},{4,7},{5,6},{6,5},{7,4},{8,11},{9,10},{10,... | collective-permute-start | bytes 811016 | tf_op jit(solution)/shard_map/ppermute | solution.py:622
  13.1 13.1 %collective-permute-start.2 = (bf16[96,3840]{1,0:T(8,128)(2,1)S(1)}, bf16[96,3840]{1,0:T(8,128)(2,1)S(1)}, u32[]{:S(2)}, u32[]{:S(2)}) collective-permute-start(bf16[96,3840]{1,0:T(8,128)(2,1)S(1)} %get-tuple-element.30), channel_id=1, source_target_pairs={{0,2},{1,5},{2,0},{3,7},{4,6},{5,1},{6,4},{7,3},{8,10},{9,13},{10,... | collective-permute-start | bytes 2211848 | tf_op jit(solution)/shard_map/ppermute | solution.py:627
  20.8 2.4 %collective-permute-start.6 = (bf16[176,1408]{1,0:T(8,128)(2,1)S(1)}, bf16[176,1408]{1,0:T(8,128)(2,1)S(1)}, u32[]{:S(2)}, u32[]{:S(2)}) collective-permute-start(bf16[176,1408]{1,0:T(8,128)(2,1)S(1)} %shard_map.139), channel_id=1, source_target_pairs={{0,1},{1,0},{2,3},{3,2},{4,5},{5,4},{6,7},{7,6},{8,9},{9,8},{10,11... | collective-permute-start | bytes 1486856 | tf_op jit(solution)/shard_map/ppermute | solution.py:622
  21.3 1.9 %collective-permute-start.4 = (bf16[384,384]{1,0:T(8,128)(2,1)S(1)}, bf16[384,384]{1,0:T(8,128)(2,1)S(1)}, u32[]{:S(2)}, u32[]{:S(2)}) collective-permute-start(bf16[384,384]{1,0:T(8,128)(2,1)S(1)} %get-tuple-element.34), channel_id=1, source_target_pairs={{0,1},{1,0},{2,3},{3,2},{4,5},{5,4},{6,7},{7,6},{8,9},{9,8},{10,11... | collective-permute-start | bytes 884744 | tf_op jit(solution)/shard_map/ppermute | solution.py:622
  26.2 8.3 %collective-permute-start.8 = (bf16[96,3840]{1,0:T(8,128)(2,1)S(1)}, bf16[96,3840]{1,0:T(8,128)(2,1)S(1)}, u32[]{:S(2)}, u32[]{:S(2)}) collective-permute-start(bf16[96,3840]{1,0:T(8,128)(2,1)S(1)} %get-tuple-element.39), channel_id=1, source_target_pairs={{0,1},{1,0},{2,3},{3,2},{4,5},{5,4},{6,7},{7,6},{8,9},{9,8},{10,11... | collective-permute-start | bytes 2211848 | tf_op jit(solution)/shard_map/ppermute | solution.py:622
  26.6 7.9 %collective-permute-start.7 = (bf16[48,3584]{1,0:T(8,128)(2,1)S(1)}, bf16[48,3584]{1,0:T(8,128)(2,1)S(1)}, u32[]{:S(2)}, u32[]{:S(2)}) collective-permute-start(bf16[48,3584]{1,0:T(8,128)(2,1)S(1)} %get-tuple-element.38), channel_id=1, source_target_pairs={{0,4},{1,3},{2,6},{3,1},{4,0},{5,7},{6,2},{7,5},{8,12},{9,11},{10,... | collective-permute-start | bytes 1032200 | tf_op jit(solution)/shard_map/ppermute | solution.py:627
  28.2 10.3 %collective-permute-start.11 = (bf16[96,1408]{1,0:T(8,128)(2,1)S(1)}, bf16[96,1408]{1,0:T(8,128)(2,1)S(1)}, u32[]{:S(2)}, u32[]{:S(2)}) collective-permute-start(bf16[96,1408]{1,0:T(8,128)(2,1)S(1)} %get-tuple-element.42), channel_id=1, source_target_pairs={{0,2},{1,3},{2,0},{3,1},{4,6},{5,7},{6,4},{7,5},{8,10},{9,11},{10,... | collective-permute-start | bytes 811016 | tf_op jit(solution)/shard_map/ppermute | solution.py:622
  29.7 13.6 %collective-permute-start.12 = (bf16[96,1408]{1,0:T(8,128)(2,1)S(1)}, bf16[96,1408]{1,0:T(8,128)(2,1)S(1)}, u32[]{:S(2)}, u32[]{:S(2)}) collective-permute-start(bf16[96,1408]{1,0:T(8,128)(2,1)S(1)} %get-tuple-element.43), channel_id=1, source_target_pairs={{0,6},{1,7},{2,4},{3,5},{4,2},{5,3},{6,0},{7,1},{8,14},{9,15},{10,... | collective-permute-start | bytes 811016 | tf_op jit(solution)/shard_map/ppermute | solution.py:622
  30.1 14.4 %collective-permute-start.13 = (bf16[96,1408]{1,0:T(8,128)(2,1)S(1)}, bf16[96,1408]{1,0:T(8,128)(2,1)S(1)}, u32[]{:S(2)}, u32[]{:S(2)}) collective-permute-start(bf16[96,1408]{1,0:T(8,128)(2,1)S(1)} %get-tuple-element.44), channel_id=1, source_target_pairs={{0,4},{1,5},{2,6},{3,7},{4,0},{5,1},{6,2},{7,3},{8,12},{9,13},{10,... | collective-permute-start | bytes 811016 | tf_op jit(solution)/shard_map/ppermute | solution.py:622
  34.6 1.5 %collective-permute-start.9 = (bf16[48,1792]{1,0:T(8,128)(2,1)S(1)}, bf16[48,1792]{1,0:T(8,128)(2,1)S(1)}, u32[]{:S(2)}, u32[]{:S(2)}) collective-permute-start(bf16[48,1792]{1,0:T(8,128)(2,1)S(1)} %get-tuple-element.40), channel_id=1, source_target_pairs={{0,1},{1,0},{2,3},{3,2},{4,5},{5,4},{6,7},{7,6},{8,9},{9,8},{10,11... | collective-permute-start | bytes 516104 | tf_op jit(solution)/shard_map/ppermute | solution.py:622
  34.6 1.6 %collective-permute-start.10 = (bf16[48,1792]{1,0:T(8,128)(2,1)S(1)}, bf16[48,1792]{1,0:T(8,128)(2,1)S(1)}, u32[]{:S(2)}, u32[]{:S(2)}) collective-permute-start(bf16[48,1792]{1,0:T(8,128)(2,1)S(1)} %get-tuple-element.41), channel_id=1, source_target_pairs={{0,1},{1,0},{2,3},{3,2},{4,5},{5,4},{6,7},{7,6},{8,9},{9,8},{10,11... | collective-permute-start | bytes 516104 | tf_op jit(solution)/shard_map/ppermute | solution.py:622
  36.3 2.3 %copy-start = (s32[2,384]{1,0:T(2,128)S(1)}, s32[2,384]{1,0:T(2,128)}, u32[]{:S(2)}) copy-start(s32[2,384]{1,0:T(2,128)} %owners.5) | copy-start | bytes 9220

commit v7 on v6

--- a/solution.py
+++ b/solution.py
@@ -11,6 +11,7 @@
 HEADS = 16
 P_HEADS = 12
 LANES = 128
+FOLD = 16
 
 
 def norm_rows(values_in):
@@ -264,11 +265,17 @@
     for other in range(4):
         first = stack[:, other * quarter : (other + 1) * quarter]
         second = stack[:, (other + 4) * quarter : (other + 5) * quarter]
-        blocks[other] = jnp.concatenate(
+        whole = jnp.concatenate(
             [first, second, jnp.zeros((row_total, pad), jnp.bfloat16)], axis=1
         )
+        blocks[other] = whole
+        for number in range(2 * quarter // pad):
+            rows = slice(number * FOLD, (number + 1) * FOLD)
+            blocks[other, rows, 2 * quarter :] = whole[
+                row_total - FOLD :, number * pad : (number + 1) * pad
+            ]
     for relation, out in ((0, block0), (2, block2), (3, block3)):
-        out[0:row_total] = blocks[slab ^ relation]
+        out[...] = blocks[slab ^ relation, 0 : out.shape[0]]
     core_block = blocks.at[slab ^ 1]
     for copy in copies[5:]:
         copy.wait()
@@ -411,11 +418,20 @@
             query_part = query_part.at[0:masked]
         else:
             key_part, value_part = block.at[0:tokens], block.at[tokens : 2 * tokens]
-            query_part = block.at[2 * tokens : 2 * tokens + masked]
+            query_part = block.at[2 * tokens :]
         keys[relation * tokens : (relation + 1) * tokens] = key_part[...]
         values[relation * tokens : (relation + 1) * tokens] = value_part[...]
         start = pl.multiple_of((slab ^ relation) * masked, masked)
-        queries[pl.ds(start, masked)] = query_part[...]
+        direct = query_part.shape[0]
+        queries[pl.ds(start, direct)] = query_part[...]
+        if direct < masked:
+            last = pl.ds(pl.multiple_of(start + direct, FOLD), FOLD)
+            used = 4 * head_size
+            queries[last, used:] = jnp.zeros((FOLD, wide - used), jnp.bfloat16)
+            for number in range(used // (wide - used)):
+                rows = slice(number * FOLD, (number + 1) * FOLD)
+                lanes = slice(number * (wide - used), (number + 1) * (wide - used))
+                queries[last, lanes] = block[rows, used:]
     scale = math.log2(math.e) / math.sqrt(head_size)
     chunk = 2 * masked
     for half in range(2):
@@ -641,6 +657,7 @@
     padded = -(-2 * quarter // LANES) * LANES
     block_rows = 2 * tokens + masked
     block = ((block_rows, padded), bf16)
+    folded = ((block_rows - FOLD, padded), bf16)
     weight_rows = w_query.shape[0]
     weight_width = 4 * pred_width + w_proj.shape[1]
     pack_width = weight_width + 2 * pred_width + context_rows * pred_width // weight_rows
@@ -650,7 +667,7 @@
     block0, block2, block3, resid_rows, slot_keys, pack, message, w_here = call(
         functools.partial(pack_kernel, capacity),
         [
-            block, block, block, ((masked, width), bf16), ((4, 2 * masked), jnp.int32), shard,
+            block, folded, folded, ((masked, width), bf16), ((4, 2 * masked), jnp.int32), shard,
             ((message_rows, width), bf16), ((quarter, width), bf16),
         ],
         [

time: 46.4 us -> 46.2 us (level)
  waiting for transfers between devices: 20.8 us -> 20.2 us
  starting transfers between devices: 13.2 us -> 13.7 us
    ppermute x12, waiting for transfers between devices: 17.3 us -> 16.3 us  [send(): lax.ppermute(rows, ('cam', 'slab'), [(source, source ^ flip) for source i...]
    ppermute x12, starting transfers between devices: 9.65 us -> 10.2 us  [send(): lax.ppermute(rows, ('cam', 'slab'), [(source, source ^ flip) for source i...]
where the time goes in v7:
time: 46.2 us; the launch traced here: 45.7 us
  waiting for transfers between devices  20.2 us (44%)
  starting transfers between devices  13.7 us (30%)
  Pallas kernels  11.6 us (25%)
    ppermute x12, waiting for transfers between devices, send(): lax.ppermute(rows, ('cam', 'slab'), [(source, source ^ flip) for source i...  16.3 us
    pallas_call x10, Pallas kernels, call(): pl.pallas_call(kernel, out_shape=shapes, in_specs=[pl.BlockSpec(memory_sp...  11.6 us
    ppermute x12, starting transfers between devices, send(): lax.ppermute(rows, ('cam', 'slab'), [(source, source ^ flip) for source i...  10.2 us
    ppermute x2, waiting for transfers between devices, send_by_core(): return lax.ppermute(rows, ('cam', 'slab'), pairs)  3.92 us
    ppermute x2, starting transfers between devices, send_by_core(): return lax.ppermute(rows, ('cam', 'slab'), pairs)  3.53 us
  transfers between devices with their start and end apart: 14, of which 9 were waited for; matrix products, arithmetic and copies ran while one was open for 0% of the time, Pallas kernels for 18%

profile of v7, /device:TPU:0, one launch (start us, length us, event | category | flops | bytes accessed | tf_op | source)
XLA Modules:
  0.0 45.7 jit_solution(3914728339958284410)
XLA Ops:
  0.0 2.4 %shard_map.136 = (bf16[352,384]{1,0:T(8,128)(2,1)S(1)}, bf16[336,384]{1,0:T(8,128)(2,1)S(1)}, bf16[336,384]{1,0:T(8,128)(2,1)S(1)}, bf16[96,1408]{1,0:T(8,128)(2...) custom-call(bf16[128,1408]{1,0:T(8,128)(2,1)} %bitcast.7, ...), custom_call_target="tpu_custom_call" | custom-call | tf_op jit(solution)/shard_map/pallas_call | solution.py:625
  2.4 0.5 %collective-permute-start = (bf16[544,1408]{1,0:T(8,128)(2,1)S(1)}, bf16[544,1408]{1,0:T(8,128)(2,1)S(1)}, u32[]{:S(2)}, u32[]{:S(2)}) collective-permute-start(bf16[544,1408]{1,0:T(8,128)(2,1)S(1)} %get-tuple-element.25), channel_id=1, source_target_pairs={{0,1},{1,0},{2,3},{3,2},{4,5},{5,4},{6,7},{7,6},{8,9},{9,8},{10,11... | collective-permute-start | bytes 4595720 | tf_op jit(solution)/shard_map/ppermute | solution.py:638
  3.0 2.6 %collective-permute-start.1 = (bf16[336,384]{1,0:T(8,128)(2,1)S(1)}, bf16[336,384]{1,0:T(8,128)(2,1)S(1)}, u32[]{:S(2)}, u32[]{:S(2)}) collective-permute-start(bf16[336,384]{1,0:T(8,128)(2,1)S(1)} %get-tuple-element.28), channel_id=1, source_target_pairs={{0,2},{1,3},{2,0},{3,1},{4,6},{5,7},{6,4},{7,5},{8,10},{9,11},{10,... | collective-permute-start | bytes 774152 | tf_op jit(solution)/shard_map/ppermute | solution.py:638
  5.5 1.5 %collective-permute-start.5 = (bf16[176,1408]{1,0:T(8,128)(2,1)S(1)}, bf16[176,1408]{1,0:T(8,128)(2,1)S(1)}, u32[]{:S(2)}, u32[]{:S(2)}) collective-permute-start(bf16[176,1408]{1,0:T(8,128)(2,1)S(1)} %get-tuple-element.35.w_own), channel_id=1, source_target_pairs={{0,4},{1,5},{2,6},{3,7},{4,0},{5,1},{6,2},{7,3},{8,12},{9,13},{10,... | collective-permute-start | bytes 1486856 | tf_op jit(solution)/shard_map/ppermute | solution.py:638
  7.0 0.0 collective-permute-start.3
  7.1 5.5 %collective-permute-done.1.after.block2 = bf16[336,384]{1,0:T(8,128)(2,1)S(1)} collective-permute-done((bf16[336,384]{1,0:T(8,128)(2,1)S(1)}, bf16[336,384]{1,0:T(8,128)(2,1)S(1)}, u32[]{:S(2)}, u32[]{:S(2)}) %collective-permute-start.1) | collective-permute-done | bytes 258080 | tf_op jit(solution)/shard_map/ppermute | solution.py:638
  12.6 0.0 collective-permute-done.message.w_core
  12.6 0.3 shard_map.137
  12.9 2.0 %collective-permute-start.2 = (bf16[96,3840]{1,0:T(8,128)(2,1)S(1)}, bf16[96,3840]{1,0:T(8,128)(2,1)S(1)}, u32[]{:S(2)}, u32[]{:S(2)}) collective-permute-start(bf16[96,3840]{1,0:T(8,128)(2,1)S(1)} %get-tuple-element.30), channel_id=1, source_target_pairs={{0,2},{1,5},{2,0},{3,7},{4,6},{5,1},{6,4},{7,3},{8,10},{9,13},{10,... | collective-permute-start | bytes 2211848 | tf_op jit(solution)/shard_map/ppermute | solution.py:643
  15.0 2.6 %collective-permute-done.3.block3 = bf16[336,384]{1,0:T(8,128)(2,1)S(1)} collective-permute-done((bf16[336,384]{1,0:T(8,128)(2,1)S(1)}, bf16[336,384]{1,0:T(8,128)(2,1)S(1)}, u32[]{:S(2)}, u32[]{:S(2)}) %collective-permute-start.3) | collective-permute-done | bytes 258080 | tf_op jit(solution)/shard_map/ppermute | solution.py:638
  17.6 2.8 %shard_map.138 = (bf16[384,384]{1,0:T(8,128)(2,1)S(1)}, bf16[384,384]{1,0:T(8,128)(2,1)S(1)}) custom-call(s32[4,192]{1,0:T(4,128)S(1)} %get-tuple-element.27.slot_keys, bf16[352,384]{1,0:T(8,128)(2,1)S(1)} %get-tuple-element.31.block0, bf16[544,1408]{1,0:T(8,128)(2,1)S(1)} %collective-permute-done.message.w_core, ...), custom_call_target="tpu_custom_call" | custom-call | tf_op jit(solution)/shard_map/pallas_call | solution.py:625
  20.5 0.4 collective-permute-start.6
  20.9 0.1 collective-permute-start.4
  21.1 1.8 %collective-permute-done.4.peer_slots = bf16[384,384]{1,0:T(8,128)(2,1)S(1)} collective-permute-done((bf16[384,384]{1,0:T(8,128)(2,1)S(1)}, bf16[384,384]{1,0:T(8,128)(2,1)S(1)}, u32[]{:S(2)}, u32[]{:S(2)}) %collective-permute-start.4) | collective-permute-done | bytes 294944 | tf_op jit(solution)/shard_map/ppermute | solution.py:638
  22.9 2.3 %shard_map.140 = (bf16[96,1408]{1,0:T(8,128)(2,1)S(1)}, bf16[96,1408]{1,0:T(8,128)(2,1)S(1)}, bf16[96,1408]{1,0:T(8,128)(2,1)S(1)}, bf16[96,1408]{1,0:T(8,128)(2,1)S(1)}) custom-call(s32[4,192]{1,0:T(4,128)S(1)} %get-tuple-element.27.slot_keys, bf16[384,384]{1,0:T(8,128)(2,1)S(1)} %get-tuple-element.33.after.own_slots, ...), custom_call_target="tpu_custom_call" | custom-call | tf_op jit(solution)/shard_map/pallas_call | solution.py:625
  25.2 0.6 %collective-permute-done.2.first = bf16[96,3840]{1,0:T(8,128)(2,1)S(1)} collective-permute-done((bf16[96,3840]{1,0:T(8,128)(2,1)S(1)}, bf16[96,3840]{1,0:T(8,128)(2,1)S(1)}, u32[]{:S(2)}, u32[]{:S(2)}) %collective-permute-start.2) | collective-permute-done | bytes 737312 | tf_op jit(solution)/shard_map/ppermute | solution.py:643
  25.8 0.1 shard_map.141
  25.8 0.9 %collective-permute-start.8 = (bf16[96,3840]{1,0:T(8,128)(2,1)S(1)}, bf16[96,3840]{1,0:T(8,128)(2,1)S(1)}, u32[]{:S(2)}, u32[]{:S(2)}) collective-permute-start(bf16[96,3840]{1,0:T(8,128)(2,1)S(1)} %get-tuple-element.39), channel_id=1, source_target_pairs={{0,1},{1,0},{2,3},{3,2},{4,5},{5,4},{6,7},{7,6},{8,9},{9,8},{10,11... | collective-permute-start | bytes 2211848 | tf_op jit(solution)/shard_map/ppermute | solution.py:638
  26.8 1.5 %collective-permute-start.7 = (bf16[48,3584]{1,0:T(8,128)(2,1)S(1)}, bf16[48,3584]{1,0:T(8,128)(2,1)S(1)}, u32[]{:S(2)}, u32[]{:S(2)}) collective-permute-start(bf16[48,3584]{1,0:T(8,128)(2,1)S(1)} %get-tuple-element.38), channel_id=1, source_target_pairs={{0,4},{1,3},{2,6},{3,1},{4,0},{5,7},{6,2},{7,5},{8,12},{9,11},{10,... | collective-permute-start | bytes 1032200 | tf_op jit(solution)/shard_map/ppermute | solution.py:643
  28.3 1.0 %collective-permute-start.11 = (bf16[96,1408]{1,0:T(8,128)(2,1)S(1)}, bf16[96,1408]{1,0:T(8,128)(2,1)S(1)}, u32[]{:S(2)}, u32[]{:S(2)}) collective-permute-start(bf16[96,1408]{1,0:T(8,128)(2,1)S(1)} %get-tuple-element.42), channel_id=1, source_target_pairs={{0,2},{1,3},{2,0},{3,1},{4,6},{5,7},{6,4},{7,5},{8,10},{9,11},{10,... | collective-permute-start | bytes 811016 | tf_op jit(solution)/shard_map/ppermute | solution.py:638
  29.3 1.0 %collective-permute-start.12 = (bf16[96,1408]{1,0:T(8,128)(2,1)S(1)}, bf16[96,1408]{1,0:T(8,128)(2,1)S(1)}, u32[]{:S(2)}, u32[]{:S(2)}) collective-permute-start(bf16[96,1408]{1,0:T(8,128)(2,1)S(1)} %get-tuple-element.43), channel_id=1, source_target_pairs={{0,6},{1,7},{2,4},{3,5},{4,2},{5,3},{6,0},{7,1},{8,14},{9,15},{10,... | collective-permute-start | bytes 811016 | tf_op jit(solution)/shard_map/ppermute | solution.py:638
  30.3 1.5 %collective-permute-start.13 = (bf16[96,1408]{1,0:T(8,128)(2,1)S(1)}, bf16[96,1408]{1,0:T(8,128)(2,1)S(1)}, u32[]{:S(2)}, u32[]{:S(2)}) collective-permute-start(bf16[96,1408]{1,0:T(8,128)(2,1)S(1)} %get-tuple-element.44), channel_id=1, source_target_pairs={{0,4},{1,5},{2,6},{3,7},{4,0},{5,1},{6,2},{7,3},{8,12},{9,13},{10,... | collective-permute-start | bytes 811016 | tf_op jit(solution)/shard_map/ppermute | solution.py:638
  31.8 3.3 %collective-permute-done.7.piece.third = bf16[48,3584]{1,0:T(8,128)(2,1)S(1)} collective-permute-done((bf16[48,3584]{1,0:T(8,128)(2,1)S(1)}, bf16[48,3584]{1,0:T(8,128)(2,1)S(1)}, u32[]{:S(2)}, u32[]{:S(2)}) %collective-permute-start.7) | collective-permute-done | bytes 344096 | tf_op jit(solution)/shard_map/ppermute | solution.py:643
  35.1 0.1 collective-permute-start.9
  35.2 0.5 %collective-permute-start.10 = (bf16[48,1792]{1,0:T(8,128)(2,1)S(1)}, bf16[48,1792]{1,0:T(8,128)(2,1)S(1)}, u32[]{:S(2)}, u32[]{:S(2)}) collective-permute-start(bf16[48,1792]{1,0:T(8,128)(2,1)S(1)} %get-tuple-element.41), channel_id=1, source_target_pairs={{0,1},{1,0},{2,3},{3,2},{4,5},{5,4},{6,7},{7,6},{8,9},{9,8},{10,11... | collective-permute-start | bytes 516104 | tf_op jit(solution)/shard_map/ppermute | solution.py:638
  35.7 0.9 %collective-permute-done.9.peer_left = bf16[48,1792]{1,0:T(8,128)(2,1)S(1)} collective-permute-done((bf16[48,1792]{1,0:T(8,128)(2,1)S(1)}, bf16[48,1792]{1,0:T(8,128)(2,1)S(1)}, u32[]{:S(2)}, u32[]{:S(2)}) %collective-permute-start.9) | collective-permute-done | bytes 172064 | tf_op jit(solution)/shard_map/ppermute | solution.py:638
  36.6 0.2 collective-permute-done.10.peer_right
  36.9 2.2 %shard_map.143.predicted = f32[192,1408]{1,0:T(8,128)S(1)} custom-call(bf16[544,1408]{1,0:T(8,128)(2,1)S(1)} %collective-permute-done.message.w_core, bf16[48,3968]{1,0:T(8,128)(2,1)S(1)} %get-tuple-element.26.pack.own_pack, bf16[48,384]{1,0:T(8,128)(2,1)S(1)} %get-tuple-element.29.own_asks, bf16[96,3840]{1,0:T(8,128)(2,1)S(1)} %collective-permute-done.2.first, ...), custom_call_target="tpu_custom_call" | custom-call | tf_op jit(solution)/shard_map/pallas_call | solution.py:625
  39.1 0.3 shard_map.144.first_rows
  39.4 4.0 %collective-permute-done.12.near = bf16[96,1408]{1,0:T(8,128)(2,1)S(1)} collective-permute-done((bf16[96,1408]{1,0:T(8,128)(2,1)S(1)}, bf16[96,1408]{1,0:T(8,128)(2,1)S(1)}, u32[]{:S(2)}, u32[]{:S(2)}) %collective-permute-start.12) | collective-permute-done | bytes 270368 | tf_op jit(solution)/shard_map/ppermute | solution.py:638
  43.4 1.2 %collective-permute-done.13.far = bf16[96,1408]{1,0:T(8,128)(2,1)S(1)} collective-permute-done((bf16[96,1408]{1,0:T(8,128)(2,1)S(1)}, bf16[96,1408]{1,0:T(8,128)(2,1)S(1)}, u32[]{:S(2)}, u32[]{:S(2)}) %collective-permute-start.13) | collective-permute-done | bytes 270368 | tf_op jit(solution)/shard_map/ppermute | solution.py:638
  44.6 1.0 %shard_map.145 = bf16[192,1408]{1,0:T(8,128)(2,1)} custom-call(s32[2,384]{1,0:T(2,128)S(1)} %copy-done, f32[192,1408]{1,0:T(8,128)S(1)} %shard_map.143.predicted, bf16[96,1408]{1,0:T(8,128)(2,1)S(1)} %shard_map.144.first_rows, bf16[96,1408]{1,0:T(8,128)(2,1)S(1)} %collective-permute-done.12.near, bf16[96,1408]{1,0:T(8,128)(2,1)S(1)} %collective-permute-done.13.far), custom_call_target="tpu_custom_call" | custom-call | tf_op jit(solution)/shard_map/pallas_call | solution.py:625
  (8 shorter events, 0.1 us)
Async XLA Ops:
  2.4 10.2 %collective-permute-start = (bf16[544,1408]{1,0:T(8,128)(2,1)S(1)}, bf16[544,1408]{1,0:T(8,128)(2,1)S(1)}, u32[]{:S(2)}, u32[]{:S(2)}) collective-permute-start(bf16[544,1408]{1,0:T(8,128)(2,1)S(1)} %get-tuple-element.25), channel_id=1, source_target_pairs={{0,1},{1,0},{2,3},{3,2},{4,5},{5,4},{6,7},{7,6},{8,9},{9,8},{10,11... | collective-permute-start | bytes 4595720 | tf_op jit(solution)/shard_map/ppermute | solution.py:638
  3.0 9.6 %collective-permute-start.1 = (bf16[336,384]{1,0:T(8,128)(2,1)S(1)}, bf16[336,384]{1,0:T(8,128)(2,1)S(1)}, u32[]{:S(2)}, u32[]{:S(2)}) collective-permute-start(bf16[336,384]{1,0:T(8,128)(2,1)S(1)} %get-tuple-element.28), channel_id=1, source_target_pairs={{0,2},{1,3},{2,0},{3,1},{4,6},{5,7},{6,4},{7,5},{8,10},{9,11},{10,... | collective-permute-start | bytes 774152 | tf_op jit(solution)/shard_map/ppermute | solution.py:638
  5.5 14.9 %collective-permute-start.5 = (bf16[176,1408]{1,0:T(8,128)(2,1)S(1)}, bf16[176,1408]{1,0:T(8,128)(2,1)S(1)}, u32[]{:S(2)}, u32[]{:S(2)}) collective-permute-start(bf16[176,1408]{1,0:T(8,128)(2,1)S(1)} %get-tuple-element.35.w_own), channel_id=1, source_target_pairs={{0,4},{1,5},{2,6},{3,7},{4,0},{5,1},{6,2},{7,3},{8,12},{9,13},{10,... | collective-permute-start | bytes 1486856 | tf_op jit(solution)/shard_map/ppermute | solution.py:638
  7.0 10.6 %collective-permute-start.3 = (bf16[336,384]{1,0:T(8,128)(2,1)S(1)}, bf16[336,384]{1,0:T(8,128)(2,1)S(1)}, u32[]{:S(2)}, u32[]{:S(2)}) collective-permute-start(bf16[336,384]{1,0:T(8,128)(2,1)S(1)} %get-tuple-element.32), channel_id=1, source_target_pairs={{0,3},{1,2},{2,1},{3,0},{4,7},{5,6},{6,5},{7,4},{8,11},{9,10},{10,... | collective-permute-start | bytes 774152 | tf_op jit(solution)/shard_map/ppermute | solution.py:638
  12.9 12.8 %collective-permute-start.2 = (bf16[96,3840]{1,0:T(8,128)(2,1)S(1)}, bf16[96,3840]{1,0:T(8,128)(2,1)S(1)}, u32[]{:S(2)}, u32[]{:S(2)}) collective-permute-start(bf16[96,3840]{1,0:T(8,128)(2,1)S(1)} %get-tuple-element.30), channel_id=1, source_target_pairs={{0,2},{1,5},{2,0},{3,7},{4,6},{5,1},{6,4},{7,3},{8,10},{9,13},{10,... | collective-permute-start | bytes 2211848 | tf_op jit(solution)/shard_map/ppermute | solution.py:643
  20.5 2.4 %collective-permute-start.6 = (bf16[176,1408]{1,0:T(8,128)(2,1)S(1)}, bf16[176,1408]{1,0:T(8,128)(2,1)S(1)}, u32[]{:S(2)}, u32[]{:S(2)}) collective-permute-start(bf16[176,1408]{1,0:T(8,128)(2,1)S(1)} %shard_map.139), channel_id=1, source_target_pairs={{0,1},{1,0},{2,3},{3,2},{4,5},{5,4},{6,7},{7,6},{8,9},{9,8},{10,11... | collective-permute-start | bytes 1486856 | tf_op jit(solution)/shard_map/ppermute | solution.py:638
  20.9 1.9 %collective-permute-start.4 = (bf16[384,384]{1,0:T(8,128)(2,1)S(1)}, bf16[384,384]{1,0:T(8,128)(2,1)S(1)}, u32[]{:S(2)}, u32[]{:S(2)}) collective-permute-start(bf16[384,384]{1,0:T(8,128)(2,1)S(1)} %get-tuple-element.34), channel_id=1, source_target_pairs={{0,1},{1,0},{2,3},{3,2},{4,5},{5,4},{6,7},{7,6},{8,9},{9,8},{10,11... | collective-permute-start | bytes 884744 | tf_op jit(solution)/shard_map/ppermute | solution.py:638
  25.8 9.3 %collective-permute-start.8 = (bf16[96,3840]{1,0:T(8,128)(2,1)S(1)}, bf16[96,3840]{1,0:T(8,128)(2,1)S(1)}, u32[]{:S(2)}, u32[]{:S(2)}) collective-permute-start(bf16[96,3840]{1,0:T(8,128)(2,1)S(1)} %get-tuple-element.39), channel_id=1, source_target_pairs={{0,1},{1,0},{2,3},{3,2},{4,5},{5,4},{6,7},{7,6},{8,9},{9,8},{10,11... | collective-permute-start | bytes 2211848 | tf_op jit(solution)/shard_map/ppermute | solution.py:638
  26.8 8.3 %collective-permute-start.7 = (bf16[48,3584]{1,0:T(8,128)(2,1)S(1)}, bf16[48,3584]{1,0:T(8,128)(2,1)S(1)}, u32[]{:S(2)}, u32[]{:S(2)}) collective-permute-start(bf16[48,3584]{1,0:T(8,128)(2,1)S(1)} %get-tuple-element.38), channel_id=1, source_target_pairs={{0,4},{1,3},{2,6},{3,1},{4,0},{5,7},{6,2},{7,5},{8,12},{9,11},{10,... | collective-permute-start | bytes 1032200 | tf_op jit(solution)/shard_map/ppermute | solution.py:643
  28.3 10.8 %collective-permute-start.11 = (bf16[96,1408]{1,0:T(8,128)(2,1)S(1)}, bf16[96,1408]{1,0:T(8,128)(2,1)S(1)}, u32[]{:S(2)}, u32[]{:S(2)}) collective-permute-start(bf16[96,1408]{1,0:T(8,128)(2,1)S(1)} %get-tuple-element.42), channel_id=1, source_target_pairs={{0,2},{1,3},{2,0},{3,1},{4,6},{5,7},{6,4},{7,5},{8,10},{9,11},{10,... | collective-permute-start | bytes 811016 | tf_op jit(solution)/shard_map/ppermute | solution.py:638
  29.3 14.2 %collective-permute-start.12 = (bf16[96,1408]{1,0:T(8,128)(2,1)S(1)}, bf16[96,1408]{1,0:T(8,128)(2,1)S(1)}, u32[]{:S(2)}, u32[]{:S(2)}) collective-permute-start(bf16[96,1408]{1,0:T(8,128)(2,1)S(1)} %get-tuple-element.43), channel_id=1, source_target_pairs={{0,6},{1,7},{2,4},{3,5},{4,2},{5,3},{6,0},{7,1},{8,14},{9,15},{10,... | collective-permute-start | bytes 811016 | tf_op jit(solution)/shard_map/ppermute | solution.py:638
  30.3 14.4 %collective-permute-start.13 = (bf16[96,1408]{1,0:T(8,128)(2,1)S(1)}, bf16[96,1408]{1,0:T(8,128)(2,1)S(1)}, u32[]{:S(2)}, u32[]{:S(2)}) collective-permute-start(bf16[96,1408]{1,0:T(8,128)(2,1)S(1)} %get-tuple-element.44), channel_id=1, source_target_pairs={{0,4},{1,5},{2,6},{3,7},{4,0},{5,1},{6,2},{7,3},{8,12},{9,13},{10,... | collective-permute-start | bytes 811016 | tf_op jit(solution)/shard_map/ppermute | solution.py:638
  35.1 1.5 %collective-permute-start.9 = (bf16[48,1792]{1,0:T(8,128)(2,1)S(1)}, bf16[48,1792]{1,0:T(8,128)(2,1)S(1)}, u32[]{:S(2)}, u32[]{:S(2)}) collective-permute-start(bf16[48,1792]{1,0:T(8,128)(2,1)S(1)} %get-tuple-element.40), channel_id=1, source_target_pairs={{0,1},{1,0},{2,3},{3,2},{4,5},{5,4},{6,7},{7,6},{8,9},{9,8},{10,11... | collective-permute-start | bytes 516104 | tf_op jit(solution)/shard_map/ppermute | solution.py:638
  35.2 1.6 %collective-permute-start.10 = (bf16[48,1792]{1,0:T(8,128)(2,1)S(1)}, bf16[48,1792]{1,0:T(8,128)(2,1)S(1)}, u32[]{:S(2)}, u32[]{:S(2)}) collective-permute-start(bf16[48,1792]{1,0:T(8,128)(2,1)S(1)} %get-tuple-element.41), channel_id=1, source_target_pairs={{0,1},{1,0},{2,3},{3,2},{4,5},{5,4},{6,7},{7,6},{8,9},{9,8},{10,11... | collective-permute-start | bytes 516104 | tf_op jit(solution)/shard_map/ppermute | solution.py:638
  36.9 2.3 %copy-start = (s32[2,384]{1,0:T(2,128)S(1)}, s32[2,384]{1,0:T(2,128)}, u32[]{:S(2)}) copy-start(s32[2,384]{1,0:T(2,128)} %owners.5) | copy-start | bytes 9220
